TPU v7x, 32 devices: a whole 2x2x4 slice. The times are simulated.
32 devices in a mesh: row: 8 (over y, x, core), col: 4 (over z).
Axes of the slice: x: 2, y: 2, z: 4, core: 2. Of those that a mesh axis runs over, the one named last changes fastest.
Arguments:
- factor_rows: float32 [512, 2, 2048], P(None, None, 'row'), may hold values from -0.00390625 to 0.00390625
- prev_solution: float32 [2048, 16384], P('row', 'col'), may hold values from -6 to 6
- cross_rows: float32 [512, 2, 16384], P('row', None, 'col'), may hold values from -0.2 to 0.2
- inverses: float32 [512, 2, 512], P('row'), as said below
- coupling: float32 [512, 512], P('row'), may hold values from -0.25 to 0.25
Outputs:
- downdate: float32 [16384, 16384], P('row', 'col')
Inputs may be any that keep to these rules, and one draw needn't show every extreme that they name: Each block inverses[:, k, :] is lower triangular with a positive diagonal.
All inputs are finite; a program needn't handle non-finite values.
Results may differ from a plain program's by a relative error of at most 0.000096.
Values sent between devices are 32-bit elements; how exact they have to be, the bound alone decides.
No kernel may reach another device: no remote copies, remote signals or barrier semaphores. Data moves between devices by JAX's collectives and lax.ppermute only.
A program may use at most 128 MiB of HBM per device.

v0:
```python
import jax
import jax.numpy as jnp
from jax import lax
from jax.sharding import PartitionSpec as P


def from_root(x, axis, root):
    mine = lax.axis_index(axis) == root
    return lax.psum(jnp.where(mine, x, jnp.zeros_like(x)), axis)


def solve_with(rows_inverse, piece):
    return jnp.dot(
        rows_inverse, piece, precision=lax.Precision.HIGHEST, preferred_element_type=jnp.float32
    )


def test_columns(panel, rank, fanout, narrow):
    return lax.dynamic_slice_in_dim(panel, rank % fanout * narrow, narrow, 1)


def outer_product(test_rows, panel):
    return jnp.einsum(
        "ki,kj->ij",
        test_rows,
        panel,
        precision=lax.Precision.HIGHEST,
        preferred_element_type=jnp.float32,
    )


def local(factor_rows, prev_solution, cross_rows, inverses, coupling):
    full = lax.Precision.HIGHEST
    width = prev_solution.shape[1]
    fanout = lax.axis_size("row") // lax.axis_size("col")
    narrow = width // fanout
    rank = lax.axis_index("row")
    summed = lax.psum_scatter(
        jnp.einsum(
            "pks,sn->pkn",
            factor_rows,
            prev_solution,
            precision=full,
            preferred_element_type=jnp.float32,
        ),
        "row",
        scatter_dimension=0,
        tiled=True,
    )
    first_update = cross_rows[:, 0, :] - summed[:, 0, :]
    second_update = cross_rows[:, 1, :] - summed[:, 1, :]
    first_own = solve_with(
        inverses[:, 0, :], lax.all_gather(first_update, "row", axis=0, tiled=True)
    )
    first_panel = lax.all_gather(first_own, "row", axis=0, tiled=True)
    rest = second_update - jnp.dot(
        coupling, first_panel, precision=full, preferred_element_type=jnp.float32
    )
    second_own = solve_with(inverses[:, 1, :], lax.all_gather(rest, "row", axis=0, tiled=True))
    second_panel = lax.all_gather(second_own, "row", axis=0, tiled=True)
    stacked = jnp.concatenate([first_panel, second_panel], axis=0)
    picked = from_root(test_columns(stacked, rank, fanout, narrow), "col", rank // fanout)
    downdate = outer_product(picked, stacked)
    return downdate


def solution(mesh):
    return jax.shard_map(
        local,
        mesh=mesh,
        in_specs=(
            P(None, None, "row"),
            P("row", "col"),
            P("row", None, "col"),
            P("row", None, None),
            P("row", None),
        ),
        out_specs=P("row", "col"),
        check_vma=False,
    )
```

profile of v0, /device:TPU:0, one launch (start us, length us, event | category | flops | bytes accessed | tf_op | source)
XLA Modules:
  0.0 818.9 jit_solution(6707729357129944821)
XLA Ops:
  6.5 0.0 copy-start
  6.5 0.0 reduce-scatter.2.cloned.1.call-start
  6.5 17.6 %fusion.6 = f32[512,2,4096]{2,0,1:T(8,128)} fusion(f32[256,4096]{1,0:T(8,128)} %param.6, f32[512,2,256]{2,1,0:T(2,128)} %param.5), kind=kOutput, calls=%fused_computation.7 | convolution fusion | flops 12884901888 | bytes 22020096 | tf_op jit(solution)/shard_map/pks,sn->pkn/dot_general | solution.py:39
  24.1 0.0 reduce-scatter.2.cloned.1.call-update
  24.2 0.0 all-gather.12.cloned.1.call-start
  24.2 4.4 fusion.10
  28.7 114.3 %reduce-scatter.2.cloned.1.call-done = f32[64,2,4096]{2,0,1:T(8,128)} async-done(((f32[512,2,4096]{2,0,1:T(8,128)}), f32[64,2,4096]{2,0,1:T(8,128)}) %reduce-scatter.2.cloned.1.call-update) | async-done | bytes 2097168 | tf_op jit(solution)/shard_map/reduce_scatter | solution.py:38
  143.0 2.9 slice_subtract_fusion.1
  145.9 0.0 copy-start.2
  145.9 0.0 all-gather.12.cloned.1.call-update
  145.9 0.0 all-gather.6.cloned.1.call-start
  145.9 1.4 fusion.11
  147.3 53.1 %all-gather.12.cloned.1.call-done = f32[512,1,4096]{2,0,1:T(8,128)} async-done(((f32[64,1,4096]{2,0,1:T(8,128)}), f32[512,1,4096]{2,0,1:T(8,128)}) %all-gather.12.cloned.1.call-update) | async-done | bytes 8388624 | tf_op jit(solution)/shard_map/all_gather | solution.py:53
  200.4 8.8 %fusion.2 = f32[64,4096]{1,0:T(8,128)} fusion(f32[512,1,4096]{2,0,1:T(8,128)} %all-gather.12.cloned.1.call-done, f32[64,1,512]{2,1,0:T(1,128)S(1)} %get-tuple-element.8), kind=kOutput, calls=%fused_computation.3 | convolution fusion | flops 1610612736 | bytes 9568256 | tf_op jit(solution)/shard_map/dot_general | solution.py:13
  209.2 0.0 all-gather.6.cloned.1.call-update
  209.3 0.2 all-gather.8.cloned.1.call-start
  209.5 54.3 %all-gather.6.cloned.1.call-done = f32[512,4096]{1,0:T(8,128)} async-done(((f32[64,4096]{1,0:T(8,128)}), f32[512,4096]{1,0:T(8,128)}) %all-gather.6.cloned.1.call-update) | async-done | bytes 8388624 | tf_op jit(solution)/shard_map/all_gather | solution.py:55
  263.8 0.0 copy-done
  263.8 0.0 copy-done.2
  263.8 10.2 %fusion.5 = f32[64,4096]{1,0:T(8,128)} fusion(f32[512,4096]{1,0:T(8,128)} %all-gather.6.cloned.1.call-done, f32[64,512]{1,0:T(8,128)S(1)} %copy-done, f32[64,2,4096]{2,0,1:T(8,128)S(1)} %copy-done.2, f32[64,1,4096]{2,1,0:T(1,128)S(1)} %get-tuple-element.5), kind=kOutput, calls=%fused_computation.6 | convolution fusion | flops 1611137024 | bytes 11665408 | tf_op jit(solution)/shard_map/dot_general | solution.py:56
  274.0 0.0 all-gather.8.cloned.1.call-update
  274.0 0.0 all-gather.10.cloned.1.call-start
  274.1 54.5 %all-gather.8.cloned.1.call-done = f32[512,4096]{1,0:T(8,128)} async-done(((f32[64,4096]{1,0:T(8,128)}), f32[512,4096]{1,0:T(8,128)}) %all-gather.8.cloned.1.call-update) | async-done | bytes 8388624 | tf_op jit(solution)/shard_map/all_gather | solution.py:59
  328.6 8.8 %convolution_bitcast_fusion = f32[64,4096]{1,0:T(8,128)} fusion(f32[512,4096]{1,0:T(8,128)} %all-gather.8.cloned.1.call-done, f32[64,1,512]{2,1,0:T(1,128)S(1)} %get-tuple-element.7), kind=kOutput, calls=%fused_computation.4 | convolution fusion | flops 1610612736 | bytes 9568256 | tf_op jit(solution)/shard_map/dot_general | solution.py:13
  337.4 0.0 all-gather.10.cloned.1.call-update
  337.5 0.0 all-reduce.2.cloned.1.call-start
  337.5 7.8 constant_dynamic-update-slice_fusion.1
  345.4 46.6 %all-gather.10.cloned.1.call-done = f32[512,4096]{1,0:T(8,128)} async-done(((f32[64,4096]{1,0:T(8,128)}), f32[512,4096]{1,0:T(8,128)}) %all-gather.10.cloned.1.call-update) | async-done | bytes 8388624 | tf_op jit(solution)/shard_map/all_gather | solution.py:60
  392.0 7.6 constant_dynamic-update-slice_fusion
  399.6 8.4 %dynamic-slice_select_fusion = f32[1024,2048]{1,0:T(8,128)} fusion(f32[1024,4096]{1,0:T(8,128)} %constant_dynamic-update-slice_fusion, s32[]{:T(128)S(6)} %select_n.25, pred[]{:T(512)S(6)} %eq.5), kind=kLoop, calls=%fused_computation.2 | loop fusion | flops 2097152 | bytes 16777220 | tf_op jit(solution)/shard_map/jit(_where)/select_n | solution.py:9
  408.0 0.0 all-reduce.2.cloned.1.call-update
  408.0 291.0 %all-reduce.2.cloned.1.call-done = f32[1024,2048]{1,0:T(8,128)} async-done(((f32[1024,2048]{1,0:T(8,128)}), f32[1024,2048]{1,0:T(8,128)}) %all-reduce.2.cloned.1.call-update) | async-done | bytes 8388624 | tf_op jit(solution)/shard_map/psum | solution.py:9
  699.0 0.0 copy-start.1
  699.0 113.1 %fusion.12 = f32[2048,4096]{1,0:T(8,128)} fusion(f32[1024,2048]{1,0:T(8,128)} %all-reduce.2.cloned.1.call-done, f32[1024,4096]{1,0:T(8,128)} %constant_dynamic-update-slice_fusion), kind=kOutput, calls=%fused_computation.19 | convolution fusion | flops 103079215104 | bytes 58720256 | tf_op jit(solution)/shard_map/ki,kj->ij/dot_general | solution.py:23
  812.1 0.0 copy-done.1
Async XLA Ops:
  6.5 257.3 %copy-start = (f32[64,512]{1,0:T(8,128)S(1)}, f32[64,512]{1,0:T(8,128)}, u32[]{:S(2)}) copy-start(f32[64,512]{1,0:T(8,128)} %param.9) | copy-start | bytes 393220
  6.5 136.4 %reduce-scatter.2.cloned.1.call-start = ((), (), s32[]{:S(2)}) async-start(), calls=%async_computation.1 | async-start | bytes 18874368 | tf_op jit(solution)/shard_map/reduce_scatter | solution.py:38
  24.2 176.2 %all-gather.12.cloned.1.call-start = ((), (), s32[]{:S(2)}) async-start(), calls=%async_computation.6 | async-start | bytes 9437184 | tf_op jit(solution)/shard_map/all_gather | solution.py:53
  145.9 118.0 %copy-start.2 = (f32[64,2,4096]{2,0,1:T(8,128)S(1)}, f32[64,2,4096]{2,0,1:T(8,128)}, u32[]{:S(2)}) copy-start(f32[64,2,4096]{2,0,1:T(8,128)} %reduce-scatter.2.cloned.1.call-done) | copy-start | bytes 6291460
  145.9 117.9 %all-gather.6.cloned.1.call-start = ((), (), s32[]{:S(2)}) async-start(), calls=%async_computation.2 | async-start | bytes 9437184 | tf_op jit(solution)/shard_map/all_gather | solution.py:55
  209.3 119.3 %all-gather.8.cloned.1.call-start = ((), (), s32[]{:S(2)}) async-start(), calls=%async_computation.3 | async-start | bytes 9437184 | tf_op jit(solution)/shard_map/all_gather | solution.py:59
  274.0 118.0 %all-gather.10.cloned.1.call-start = ((), (), s32[]{:S(2)}) async-start(), calls=%async_computation.4 | async-start | bytes 9437184 | tf_op jit(solution)/shard_map/all_gather | solution.py:60
  337.5 361.6 %all-reduce.2.cloned.1.call-start = ((), (), s32[]{:S(2)}) async-start(), calls=%async_computation.5 | async-start | bytes 16777216 | tf_op jit(solution)/shard_map/psum | solution.py:9
  699.0 113.1 %copy-start.1 = (f32[64,512]{1,0:T(8,128)S(1)}, f32[64,512]{1,0:T(8,128)}, u32[]{:S(2)}) copy-start(f32[64,512]{1,0:T(8,128)} %param.9) | copy-start | bytes 393220
Sparse Core Ops, SparseCore 0:
  24.3 118.6 reduce-scatter.1
  146.0 54.3 all-gather.11
  209.4 54.3 all-gather.5
  274.2 54.3 all-gather.7
  337.6 54.3 all-gather.9
  408.2 290.8 all-reduce.1
where the time goes:
time: 819 us
  waiting for transfers between devices  614 us (75%)
  matrix products  159 us (19%)
  local copies, waits for them, and re-layouts  21.3 us (3%)
  between operations  13.5 us (2%)
  other arithmetic  11.3 us (1%)
    psum x1, waiting for transfers between devices, from_root(): return lax.psum(jnp.where(mine, x, jnp.zeros_like(x)), axis)  291 us
    reduce_scatter x1, waiting for transfers between devices, local(): lax.psum_scatter(jnp.einsum('pks,sn->pkn', factor_rows, prev_solution, pr...  114 us
    dot_general x1, matrix products, outer_product(): jnp.einsum('ki,kj->ij', test_rows, panel, precision=lax.Precision.HIGHEST...  113 us
    all_gather x1, waiting for transfers between devices, local(): lax.all_gather(rest, 'row', axis=0, tiled=True)  54.5 us
    all_gather x1, waiting for transfers between devices, local(): first_panel = lax.all_gather(first_own, 'row', axis=0, tiled=True)  54.3 us
    all_gather x1, waiting for transfers between devices, local(): lax.all_gather(first_update, 'row', axis=0, tiled=True)  53.1 us
    all_gather x1, waiting for transfers between devices, local(): second_panel = lax.all_gather(second_own, 'row', axis=0, tiled=True)  46.6 us
    dot_general x2, matrix products, solve_with(): jnp.dot(rows_inverse, piece, precision=lax.Precision.HIGHEST, preferred_e...  17.7 us
  transfers between devices with their start and end apart: 6, of which 6 were waited for; matrix products, arithmetic and copies ran while one was open for 2% of the time, Pallas kernels for 0%

commit v1 on v0

v1 whole, which is shorter than its diff:
```python
import functools

import jax
import jax.numpy as jnp
from jax import lax
from jax.experimental import pallas as pl
from jax.experimental.pallas import tpu as pltpu
from jax.sharding import PartitionSpec as P

def dot(a, b, precision=lax.Precision.HIGHEST):
    return jnp.dot(a, b, precision=precision, preferred_element_type=jnp.float32)


def halves(x):
    high = x.astype(jnp.bfloat16)
    return high, (x - high.astype(jnp.float32)).astype(jnp.bfloat16)


def product(a, b, contract=1):
    return lax.dot_general(
        a, b, (((contract,), (0,)), ((), ())), preferred_element_type=jnp.float32
    )


def three(a, b, contract=1):
    (a_high, a_low), (b_high, b_low) = a, b
    small = product(a_high, b_low, contract) + product(a_low, b_high, contract)
    return product(a_high, b_high, contract) + small


def cost(flops, moved):
    return pl.CostEstimate(flops=flops, bytes_accessed=moved, transcendentals=0)


def roomy(limit=56):
    return pltpu.CompilerParams(vmem_limit_bytes=limit << 20)


def corner_kernel(table, *outs):
    depth = table.shape[0] * table.shape[2]
    first, second, couple = [halves(table[:, n].reshape(depth, -1)) for n in range(3)]
    corner = -three(second, halves(three(couple, first)))
    outs[0][...], outs[1][...] = first
    outs[2][...], outs[3][...] = halves(corner)
    outs[4][...], outs[5][...] = second


def transfer_matrix(inverses, coupling):
    table = jnp.concatenate([jnp.swapaxes(inverses, 0, 1), coupling[None]], axis=0)
    table = lax.all_gather(table, "row", axis=0)
    panel = coupling.shape[1]
    return pl.pallas_call(
        corner_kernel,
        out_shape=[jax.ShapeDtypeStruct((panel, panel), jnp.bfloat16)] * 6,
        compiler_params=roomy(),
        cost_estimate=cost(12 * panel**3, 24 * panel**2),
    )(table)


def partial_updates(steps, info, f_own, f_given, p_own, p_given, c_own, c_given, *refs):
    outs, (f_high, f_low) = refs[:-2], refs[-2:]
    step = pl.program_id(0)
    depth, span = f_own.shape
    near = c_own.shape[1]

    @pl.when(step == 0)
    def _():
        for side, part in enumerate((f_own, f_given)):
            cut = slice(side * span, (side + 1) * span)
            f_high[:, cut], f_low[:, cut] = halves(part[...])

    columns = jnp.concatenate([p_own[...], p_given[...]], axis=0)
    total = -three((f_high[...], f_low[...]), halves(columns))
    for n, parts in enumerate(steps):

        @pl.when(step == n)
        def _(parts=parts):
            for out, start, taken, size in parts:
                into, cut = slice(start, start + size), slice(taken, taken + size)
                outs[out][:, into] = total[:, cut]
                for part, rank in ((c_own, info[-2]), (c_given, info[-1])):
                    for k in range(2):
                        rows = pl.ds(pl.multiple_of(k * (depth // 2) + rank * near, near), near)
                        outs[out][rows, into] = outs[out][rows, into] + part[k][:, cut]


def update_blocks(info, steps, widths, sources):
    f_own, _, p_own, _, c_own, _ = sources
    depth, span = f_own.shape
    near = c_own.shape[1]
    wide = p_own.shape[1] // 16
    count = len(steps)
    own = lambda i, info: info[count] * 8 + info[i]
    return pl.pallas_call(
        lambda info, *refs: partial_updates(
            steps, [info[count + n] for n in range(3)], *refs
        ),
        grid_spec=pltpu.PrefetchScalarGridSpec(
            num_scalar_prefetch=1,
            grid=(count,),
            in_specs=[
                pl.BlockSpec((depth, span), lambda i, info: (0, 0)),
                pl.BlockSpec((depth, span), lambda i, info: (0, 0)),
                pl.BlockSpec((span, wide), lambda i, info: (0, own(i, info))),
                pl.BlockSpec((span, wide), lambda i, info: (0, info[i])),
                pl.BlockSpec((2, near, wide), lambda i, info: (0, 0, own(i, info))),
                pl.BlockSpec((2, near, wide), lambda i, info: (0, 0, info[i])),
            ],
            out_specs=[pl.BlockSpec((depth, w), lambda i, info: (0, 0)) for w in widths],
            scratch_shapes=[pltpu.VMEM((depth, 2 * span), jnp.bfloat16)] * 2,
        ),
        out_shape=[jax.ShapeDtypeStruct((depth, w), jnp.float32) for w in widths],
        compiler_params=roomy(),
        cost_estimate=cost(
            6 * depth * 2 * span * count * wide, 4 * depth * (2 * span + count * wide)
        ),
    )(info, *sources)


def solve_kernel(*refs):
    matrix, (keep, a_got, b_got, a_last, b_last) = refs[:6], refs[6:11]
    solved, chunks = refs[11], refs[12:]
    panel, half = keep.shape[0] // 2, a_last.shape[1]
    arrived = [
        got[:, half:] + last[...] for got, last in ((a_got, a_last), (b_got, b_last))
    ]
    update = keep[...] + jnp.concatenate(arrived, axis=1)
    upper, lower = halves(update[:panel]), halves(update[panel:])
    first, corner, second = [(matrix[n][...], matrix[n + 1][...]) for n in (0, 2, 4)]
    top = three(first, upper)
    low = three(corner, upper) + three(second, lower)
    solved[:panel, :] = top
    solved[panel:, :] = low
    for n, chunk in enumerate(chunks):
        cut = slice(n * chunk.shape[1], (n + 1) * chunk.shape[1])
        chunk[:panel, :] = top[:, cut]
        chunk[panel:, :] = low[:, cut]


def solve(matrix, terms, widths, whole):
    panel = matrix[0].shape[0]
    depth, wide = terms[0].shape
    shape = lambda w: jax.ShapeDtypeStruct((depth, w), jnp.float32)
    full = lambda x: pl.BlockSpec(x.shape, lambda i: (0, 0))
    ins = [*matrix, *terms]
    kernel, specs, side, aliases = solve_kernel, [full(x) for x in ins], 0, {}
    if whole is not None:
        kernel = lambda *refs: solve_kernel(*refs[:11], *refs[12:])
        specs, side, aliases = [*specs, pl.BlockSpec(memory_space=pl.ANY)], 1, {11: 0}
        ins = [*ins, whole]
    return pl.pallas_call(
        kernel,
        grid=(1,),
        in_specs=specs,
        out_specs=[pl.BlockSpec((depth, wide), lambda i: (0, side))]
        + [pl.BlockSpec((depth, w), lambda i: (0, 0)) for w in widths],
        out_shape=[shape(2 * wide)] + [shape(w) for w in widths],
        input_output_aliases=aliases,
        compiler_params=roomy(),
        cost_estimate=cost(18 * panel * panel * wide, 4 * (3 * panel**2 + 6 * depth * wide)),
    )(*ins)


def split_kernel(parts, place, *refs):
    del place
    high, low = refs[-2:]
    for m in range(4):

        @pl.when(pl.program_id(0) // parts == m)
        def _(block=refs[m]):
            high[0], low[0] = halves(block[...])


def split_blocks(place, blocks, held):
    depth, width = blocks[0].shape
    parts = 2
    rows = depth // parts
    shape = jax.ShapeDtypeStruct((8, depth, width), jnp.bfloat16)
    spec = pl.BlockSpec((1, rows, width), lambda i, place: (place[i // parts], i % parts, 0))

    def taken(m):
        return pl.BlockSpec(
            (rows, width), lambda i, place: (jnp.clip(i - parts * m, 0, parts - 1), 0)
        )

    held = list(held)
    return pl.pallas_call(
        functools.partial(split_kernel, parts),
        grid_spec=pltpu.PrefetchScalarGridSpec(
            num_scalar_prefetch=1,
            grid=(4 * parts,),
            in_specs=[taken(m) for m in range(4)]
            + [pl.BlockSpec(memory_space=pl.ANY)] * len(held),
            out_specs=[spec, spec],
        ),
        out_shape=[shape, shape],
        input_output_aliases={5: 0, 6: 1} if held else {},
        compiler_params=roomy(40),
        cost_estimate=cost(0, 8 * 4 * depth * width),
    )(place, *blocks, *held)


def downdate_kernel(info, mine, *refs):
    others, gathered = refs[:3], refs[3:6]
    high, low = refs[6:8]
    out, left_high, left_low = refs[-3:]
    width = others[0].shape[1]

    @pl.when(pl.program_id(0) == 0)
    def _():
        inside = info[1] == 1
        pieces = [mine[0]] + [
            jnp.where(inside, own[...], other[...]) for other, own in zip(others, gathered)
        ]
        for m, piece in enumerate(pieces):
            cut = slice(m * width, (m + 1) * width)
            left_high[:, cut], left_low[:, cut] = halves(piece)

    total = three((left_high[...], left_low[...]), (high[0], low[0]), 0)
    for m in range(4):
        out[info[0] ^ m] = total[m * width : (m + 1) * width]


def downdate_part(info, blocks, others, gathered, held, out, at):
    _, depth, width = blocks.shape
    wide = held[0].shape[2]
    rows = 4 * width
    specs = [pl.BlockSpec((1, depth, width), lambda j, info: (info[0], 0, 0))]
    specs += [pl.BlockSpec((depth, width), lambda j, info: (0, 0))] * 3
    specs += [pl.BlockSpec((depth, width), lambda j, info: (0, at))] * 3
    specs += [pl.BlockSpec((1, depth, wide), lambda j, info: (j, 0, 0))] * 2
    ins = [blocks, *others, *gathered, *held]
    aliases = {}
    if out is not None:
        specs += [pl.BlockSpec(memory_space=pl.ANY)]
        ins += [out]
        aliases = {len(ins): 0}
    return pl.pallas_call(
        downdate_kernel,
        grid_spec=pltpu.PrefetchScalarGridSpec(
            num_scalar_prefetch=1,
            grid=(8,),
            in_specs=specs,
            out_specs=pl.BlockSpec((4, width, wide), lambda j, info: (0, at, j)),
            scratch_shapes=[pltpu.VMEM((depth, rows), jnp.bfloat16)] * 2,
        ),
        out_shape=jax.ShapeDtypeStruct((4, wide, 8 * wide), jnp.float32),
        input_output_aliases=aliases,
        compiler_params=roomy(),
        cost_estimate=cost(
            6 * depth * rows * 8 * wide, 4 * (2 * depth * rows + 8 * depth * wide + rows * 8 * wide)
        ),
    )(info, *ins)


CORE = [(i, i ^ 1) for i in range(8)]
ALONG_X = [(i, i ^ 2) for i in range(8)]
ALONG_Y = [(i, i ^ 4) for i in range(8)]


def to_others(across):
    return [
        ((j * 2 + c) * 4 + z, ((j ^ across) * 2 + c) * 4 + z)
        for j in range(4)
        for c in range(2)
        for z in range(4)
        if j ^ across != z
    ]


def after(x, *others):
    return lax.optimization_barrier((x, *others))[0]


def local(factor_rows, prev_solution, cross_rows, inverses, coupling):
    rank, plane = lax.axis_index("row"), lax.axis_index("col")
    chip, core = rank // 2, rank % 2
    depth = 2 * factor_rows.shape[0]
    width = prev_solution.shape[1]
    half, quarter = width // 16, width // 32
    ints = lambda *values: jnp.stack([jnp.asarray(v, jnp.int32) for v in values])

    matrix = transfer_matrix(inverses, coupling)
    there = lambda x: lax.dynamic_slice_in_dim(
        x, (1 - core) * (width // 2), width // 2, x.ndim - 1
    )
    p_given = lax.ppermute(there(prev_solution), "row", CORE)
    c_own = jnp.swapaxes(cross_rows, 0, 1)
    c_given = lax.ppermute(there(c_own), "row", CORE)
    f_own = jnp.swapaxes(factor_rows, 0, 1).reshape(depth, -1)
    f_given = lax.ppermute(f_own, "row", CORE)
    sources = (f_own, f_given, prev_solution, p_given, c_own, c_given)

    away = (
        ((0, 0, 0, quarter), (1, 0, quarter, quarter)),
        ((0, quarter, 0, quarter), (3, 0, quarter, quarter)),
        ((2, 0, 0, quarter), (1, quarter, quarter, quarter)),
    )
    away_widths = (half, half, quarter, quarter)

    def updates(places, steps, widths):
        spots = [(chip ^ across) * 2 + side for across, side in places]
        return update_blocks(ints(*spots, core, rank, rank ^ 1), steps, widths, sources)

    def arrivals(a_out, b_out, a_on, b_on):
        a_got = lax.ppermute(a_out, "row", ALONG_X)
        b_got = lax.ppermute(b_out, "row", ALONG_Y)
        a_on, b_on = a_on + a_got[:, :quarter], b_on + b_got[:, :quarter]
        a_last = lax.ppermute(a_on, "row", ALONG_Y)
        b_last = lax.ppermute(b_on, "row", ALONG_X)
        return (a_got, b_got, a_last, b_last), a_on

    early = updates(((3, 0), (1, 0), (2, 0)), away, away_widths)
    *late, keep, late_keep = updates(
        ((3, 1), (1, 1), (2, 1), (0, 0), (0, 1)),
        (*away, ((4, 0, 0, half),), ((5, 0, 0, half),)),
        (*away_widths, half, half),
    )
    terms, sent = arrivals(*early)
    solved, chunk = solve(matrix, (keep, *terms), (half,), None)
    late = [after(x, sent) for x in late[:2]] + late[2:]
    terms, _ = arrivals(*late)
    solved, *chunks = solve(matrix, (late_keep, *terms), (quarter, quarter), solved)
    blocks = [lax.all_gather(x, "col", axis=0) for x in (chunk, *chunks)]

    from_x = lax.ppermute(solved, "row", ALONG_X)
    from_y = lax.ppermute(solved, "row", ALONG_Y)
    far_a = lax.ppermute(from_x[:, :half], "row", ALONG_Y)
    far_b = lax.ppermute(from_y[:, half:], "row", ALONG_X)
    far = jnp.concatenate([far_a, far_b], axis=1)
    gathered = [solved, from_x, from_y, far]
    held = split_blocks(ints(*[core * 4 + (chip ^ m) for m in range(4)]), gathered, ())
    given = [lax.ppermute(block, "row", CORE) for block in gathered]
    held = split_blocks(ints(*[(1 - core) * 4 + (chip ^ m) for m in range(4)]), given, held)

    info = ints(chip, chip == plane)
    out = None
    for block, at in zip(blocks, (0, 2, 3)):
        others = [
            lax.ppermute(
                lax.dynamic_index_in_dim(block, chip ^ m, 0, keepdims=False),
                ("row", "col"),
                to_others(m),
            )
            for m in (1, 2, 3)
        ]
        out = downdate_part(info, block, others, gathered[1:], held, out, at)
    return out.reshape(-1, width)


def local_any(factor_rows, prev_solution, cross_rows, inverses, coupling):
    full = lax.Precision.HIGHEST
    width = prev_solution.shape[1]
    fanout = lax.axis_size("row") // lax.axis_size("col")
    narrow = width // fanout
    rank = lax.axis_index("row")
    sums = lax.psum_scatter(
        jnp.einsum(
            "pks,sn->pkn",
            factor_rows,
            prev_solution,
            precision=full,
            preferred_element_type=jnp.float32,
        ),
        "row",
        scatter_dimension=0,
        tiled=True,
    )
    update = lax.all_gather(cross_rows - sums, "row", axis=0, tiled=True)
    lower = lax.all_gather(inverses, "row", axis=0, tiled=True)
    couple = lax.all_gather(coupling, "row", axis=0, tiled=True)
    first = dot(lower[:, 0, :], update[:, 0, :], full)
    rest = update[:, 1, :] - dot(couple, first, full)
    second = dot(lower[:, 1, :], rest, full)
    stacked = jnp.concatenate([first, second], axis=0)
    cut = lax.dynamic_slice_in_dim(stacked, rank % fanout * narrow, narrow, 1)
    mine = lax.axis_index("col") == rank // fanout
    picked = lax.psum(jnp.where(mine, cut, jnp.zeros_like(cut)), "col")
    return lax.dot_general(
        picked, stacked, (((0,), (0,)), ((), ())), precision=full, preferred_element_type=jnp.float32
    )


def solution(mesh):
    body = local if (mesh.shape["row"], mesh.shape["col"]) == (8, 4) else local_any
    return jax.shard_map(
        body,
        mesh=mesh,
        in_specs=(
            P(None, None, "row"),
            P("row", "col"),
            P("row", None, "col"),
            P("row", None, None),
            P("row", None),
        ),
        out_specs=P("row", "col"),
        check_vma=False,
    )
```

time: 819 us -> 380 us (0.46)
  waiting for transfers between devices: 614 us -> 162 us
  matrix products: 159 us -> 0 us
  Pallas kernels: 0 us -> 130 us
  starting transfers between devices: 0.39 us -> 42.7 us
    psum x1 -> x0, waiting for transfers between devices: 291 us -> none  [from_root(): return lax.psum(jnp.where(mine, x, jnp.zeros_like(x)), axis)]
    all_gather x4, waiting for transfers between devices: 209 us -> 34.3 us  [the longest x3 34.3 us: local(): blocks = [lax.all_gather(x, 'col', axis=0) for x in (chunk, *chunks)]]
    dot_general x5 -> x0, matrix products: 159 us -> none  [the longest x1 113 us: outer_product(): jnp.einsum('ki,kj->ij', test_rows, panel, precision=lax.Precision.HIGHEST...]
    pallas_call x0 -> x10, Pallas kernels: none -> 130 us  [the longest x3 73.9 us: downdate_part(): pl.pallas_call(downdate_kernel, grid_spec=pltpu.PrefetchScalarGridSpec(nu...]
    ppermute x0 -> x28, waiting for transfers between devices: none -> 128 us  [the longest x2 53.2 us: arrivals(): b_got = lax.ppermute(b_out, 'row', ALONG_Y)]
    reduce_scatter x1 -> x0, waiting for transfers between devices: 114 us -> none  [local(): lax.psum_scatter(jnp.einsum('pks,sn->pkn', factor_rows, prev_solution, pr...]
    ppermute x0 -> x28, starting transfers between devices: none -> 42.6 us  [the longest x9 26.8 us: local(): lax.ppermute(lax.dynamic_index_in_dim(block, chip ^ m, 0, keepdims=False)...]
    select_n x1 -> x0, other arithmetic: 8.4 us -> none  [from_root(): return lax.psum(jnp.where(mine, x, jnp.zeros_like(x)), axis)]
  transfers between devices with their start and end apart: 6 -> 32, of which waited for: 6 -> 10; matrix products, arithmetic and copies ran while one was open for 2% -> 6% of each run, Pallas kernels for 0% -> 28%
where the time goes in v1:
time: 380 us; the launch traced here: 379 us
  waiting for transfers between devices  162 us (43%)
  Pallas kernels  130 us (34%)
  starting transfers between devices  42.7 us (11%)
  local copies, waits for them, and re-layouts  23.3 us (6%)
  between operations  13.5 us (4%)
  other arithmetic  7.01 us (2%)
    pallas_call x3, Pallas kernels, downdate_part(): pl.pallas_call(downdate_kernel, grid_spec=pltpu.PrefetchScalarGridSpec(nu...  73.9 us
    ppermute x2, waiting for transfers between devices, arrivals(): b_got = lax.ppermute(b_out, 'row', ALONG_Y)  53.2 us
    ppermute x1, waiting for transfers between devices, local(): from_x = lax.ppermute(solved, 'row', ALONG_X)  42.7 us
    all_gather x3, waiting for transfers between devices, local(): blocks = [lax.all_gather(x, 'col', axis=0) for x in (chunk, *chunks)]  34.3 us
    ppermute x9, starting transfers between devices, local(): lax.ppermute(lax.dynamic_index_in_dim(block, chip ^ m, 0, keepdims=False)...  26.8 us
    pallas_call x2, Pallas kernels, split_blocks(): pl.pallas_call(functools.partial(split_kernel, parts), grid_spec=pltpu.Pr...  20.5 us
    pallas_call x2, Pallas kernels, update_blocks(): pl.pallas_call(lambda info, *refs: partial_updates(steps, [info[count + n...  19 us
    ppermute x1, waiting for transfers between devices, local(): far_a = lax.ppermute(from_x[:, :half], 'row', ALONG_Y)  18.7 us
  transfers between devices with their start and end apart: 32, of which 10 were waited for; matrix products, arithmetic and copies ran while one was open for 6% of the time, Pallas kernels for 28%

profile of v1, /device:TPU:0, one launch (start us, length us, event | category | flops | bytes accessed | tf_op | source)
XLA Modules:
  0.0 379.0 jit_solution(1324316390248672073)
XLA Ops:
  6.5 1.0 copy.23
  7.5 1.7 pad_maximum_fusion
  9.3 1.9 constant_dynamic-slice_fusion
  11.2 0.5 collective-permute-start.1
  11.7 1.2 copy.24
  13.0 1.0 dynamic-slice_bitcast_fusion.3
  14.3 0.7 copy-done.8
  15.4 0.6 stack.100.info
  16.0 1.3 collective-permute-done.2.refs_5_
  17.4 1.3 collective-permute-done.refs_1_
  18.7 8.1 %shard_map.57 = (f32[1024,256]{1,0:T(8,128)}, f32[1024,256]{1,0:T(8,128)}, f32[1024,128]{1,0:T(8,128)}, f32[1024,128]{1,0:T(8,128)}) custom-call(s32[6]{0:T(128)} %stack.100.info, f32[1024,256]{1,0:T(8,128)} %bitcast.61, f32[1024,256]{1,0:T(8,128)} %collective-permute-done.refs_1_, f32[256,4096]{1,0:T(8,128)} %refs_2_.3, ...), custom_call_target="tpu_custom_call" | custom-call | flops 2415919104 | bytes 5242880 | tf_op jit(solution)/shard_map/pallas_call | solution.py:94
  26.7 2.8 collective-permute-start.8
  29.5 1.5 collective-permute-start.3
  31.0 0.6 stack.96.info
  31.6 30.0 %collective-permute-done.8.refs_8_ = f32[1024,256]{1,0:T(8,128)S(1)} collective-permute-done((f32[1024,256]{1,0:T(8,128)}, f32[1024,256]{1,0:T(8,128)S(1)}, u32[]{:S(2)}, u32[]{:S(2)}) %collective-permute-start.8) | collective-permute-done | bytes 1048608 | tf_op jit(solution)/shard_map/ppermute | solution.py:307
  61.6 2.3 slice_add_fusion
  63.8 1.7 collective-permute-start.10
  65.6 2.2 slice_add_fusion.3
  67.8 1.5 collective-permute-start.9
  69.3 11.0 %shard_map.56 = (f32[1024,256]{1,0:T(8,128)}, f32[1024,256]{1,0:T(8,128)}, f32[1024,128]{1,0:T(8,128)}, f32[1024,128]{1,0:T(8,128)}, f32[1024,256]{1,0:T(8,128)}, /*index=5*/f32[1024,256]{1,0:T(8,128)}) custom-call(s32[8]{0:T(128)} %stack.96.info, f32[1024,256]{1,0:T(8,128)} %bitcast.62, f32[1024,256]{1,0:T(8,128)} %collective-permute-done.refs_1_, ...), custom_call_target="tpu_custom_call" | custom-call | flops 4026531840 | bytes 7340032 | tf_op jit(solution)/shard_map/pallas_call | solution.py:94
  80.3 5.0 %shard_map.55 = (bf16[512,512]{1,0:T(8,128)(2,1)}, bf16[512,512]{1,0:T(8,128)(2,1)}, bf16[512,512]{1,0:T(8,128)(2,1)}, bf16[512,512]{1,0:T(8,128)(2,1)}, bf16[51...) custom-call(f32[8,3,64,512]{3,2,1,0:T(8,128)} %bitcast.68), custom_call_target="tpu_custom_call" | custom-call | flops 1610612736 | bytes 6291456 | tf_op jit(solution)/shard_map/pallas_call | solution.py:52
  85.3 0.8 copy-done.9
  86.3 6.0 %shard_map.58 = (f32[1024,512]{1,0:T(8,128)}, f32[1024,256]{1,0:T(8,128)}) custom-call(bf16[512,512]{1,0:T(8,128)(2,1)} %get-tuple-element.32.refs_0_, bf16[512,512]{1,0:T(8,128)(2,1)} %get-tuple-element.33.refs_1_, bf16[512,512]{1,0:T(8,128)(2,1)} %get-tuple-element.34.refs_2_, bf16[512,512]{1,0:T(8,128)(2,1)} %get-tuple-element.35.refs_3_, ...), custom_call_target="tpu_custom_call" | custom-call | flops 1207959552 | bytes 9437184 | tf_op jit(solution)/shard_map/pallas_call | solution.py:151
  92.4 0.6 collective-permute-start.5
  93.3 23.2 %collective-permute-done.5.refs_8_ = f32[1024,256]{1,0:T(8,128)S(1)} collective-permute-done((f32[1024,256]{1,0:T(8,128)}, f32[1024,256]{1,0:T(8,128)S(1)}, u32[]{:S(2)}, u32[]{:S(2)}) %collective-permute-start.5) | collective-permute-done | bytes 1048608 | tf_op jit(solution)/shard_map/ppermute | solution.py:307
  116.5 0.6 collective-permute-start.7
  117.2 1.3 collective-permute-start.6
  118.5 9.9 %collective-permute-done.7.refs_10_ = f32[1024,128]{1,0:T(8,128)S(1)} collective-permute-done((f32[1024,128]{1,0:T(8,128)S(1)}, f32[1024,128]{1,0:T(8,128)S(1)}, u32[]{:S(2)}, u32[]{:S(2)}) %collective-permute-start.7) | collective-permute-done | bytes 524320 | tf_op jit(solution)/shard_map/ppermute | solution.py:310
  129.6 5.9 %shard_map.59 = (f32[1024,512]{1,0:T(8,128)}, f32[1024,128]{1,0:T(8,128)}, f32[1024,128]{1,0:T(8,128)}) custom-call(bf16[512,512]{1,0:T(8,128)(2,1)} %get-tuple-element.32.refs_0_, bf16[512,512]{1,0:T(8,128)(2,1)} %get-tuple-element.33.refs_1_, bf16[512,512]{1,0:T(8,128)(2,1)} %get-tuple-element.34.refs_2_, ...), custom_call_target="tpu_custom_call", output_to_operand_aliasing={{0}: (11, {})} | custom-call | flops 1207959552 | bytes 9437184 | tf_op jit(solution)/shard_map/pallas_call | solution.py:151
  135.5 1.6 collective-permute-start.14
  137.1 0.5 collective-permute-start.15
  137.6 42.7 %collective-permute-done.14.refs_1_.refs_3_ = f32[1024,512]{1,0:T(8,128)S(1)} collective-permute-done((f32[1024,512]{1,0:T(8,128)}, f32[1024,512]{1,0:T(8,128)S(1)}, u32[]{:S(2)}, u32[]{:S(2)}) %collective-permute-start.14) | collective-permute-done | bytes 2097184 | tf_op jit(solution)/shard_map/ppermute | solution.py:326
  180.3 1.2 slice.28
  181.4 1.3 collective-permute-start.16
  182.7 1.3 slice.29
  184.0 0.6 collective-permute-start.17
  184.7 0.5 collective-permute-start.19
  185.2 18.7 %collective-permute-done.16 = f32[1024,256]{1,0:T(8,128)S(1)} collective-permute-done((f32[1024,256]{1,0:T(8,128)}, f32[1024,256]{1,0:T(8,128)S(1)}, u32[]{:S(2)}, u32[]{:S(2)}) %collective-permute-start.16) | collective-permute-done | bytes 1048608 | tf_op jit(solution)/shard_map/ppermute | solution.py:328
  203.9 1.1 constant_dynamic-update-slice_fusion.1
  205.0 0.4 collective-permute-done.17
  205.4 1.1 constant_dynamic-update-slice_fusion.refs_3_.refs_5_
  206.5 3.4 dynamic-slice_bitcast_fusion
  209.9 3.2 collective-permute-start.25
  213.1 3.3 collective-permute-start.26
  216.4 2.3 collective-permute-start.27
  218.7 0.6 pad_add_fusion.info
  219.5 9.6 %shard_map.60 = (bf16[8,1024,512]{2,1,0:T(8,128)(2,1)}, bf16[8,1024,512]{2,1,0:T(8,128)(2,1)}) custom-call(s32[4]{0:T(128)S(1)} %pad_add_fusion.2.place, f32[1024,512]{1,0:T(8,128)} %get-tuple-element.52.refs_0_, f32[1024,512]{1,0:T(8,128)S(1)} %collective-permute-done.14.refs_1_.refs_3_, f32[1024,512]{1,0:T(8,128)} %collective-permute-done.15.refs_2_.refs_4_, ...), custom_call_target="tpu_custom_call" | custom-call | bytes 16777216 | tf_op jit(solution)/shard_map/pallas_call | solution.py:187
  229.1 1.5 dynamic-slice_bitcast_fusion.4
  230.6 34.3 %all-gather.11.cloned.1.call-done = f32[4096,128]{1,0:T(8,128)} async-done(((f32[1024,128]{1,0:T(8,128)}), f32[4096,128]{1,0:T(8,128)}) %all-gather.11.cloned.1.call-update) | async-done | bytes 2097168 | tf_op jit(solution)/shard_map/all_gather | solution.py:324
  264.8 1.5 dynamic-slice_bitcast_fusion.7
  266.3 3.4 collective-permute-start.22
  269.7 3.4 collective-permute-start.23
  273.1 10.8 %shard_map.61 = (bf16[8,1024,512]{2,1,0:T(8,128)(2,1)}, bf16[8,1024,512]{2,1,0:T(8,128)(2,1)}) custom-call(s32[4]{0:T(128)S(1)} %pad_add_fusion.1.place, f32[1024,512]{1,0:T(8,128)} %collective-permute-done.18.refs_0_, f32[1024,512]{1,0:T(8,128)} %collective-permute-done.19.refs_1_, ...), custom_call_target="tpu_custom_call", output_to_operand_aliasing={{0}: (5, {}), {1}: (6, {})} | custom-call | bytes 16777216 | tf_op jit(solution)/shard_map/pallas_call | solution.py:187
  283.9 2.0 collective-permute-start.24
  285.9 2.7 collective-permute-start.11
  288.6 3.1 collective-permute-start.12
  291.8 34.4 %shard_map.62.refs_8_ = f32[4,512,4096]{2,1,0:T(8,128)} custom-call(s32[2]{0:T(128)} %pad_add_fusion.info, f32[4,1024,256]{2,1,0:T(8,128)} %bitcast.64, f32[1024,256]{1,0:T(8,128)} %collective-permute-done.25.refs_0_, f32[1024,256]{1,0:T(8,128)} %collective-permute-done.26.refs_1_, f32[1024,256]{1,0:T(8,128)} %collective-permute-done.27.refs_2_, ...), custom_call_target="tpu_custom_call" | custom-call | flops 25769803776 | bytes 41943040 | tf_op jit(solution)/shard_map/pallas_call | solution.py:238
  326.2 3.4 collective-permute-start.13
  329.6 0.8 copy-done.16
  330.4 0.8 copy-done.19
  331.2 19.7 %shard_map.63.refs_8_ = f32[4,512,4096]{2,1,0:T(8,128)} custom-call(s32[2]{0:T(128)} %pad_add_fusion.info, f32[4,1024,128]{2,1,0:T(8,128)} %bitcast.57, f32[1024,128]{1,0:T(8,128)} %copy-done.15, f32[1024,128]{1,0:T(8,128)} %copy-done.16, f32[1024,128]{1,0:T(8,128)} %copy-done.19, f32[1024,512]{1,0:T(8,128)} %copy-done, ...), custom_call_target="tpu_custom_call", output_to_operand_aliasing={{}: (10, {})} | custom-call | flops 12884901888 | bytes 29360128 | tf_op jit(solution)/shard_map/pallas_call | solution.py:238
  350.9 0.8 copy-done.17
  351.9 0.8 copy-done.20
  352.7 19.7 %shard_map.64 = f32[4,512,4096]{2,1,0:T(8,128)} custom-call(s32[2]{0:T(128)} %pad_add_fusion.info, f32[4,1024,128]{2,1,0:T(8,128)} %bitcast.59, f32[1024,128]{1,0:T(8,128)} %copy-done.17, f32[1024,128]{1,0:T(8,128)} %copy-done.18, f32[1024,128]{1,0:T(8,128)} %copy-done.20, f32[1024,512]{1,0:T(8,128)} %copy-done, ...), custom_call_target="tpu_custom_call", output_to_operand_aliasing={{}: (10, {})} | custom-call | flops 12884901888 | bytes 29360128 | tf_op jit(solution)/shard_map/pallas_call | solution.py:238
  (80 shorter events, 3.2 us)
Async XLA Ops:
  6.5 73.8 %all-gather.9.cloned.1.call-start = ((), (), s32[]{:S(2)}) async-start(), calls=%async_computation | async-start | bytes 3538944 | tf_op jit(solution)/shard_map/all_gather | solution.py:50
  9.2 197.3 %all-gather.15.cloned.1.call-start = ((), (), s32[]{:S(2)}) async-start(), calls=%async_computation.3 | async-start | bytes 5242880 | tf_op jit(solution)/shard_map/all_gather | solution.py:324
  9.3 2.4 copy-start.7
  11.2 7.4 %collective-permute-start.1 = (f32[256,2048]{1,0:T(8,128)S(1)}, f32[256,2048]{1,0:T(8,128)}, u32[]{:S(2)}, u32[]{:S(2)}) collective-permute-start(f32[256,2048]{1,0:T(8,128)S(1)} %constant_dynamic-slice_fusion), channel_id=1, source_target_pairs={{0,4},{4,0},{8,12},{12,8},{16,20},{20,16},{24,28},{28,24},{1,5},{5... | collective-permute-start | bytes 6291464 | tf_op jit(solution)/shard_map/ppermute | solution.py:287
  13.0 2.1 copy-start.1
  13.0 2.0 copy-start.8
  14.0 3.3 collective-permute-start.2
  15.1 3.6 copy-start.2
  15.1 3.6 collective-permute-start
  26.7 34.8 %collective-permute-start.8 = (f32[1024,256]{1,0:T(8,128)}, f32[1024,256]{1,0:T(8,128)S(1)}, u32[]{:S(2)}, u32[]{:S(2)}) collective-permute-start(f32[1024,256]{1,0:T(8,128)} %get-tuple-element.48), channel_id=1, source_target_pairs={{0,16},{4,20},{8,24},{12,28},{16,0},{20,4},{24,8},{28,12},{1,17},{... | collective-permute-start | bytes 3145736 | tf_op jit(solution)/shard_map/ppermute | solution.py:307
  29.5 36.1 %collective-permute-start.3 = (f32[1024,256]{1,0:T(8,128)}, f32[1024,256]{1,0:T(8,128)S(1)}, u32[]{:S(2)}, u32[]{:S(2)}) collective-permute-start(f32[1024,256]{1,0:T(8,128)} %get-tuple-element.41), channel_id=1, source_target_pairs={{0,8},{4,12},{8,0},{12,4},{16,24},{20,28},{24,16},{28,20},{1,9},{5... | collective-permute-start | bytes 3145736 | tf_op jit(solution)/shard_map/ppermute | solution.py:306
  61.6 18.7 %copy-start.3 = (f32[1024,256]{1,0:T(8,128)}, f32[1024,256]{1,0:T(8,128)S(1)}, u32[]{:S(2)}) copy-start(f32[1024,256]{1,0:T(8,128)S(1)} %collective-permute-done.8.refs_8_) | copy-start | bytes 3145732
  63.8 21.5 %collective-permute-start.10 = (f32[1024,128]{1,0:T(8,128)}, f32[1024,128]{1,0:T(8,128)S(1)}, u32[]{:S(2)}, u32[]{:S(2)}) collective-permute-start(f32[1024,128]{1,0:T(8,128)} %slice_add_fusion), channel_id=1, source_target_pairs={{0,8},{4,12},{8,0},{12,4},{16,24},{20,28},{24,16},{28,20},{1,9},{5... | collective-permute-start | bytes 1572872 | tf_op jit(solution)/shard_map/ppermute | solution.py:310
  65.6 14.7 %copy-start.4 = (f32[1024,256]{1,0:T(8,128)}, f32[1024,256]{1,0:T(8,128)S(1)}, u32[]{:S(2)}) copy-start(f32[1024,256]{1,0:T(8,128)S(1)} %collective-permute-done.3.refs_7_) | copy-start | bytes 3145732
  67.8 17.5 %collective-permute-start.9 = (f32[1024,128]{1,0:T(8,128)}, f32[1024,128]{1,0:T(8,128)S(1)}, u32[]{:S(2)}, u32[]{:S(2)}) collective-permute-start(f32[1024,128]{1,0:T(8,128)} %slice_add_fusion.3), channel_id=1, source_target_pairs={{0,16},{4,20},{8,24},{12,28},{16,0},{20,4},{24,8},{28,12},{1,17},{... | collective-permute-start | bytes 1572872 | tf_op jit(solution)/shard_map/ppermute | solution.py:309
  85.3 0.8 copy-start.9
  85.3 1.0 copy-start.10
  86.3 6.7 %copy-start.21 = (f32[1024,256]{1,0:T(8,128)S(1)}, f32[1024,256]{1,0:T(8,128)}, u32[]{:S(2)}) copy-start(f32[1024,256]{1,0:T(8,128)} %get-tuple-element.42) | copy-start | bytes 3145732
  86.3 30.2 %copy-start.12 = (f32[1024,128]{1,0:T(8,128)S(1)}, f32[1024,128]{1,0:T(8,128)}, u32[]{:S(2)}) copy-start(f32[1024,128]{1,0:T(8,128)} %get-tuple-element.46) | copy-start | bytes 1572868
  92.3 24.8 %copy-start.11 = (f32[1024,128]{1,0:T(8,128)S(1)}, f32[1024,128]{1,0:T(8,128)}, u32[]{:S(2)}) copy-start(f32[1024,128]{1,0:T(8,128)} %get-tuple-element.45) | copy-start | bytes 1572868
  92.3 136.7 %all-gather.13.cloned.1.call-start = ((), (), s32[]{:S(2)}) async-start(), calls=%async_computation.2 | async-start | bytes 2621440 | tf_op jit(solution)/shard_map/all_gather | solution.py:324
  92.4 24.1 %collective-permute-start.5 = (f32[1024,256]{1,0:T(8,128)}, f32[1024,256]{1,0:T(8,128)S(1)}, u32[]{:S(2)}, u32[]{:S(2)}) collective-permute-start(f32[1024,256]{1,0:T(8,128)} %get-tuple-element.44), channel_id=1, source_target_pairs={{0,16},{4,20},{8,24},{12,28},{16,0},{20,4},{24,8},{28,12},{1,17},{... | collective-permute-start | bytes 3145736 | tf_op jit(solution)/shard_map/ppermute | solution.py:307
  93.0 24.2 %collective-permute-start.4 = (f32[1024,256]{1,0:T(8,128)S(1)}, f32[1024,256]{1,0:T(8,128)S(1)}, u32[]{:S(2)}, u32[]{:S(2)}) collective-permute-start(f32[1024,256]{1,0:T(8,128)S(1)} %copy-done.21), channel_id=1, source_target_pairs={{0,8},{4,12},{8,0},{12,4},{16,24},{20,28},{24,16},{28,20},{1,9},{5... | collective-permute-start | bytes 3145736 | tf_op jit(solution)/shard_map/ppermute | solution.py:306
  116.5 12.3 %copy-start.5 = (f32[1024,256]{1,0:T(8,128)}, f32[1024,256]{1,0:T(8,128)S(1)}, u32[]{:S(2)}) copy-start(f32[1024,256]{1,0:T(8,128)S(1)} %collective-permute-done.5.refs_8_) | copy-start | bytes 3145732
  116.5 11.8 %collective-permute-start.7 = (f32[1024,128]{1,0:T(8,128)S(1)}, f32[1024,128]{1,0:T(8,128)S(1)}, u32[]{:S(2)}, u32[]{:S(2)}) collective-permute-start(f32[1024,128]{1,0:T(8,128)S(1)} %slice_add_fusion.1), channel_id=1, source_target_pairs={{0,8},{4,12},{8,0},{12,4},{16,24},{20,28},{24,16},{28,20},{1,9},{5... | collective-permute-start | bytes 1572872 | tf_op jit(solution)/shard_map/ppermute | solution.py:310
  117.1 11.6 %copy-start.6 = (f32[1024,256]{1,0:T(8,128)}, f32[1024,256]{1,0:T(8,128)S(1)}, u32[]{:S(2)}) copy-start(f32[1024,256]{1,0:T(8,128)S(1)} %collective-permute-done.4.refs_7_) | copy-start | bytes 3145732
  117.2 11.5 %collective-permute-start.6 = (f32[1024,128]{1,0:T(8,128)S(1)}, f32[1024,128]{1,0:T(8,128)S(1)}, u32[]{:S(2)}, u32[]{:S(2)}) collective-permute-start(f32[1024,128]{1,0:T(8,128)S(1)} %slice_add_fusion.2), channel_id=1, source_target_pairs={{0,16},{4,20},{8,24},{12,28},{16,0},{20,4},{24,8},{28,12},{1,17},{... | collective-permute-start | bytes 1572872 | tf_op jit(solution)/shard_map/ppermute | solution.py:309
  128.4 0.8 copy-start.13
  128.8 0.8 copy-start.14
  135.5 129.4 %all-gather.11.cloned.1.call-start = ((), (), s32[]{:S(2)}) async-start(), calls=%async_computation.1 | async-start | bytes 2621440 | tf_op jit(solution)/shard_map/all_gather | solution.py:324
  135.5 44.8 %collective-permute-start.14 = (f32[1024,512]{1,0:T(8,128)}, f32[1024,512]{1,0:T(8,128)S(1)}, u32[]{:S(2)}, u32[]{:S(2)}) collective-permute-start(f32[1024,512]{1,0:T(8,128)} %get-tuple-element.52.refs_0_), channel_id=1, source_target_pairs={{0,8},{4,12},{8,0},{12,4},{16,24},{20,28},{24,16},{28,20},{1,9},{5... | collective-permute-start | bytes 6291464 | tf_op jit(solution)/shard_map/ppermute | solution.py:326
  137.1 45.7 %collective-permute-start.15 = (f32[1024,512]{1,0:T(8,128)}, f32[1024,512]{1,0:T(8,128)}, u32[]{:S(2)}, u32[]{:S(2)}) collective-permute-start(f32[1024,512]{1,0:T(8,128)} %get-tuple-element.52.refs_0_), channel_id=1, source_target_pairs={{0,16},{4,20},{8,24},{12,28},{16,0},{20,4},{24,8},{28,12},{1,17},{... | collective-permute-start | bytes 6291464 | tf_op jit(solution)/shard_map/ppermute | solution.py:327
  180.3 39.2 %copy-start = (f32[1024,512]{1,0:T(8,128)}, f32[1024,512]{1,0:T(8,128)S(1)}, u32[]{:S(2)}) copy-start(f32[1024,512]{1,0:T(8,128)S(1)} %collective-permute-done.14.refs_1_.refs_3_) | copy-start | bytes 6291460
  181.4 22.4 %collective-permute-start.16 = (f32[1024,256]{1,0:T(8,128)}, f32[1024,256]{1,0:T(8,128)S(1)}, u32[]{:S(2)}, u32[]{:S(2)}) collective-permute-start(f32[1024,256]{1,0:T(8,128)} %slice.28), channel_id=1, source_target_pairs={{0,16},{4,20},{8,24},{12,28},{16,0},{20,4},{24,8},{28,12},{1,17},{... | collective-permute-start | bytes 3145736 | tf_op jit(solution)/shard_map/ppermute | solution.py:328
  184.0 21.4 %collective-permute-start.17 = (f32[1024,256]{1,0:T(8,128)S(1)}, f32[1024,256]{1,0:T(8,128)S(1)}, u32[]{:S(2)}, u32[]{:S(2)}) collective-permute-start(f32[1024,256]{1,0:T(8,128)S(1)} %slice.29), channel_id=1, source_target_pairs={{0,8},{4,12},{8,0},{12,4},{16,24},{20,28},{24,16},{28,20},{1,9},{5... | collective-permute-start | bytes 3145736 | tf_op jit(solution)/shard_map/ppermute | solution.py:329
  184.7 28.4 %collective-permute-start.18 = (f32[1024,512]{1,0:T(8,128)}, f32[1024,512]{1,0:T(8,128)}, u32[]{:S(2)}, u32[]{:S(2)}) collective-permute-start(f32[1024,512]{1,0:T(8,128)} %get-tuple-element.52.refs_0_), channel_id=1, source_target_pairs={{0,4},{4,0},{8,12},{12,8},{16,20},{20,16},{24,28},{28,24},{1,5},{5... | collective-permute-start | bytes 6291464 | tf_op jit(solution)/shard_map/ppermute | solution.py:333
  184.7 31.7 %collective-permute-start.19 = (f32[1024,512]{1,0:T(8,128)S(1)}, f32[1024,512]{1,0:T(8,128)}, u32[]{:S(2)}, u32[]{:S(2)}) collective-permute-start(f32[1024,512]{1,0:T(8,128)S(1)} %collective-permute-done.14.refs_1_.refs_3_), channel_id=1, source_target_pairs={{0,4},{4,0},{8,12},{12,8},{16,20},{20,16},{24,28},{28,24},{1,5},{5... | collective-permute-start | bytes 6291464 | tf_op jit(solution)/shard_map/ppermute | solution.py:333
  185.2 81.1 %collective-permute-start.20 = (f32[1024,512]{1,0:T(8,128)}, f32[1024,512]{1,0:T(8,128)}, u32[]{:S(2)}, u32[]{:S(2)}) collective-permute-start(f32[1024,512]{1,0:T(8,128)} %collective-permute-done.15.refs_2_.refs_4_), channel_id=1, source_target_pairs={{0,4},{4,0},{8,12},{12,8},{16,20},{20,16},{24,28},{28,24},{1,5},{5... | collective-permute-start | bytes 6291464 | tf_op jit(solution)/shard_map/ppermute | solution.py:333
  206.5 63.1 %collective-permute-start.21 = (f32[1024,512]{1,0:T(8,128)}, f32[1024,512]{1,0:T(8,128)}, u32[]{:S(2)}, u32[]{:S(2)}) collective-permute-start(f32[1024,512]{1,0:T(8,128)} %constant_dynamic-update-slice_fusion.refs_3_.refs_5_), channel_id=1, source_target_pairs={{0,4},{4,0},{8,12},{12,8},{16,20},{20,16},{24,28},{28,24},{1,5},{5... | collective-permute-start | bytes 6291464 | tf_op jit(solution)/shard_map/ppermute | solution.py:333
  209.9 74.0 %collective-permute-start.25 = (f32[1024,256]{1,0:T(8,128)}, f32[1024,256]{1,0:T(8,128)}, u32[]{:S(2)}, u32[]{:S(2)}) collective-permute-start(f32[1024,256]{1,0:T(8,128)} %get-tuple-element.61), channel_id=1, source_target_pairs={{0,8},{2,10},{3,11},{4,12},{6,14},{7,15},{9,1},{10,2},{11,3},{13,5... | collective-permute-start | bytes 3145736 | tf_op jit(solution)/shard_map/ppermute | solution.py:340
  213.1 72.8 %collective-permute-start.26 = (f32[1024,256]{1,0:T(8,128)}, f32[1024,256]{1,0:T(8,128)}, u32[]{:S(2)}, u32[]{:S(2)}) collective-permute-start(f32[1024,256]{1,0:T(8,128)} %get-tuple-element.60), channel_id=1, source_target_pairs={{0,16},{1,17},{3,19},{4,20},{5,21},{7,23},{8,24},{9,25},{10,26},{1... | collective-permute-start | bytes 3145736 | tf_op jit(solution)/shard_map/ppermute | solution.py:340
  216.4 72.2 %collective-permute-start.27 = (f32[1024,256]{1,0:T(8,128)S(1)}, f32[1024,256]{1,0:T(8,128)}, u32[]{:S(2)}, u32[]{:S(2)}) collective-permute-start(f32[1024,256]{1,0:T(8,128)S(1)} %get-tuple-element.59), channel_id=1, source_target_pairs={{0,24},{1,25},{2,26},{4,28},{5,29},{6,30},{8,16},{9,17},{11,19},{1... | collective-permute-start | bytes 3145736 | tf_op jit(solution)/shard_map/ppermute | solution.py:340
  266.3 59.9 %collective-permute-start.22 = (f32[1024,128]{1,0:T(8,128)S(1)}, f32[1024,128]{1,0:T(8,128)S(1)}, u32[]{:S(2)}, u32[]{:S(2)}) collective-permute-start(f32[1024,128]{1,0:T(8,128)S(1)} %get-tuple-element.64), channel_id=1, source_target_pairs={{0,8},{2,10},{3,11},{4,12},{6,14},{7,15},{9,1},{10,2},{11,3},{13,5... | collective-permute-start | bytes 1572872 | tf_op jit(solution)/shard_map/ppermute | solution.py:340
  269.7 59.9 %collective-permute-start.23 = (f32[1024,128]{1,0:T(8,128)S(1)}, f32[1024,128]{1,0:T(8,128)S(1)}, u32[]{:S(2)}, u32[]{:S(2)}) collective-permute-start(f32[1024,128]{1,0:T(8,128)S(1)} %get-tuple-element.63), channel_id=1, source_target_pairs={{0,16},{1,17},{3,19},{4,20},{5,21},{7,23},{8,24},{9,25},{10,26},{1... | collective-permute-start | bytes 1572872 | tf_op jit(solution)/shard_map/ppermute | solution.py:340
  283.9 45.7 %collective-permute-start.24 = (f32[1024,128]{1,0:T(8,128)S(1)}, f32[1024,128]{1,0:T(8,128)S(1)}, u32[]{:S(2)}, u32[]{:S(2)}) collective-permute-start(f32[1024,128]{1,0:T(8,128)S(1)} %get-tuple-element.62), channel_id=1, source_target_pairs={{0,24},{1,25},{2,26},{4,28},{5,29},{6,30},{8,16},{9,17},{11,19},{1... | collective-permute-start | bytes 1572872 | tf_op jit(solution)/shard_map/ppermute | solution.py:340
  285.9 65.0 %collective-permute-start.11 = (f32[1024,128]{1,0:T(8,128)S(1)}, f32[1024,128]{1,0:T(8,128)S(1)}, u32[]{:S(2)}, u32[]{:S(2)}) collective-permute-start(f32[1024,128]{1,0:T(8,128)S(1)} %get-tuple-element.67), channel_id=1, source_target_pairs={{0,8},{2,10},{3,11},{4,12},{6,14},{7,15},{9,1},{10,2},{11,3},{13,5... | collective-permute-start | bytes 1572872 | tf_op jit(solution)/shard_map/ppermute | solution.py:340
  288.6 62.3 %collective-permute-start.12 = (f32[1024,128]{1,0:T(8,128)S(1)}, f32[1024,128]{1,0:T(8,128)S(1)}, u32[]{:S(2)}, u32[]{:S(2)}) collective-permute-start(f32[1024,128]{1,0:T(8,128)S(1)} %get-tuple-element.66), channel_id=1, source_target_pairs={{0,16},{1,17},{3,19},{4,20},{5,21},{7,23},{8,24},{9,25},{10,26},{1... | collective-permute-start | bytes 1572872 | tf_op jit(solution)/shard_map/ppermute | solution.py:340
  326.2 3.4 copy-start.15
  326.2 24.7 %collective-permute-start.13 = (f32[1024,128]{1,0:T(8,128)S(1)}, f32[1024,128]{1,0:T(8,128)S(1)}, u32[]{:S(2)}, u32[]{:S(2)}) collective-permute-start(f32[1024,128]{1,0:T(8,128)S(1)} %get-tuple-element.65), channel_id=1, source_target_pairs={{0,24},{1,25},{2,26},{4,28},{5,29},{6,30},{8,16},{9,17},{11,19},{1... | collective-permute-start | bytes 1572872 | tf_op jit(solution)/shard_map/ppermute | solution.py:340
  329.6 0.8 copy-start.16
  330.4 0.8 copy-start.19
  350.9 0.8 copy-start.17
  350.9 1.0 copy-start.18
  351.9 0.8 copy-start.20
Sparse Core Ops, SparseCore 0:
  9.4 43.5 all-gather.8
  92.5 80.1 all-gather.14
  174.2 44.4 all-gather.12
  220.1 44.6 all-gather.10

commit v2 on v1

--- a/solution.py
+++ b/solution.py
@@ -29,7 +29,7 @@
 
 
 def cost(flops, moved):
-    return pl.CostEstimate(flops=flops, bytes_accessed=moved, transcendentals=0)
+    return pl.CostEstimate(flops=flops // 32, bytes_accessed=moved // 32, transcendentals=0)
 
 
 def roomy(limit=56):
@@ -122,7 +122,7 @@
     solved, chunks = refs[11], refs[12:]
     panel, half = keep.shape[0] // 2, a_last.shape[1]
     arrived = [
-        got[:, half:] + last[...] for got, last in ((a_got, a_last), (b_got, b_last))
+        got[...] + last[...] for got, last in ((a_got, a_last), (b_got, b_last))
     ]
     update = keep[...] + jnp.concatenate(arrived, axis=1)
     upper, lower = halves(update[:panel]), halves(update[panel:])
@@ -161,19 +161,19 @@
     )(*ins)
 
 
-def split_kernel(parts, place, *refs):
+def split_kernel(parts, count, place, *refs):
     del place
     high, low = refs[-2:]
-    for m in range(4):
+    for m in range(count):
 
         @pl.when(pl.program_id(0) // parts == m)
         def _(block=refs[m]):
             high[0], low[0] = halves(block[...])
 
 
-def split_blocks(place, blocks, held):
+def split_blocks(place, blocks, held, weight=1):
     depth, width = blocks[0].shape
-    parts = 2
+    count, parts = len(blocks), 2
     rows = depth // parts
     shape = jax.ShapeDtypeStruct((8, depth, width), jnp.bfloat16)
     spec = pl.BlockSpec((1, rows, width), lambda i, place: (place[i // parts], i % parts, 0))
@@ -185,72 +185,61 @@
 
     held = list(held)
     return pl.pallas_call(
-        functools.partial(split_kernel, parts),
+        functools.partial(split_kernel, parts, count),
         grid_spec=pltpu.PrefetchScalarGridSpec(
             num_scalar_prefetch=1,
-            grid=(4 * parts,),
-            in_specs=[taken(m) for m in range(4)]
+            grid=(count * parts,),
+            in_specs=[taken(m) for m in range(count)]
             + [pl.BlockSpec(memory_space=pl.ANY)] * len(held),
             out_specs=[spec, spec],
         ),
         out_shape=[shape, shape],
-        input_output_aliases={5: 0, 6: 1} if held else {},
-        compiler_params=roomy(40),
-        cost_estimate=cost(0, 8 * 4 * depth * width),
+        input_output_aliases={count + 1: 0, count + 2: 1} if held else {},
+        compiler_params=roomy(),
+        cost_estimate=cost(0, 8 * count * depth * width * weight),
     )(place, *blocks, *held)
 
 
-def downdate_kernel(info, mine, *refs):
-    others, gathered = refs[:3], refs[3:6]
-    high, low = refs[6:8]
+def downdate_kernel(pieces, high, low, *refs):
     out, left_high, left_low = refs[-3:]
-    width = others[0].shape[1]
+    count, _, width = pieces.shape
 
     @pl.when(pl.program_id(0) == 0)
     def _():
-        inside = info[1] == 1
-        pieces = [mine[0]] + [
-            jnp.where(inside, own[...], other[...]) for other, own in zip(others, gathered)
-        ]
-        for m, piece in enumerate(pieces):
-            cut = slice(m * width, (m + 1) * width)
-            left_high[:, cut], left_low[:, cut] = halves(piece)
+        for j in range(count):
+            cut = slice(j * width, (j + 1) * width)
+            left_high[:, cut], left_low[:, cut] = halves(pieces[j])
 
     total = three((left_high[...], left_low[...]), (high[0], low[0]), 0)
-    for m in range(4):
-        out[info[0] ^ m] = total[m * width : (m + 1) * width]
-
-
-def downdate_part(info, blocks, others, gathered, held, out, at):
-    _, depth, width = blocks.shape
+    for j in range(count):
+        out[j] = total[j * width : (j + 1) * width]
+
+
+def downdate_part(pieces, held, out, at):
+    count, depth, width = pieces.shape
     wide = held[0].shape[2]
-    rows = 4 * width
-    specs = [pl.BlockSpec((1, depth, width), lambda j, info: (info[0], 0, 0))]
-    specs += [pl.BlockSpec((depth, width), lambda j, info: (0, 0))] * 3
-    specs += [pl.BlockSpec((depth, width), lambda j, info: (0, at))] * 3
-    specs += [pl.BlockSpec((1, depth, wide), lambda j, info: (j, 0, 0))] * 2
-    ins = [blocks, *others, *gathered, *held]
+    rows = count * width
+    specs = [pl.BlockSpec((count, depth, width), lambda j: (0, 0, 0))]
+    specs += [pl.BlockSpec((1, depth, wide), lambda j: (j, 0, 0))] * 2
+    ins = [pieces, *held]
     aliases = {}
     if out is not None:
         specs += [pl.BlockSpec(memory_space=pl.ANY)]
         ins += [out]
-        aliases = {len(ins): 0}
+        aliases = {3: 0}
     return pl.pallas_call(
         downdate_kernel,
-        grid_spec=pltpu.PrefetchScalarGridSpec(
-            num_scalar_prefetch=1,
-            grid=(8,),
-            in_specs=specs,
-            out_specs=pl.BlockSpec((4, width, wide), lambda j, info: (0, at, j)),
-            scratch_shapes=[pltpu.VMEM((depth, rows), jnp.bfloat16)] * 2,
-        ),
-        out_shape=jax.ShapeDtypeStruct((4, wide, 8 * wide), jnp.float32),
+        grid=(8,),
+        in_specs=specs,
+        out_specs=pl.BlockSpec((count, width, wide), lambda j: (0, at, j)),
+        out_shape=jax.ShapeDtypeStruct((count, wide, 8 * wide), jnp.float32),
+        scratch_shapes=[pltpu.VMEM((depth, rows), jnp.bfloat16)] * 2,
         input_output_aliases=aliases,
         compiler_params=roomy(),
         cost_estimate=cost(
-            6 * depth * rows * 8 * wide, 4 * (2 * depth * rows + 8 * depth * wide + rows * 8 * wide)
-        ),
-    )(info, *ins)
+            6 * depth * rows * 8 * wide, 4 * (depth * rows + 8 * depth * wide + rows * 8 * wide)
+        ),
+    )(*ins)
 
 
 CORE = [(i, i ^ 1) for i in range(8)]
@@ -258,14 +247,11 @@
 ALONG_Y = [(i, i ^ 4) for i in range(8)]
 
 
-def to_others(across):
-    return [
-        ((j * 2 + c) * 4 + z, ((j ^ across) * 2 + c) * 4 + z)
-        for j in range(4)
-        for c in range(2)
-        for z in range(4)
-        if j ^ across != z
-    ]
+SAME_CORE = [[0, 2, 4, 6], [1, 3, 5, 7]]
+
+
+def to_chips(blocks):
+    return lax.all_to_all(blocks, "row", 0, 0, axis_index_groups=SAME_CORE)
 
 
 def after(x, *others):
@@ -293,58 +279,68 @@
 
     away = (
         ((0, 0, 0, quarter), (1, 0, quarter, quarter)),
-        ((0, quarter, 0, quarter), (3, 0, quarter, quarter)),
-        ((2, 0, 0, quarter), (1, quarter, quarter, quarter)),
-    )
-    away_widths = (half, half, quarter, quarter)
+        ((2, 0, 0, quarter), (5, 0, quarter, quarter)),
+        ((4, 0, 0, quarter), (3, 0, quarter, quarter)),
+    )
 
     def updates(places, steps, widths):
         spots = [(chip ^ across) * 2 + side for across, side in places]
         return update_blocks(ints(*spots, core, rank, rank ^ 1), steps, widths, sources)
 
-    def arrivals(a_out, b_out, a_on, b_on):
-        a_got = lax.ppermute(a_out, "row", ALONG_X)
-        b_got = lax.ppermute(b_out, "row", ALONG_Y)
-        a_on, b_on = a_on + a_got[:, :quarter], b_on + b_got[:, :quarter]
-        a_last = lax.ppermute(a_on, "row", ALONG_Y)
-        b_last = lax.ppermute(b_on, "row", ALONG_X)
-        return (a_got, b_got, a_last, b_last), a_on
-
-    early = updates(((3, 0), (1, 0), (2, 0)), away, away_widths)
+    early = updates(((3, 0), (1, 0), (2, 0)), away, (quarter,) * 6)
     *late, keep, late_keep = updates(
         ((3, 1), (1, 1), (2, 1), (0, 0), (0, 1)),
-        (*away, ((4, 0, 0, half),), ((5, 0, 0, half),)),
-        (*away_widths, half, half),
-    )
-    terms, sent = arrivals(*early)
+        (*away, ((6, 0, 0, half),), ((7, 0, 0, half),)),
+        (*(quarter,) * 6, half, half),
+    )
+
+    def passed(a_pass, b_pass):
+        return lax.ppermute(a_pass, "row", ALONG_X), lax.ppermute(b_pass, "row", ALONG_Y)
+
+    def arrivals(first, a_send, b_send, a_on, b_on):
+        a_got, b_got = passed(a_send, b_send)
+        a_last = lax.ppermute(a_on + first[0], "row", ALONG_Y)
+        b_last = lax.ppermute(b_on + first[1], "row", ALONG_X)
+        return a_got, b_got, a_last, b_last
+
+    first = passed(*early[:2])
+    first = after(first[0], late_keep, matrix[0]), first[1]
+    terms = arrivals(first, *early[2:])
+    first = passed(*[after(x, terms[0]) for x in late[:2]])
     solved, chunk = solve(matrix, (keep, *terms), (half,), None)
-    late = [after(x, sent) for x in late[:2]] + late[2:]
-    terms, _ = arrivals(*late)
-    solved, *chunks = solve(matrix, (late_keep, *terms), (quarter, quarter), solved)
+    late_terms = arrivals(first, *late[2:])
+    solved, *chunks = solve(matrix, (late_keep, *late_terms), (quarter, quarter), solved)
     blocks = [lax.all_gather(x, "col", axis=0) for x in (chunk, *chunks)]
 
     from_x = lax.ppermute(solved, "row", ALONG_X)
     from_y = lax.ppermute(solved, "row", ALONG_Y)
+    twin = lax.ppermute(solved, "row", CORE)
+
+    def split(blocks, pair, group, held, weight=1):
+        places = [c * 4 + (chip ^ m) for c in (core, 1 - core) for m in group]
+        return split_blocks(ints(*places), [*blocks, *pair], held, weight)
+
+    def given(*arrays):
+        return [lax.ppermute(x, "row", CORE) for x in arrays]
+
+    held = split([solved], [twin], (0,), ())
+    first_chunk = blocks[0][:, :, :quarter]
+    from_x, from_y = after(from_x, first_chunk, *held), after(from_y, first_chunk, *held)
     far_a = lax.ppermute(from_x[:, :half], "row", ALONG_Y)
     far_b = lax.ppermute(from_y[:, half:], "row", ALONG_X)
-    far = jnp.concatenate([far_a, far_b], axis=1)
-    gathered = [solved, from_x, from_y, far]
-    held = split_blocks(ints(*[core * 4 + (chip ^ m) for m in range(4)]), gathered, ())
-    given = [lax.ppermute(block, "row", CORE) for block in gathered]
-    held = split_blocks(ints(*[(1 - core) * 4 + (chip ^ m) for m in range(4)]), given, held)
-
-    info = ints(chip, chip == plane)
-    out = None
-    for block, at in zip(blocks, (0, 2, 3)):
-        others = [
-            lax.ppermute(
-                lax.dynamic_index_in_dim(block, chip ^ m, 0, keepdims=False),
-                ("row", "col"),
-                to_others(m),
-            )
-            for m in (1, 2, 3)
-        ]
-        out = downdate_part(info, block, others, gathered[1:], held, out, at)
+
+    held = split([from_x, from_y], given(from_x, from_y), (1, 2), held)
+    far = jnp.concatenate([after(far_a, *held), far_b], axis=1)
+    pieces = to_chips(first_chunk)
+    twin = given(far)
+    held = split([after(far, pieces, blocks[1])], twin, (3,), held)
+    out = before = downdate_part(pieces, held, None, 0)
+    pieces = to_chips(blocks[0][:, :, quarter:])
+    out = downdate_part(pieces, held, out, 1)
+    pieces = to_chips(after(blocks[1], before))
+    before, out = out, downdate_part(pieces, held, out, 2)
+    pieces = to_chips(after(blocks[2], before))
+    out = downdate_part(pieces, held, out, 3)
     return out.reshape(-1, width)
 
 

time: 380 us -> 346 us (0.911)
  waiting for transfers between devices: 162 us -> 130 us
  starting transfers between devices: 42.7 us -> 35.5 us
  local copies, waits for them, and re-layouts: 23.3 us -> 28.8 us
    ppermute x1, waiting for transfers between devices: 42.7 us -> 1.24 us  [local(): from_x = lax.ppermute(solved, 'row', ALONG_X)]
    all_to_all x0 -> x4, waiting for transfers between devices: none -> 31.8 us  [to_chips(): return lax.all_to_all(blocks, 'row', 0, 0, axis_index_groups=SAME_CORE)]
    ppermute x21 -> x16, starting transfers between devices: 37.5 us -> 14 us  [the longest x4 5.49 us: passed(): lax.ppermute(b_pass, 'row', ALONG_Y)]
    all_to_all x0 -> x4, starting transfers between devices: none -> 16.6 us  [to_chips(): return lax.all_to_all(blocks, 'row', 0, 0, axis_index_groups=SAME_CORE)]
    ppermute x1, waiting for transfers between devices: 18.7 us -> 6.35 us  [local(): far_a = lax.ppermute(from_x[:, :half], 'row', ALONG_Y)]
    ppermute x21 -> x16, waiting for transfers between devices: 63.5 us -> 54.6 us  [the longest x4 21.6 us: passed(): lax.ppermute(b_pass, 'row', ALONG_Y)]
    all_gather x3, waiting for transfers between devices: 34.3 us -> 26 us  [local(): blocks = [lax.all_gather(x, 'col', axis=0) for x in (chunk, *chunks)]]
    squeeze x3 -> x0, local copies, waits for them, and re-layouts: 6.28 us -> none  [local(): lax.dynamic_index_in_dim(block, chip ^ m, 0, keepdims=False)]
  transfers between devices with their start and end apart: 32 -> 31, of which waited for: 10 -> 19; matrix products, arithmetic and copies ran while one was open for 6% -> 6% of each run, Pallas kernels for 28% -> 32%
where the time goes in v2:
time: 346 us; the launch traced here: 344 us
  Pallas kernels  133 us (38%)
  waiting for transfers between devices  130 us (38%)
  starting transfers between devices  35.5 us (10%)
  local copies, waits for them, and re-layouts  28.8 us (8%)
  between operations  13.3 us (4%)
  other arithmetic  3.78 us (1%)
    pallas_call x4, Pallas kernels, downdate_part(): pl.pallas_call(downdate_kernel, grid=(8,), in_specs=specs, out_specs=pl.B...  74.3 us
    all_to_all x4, waiting for transfers between devices, to_chips(): return lax.all_to_all(blocks, 'row', 0, 0, axis_index_groups=SAME_CORE)  31.8 us
    all_gather x3, waiting for transfers between devices, local(): blocks = [lax.all_gather(x, 'col', axis=0) for x in (chunk, *chunks)]  26 us
    pallas_call x3, Pallas kernels, split_blocks(): pl.pallas_call(functools.partial(split_kernel, parts, count), grid_spec=p...  23.2 us
    ppermute x4, waiting for transfers between devices, passed(): lax.ppermute(b_pass, 'row', ALONG_Y)  21.6 us
    ppermute x2, waiting for transfers between devices, arrivals(): b_last = lax.ppermute(b_on + first[1], 'row', ALONG_X)  20.3 us
    pallas_call x2, Pallas kernels, update_blocks(): pl.pallas_call(lambda info, *refs: partial_updates(steps, [info[count + n...  19.2 us
    all_to_all x4, starting transfers between devices, to_chips(): return lax.all_to_all(blocks, 'row', 0, 0, axis_index_groups=SAME_CORE)  16.6 us
  transfers between devices with their start and end apart: 31, of which 19 were waited for; matrix products, arithmetic and copies ran while one was open for 6% of the time, Pallas kernels for 32%

profile of v2, /device:TPU:0, one launch (start us, length us, event | category | flops | bytes accessed | tf_op | source)
XLA Modules:
  0.0 343.8 jit_solution(10848571309122040951)
XLA Ops:
  6.5 1.0 copy.26
  7.5 1.7 pad_maximum_fusion
  9.3 3.3 constant_dynamic-slice_fusion
  13.1 1.2 copy.27
  14.3 1.0 dynamic-slice_bitcast_fusion
  15.4 0.9 copy-done.7
  16.5 0.8 stack.87.info
  17.3 1.4 collective-permute-done.2.refs_5_
  18.7 1.3 collective-permute-done.refs_1_
  20.0 1.3 copy-done.3
  21.3 7.9 %shard_map.57 = (f32[1024,128]{1,0:T(8,128)}, f32[1024,128]{1,0:T(8,128)}, f32[1024,128]{1,0:T(8,128)}, f32[1024,128]{1,0:T(8,128)}, f32[1024,128]{1,0:T(8,128)}, /*index=5*/f32[1024,128]{1,0:T(8,128)}) custom-call(s32[6]{0:T(128)} %stack.87.info, f32[1024,256]{1,0:T(8,128)} %bitcast.37, f32[1024,256]{1,0:T(8,128)} %collective-permute-done.refs_1_, ...), custom_call_target="tpu_custom_call" | custom-call | flops 75497472 | bytes 163840 | tf_op jit(solution)/shard_map/pallas_call | solution.py:94
  29.2 2.9 collective-permute-start.13
  32.1 1.5 collective-permute-start.11
  34.8 11.3 %shard_map.56 = (f32[1024,128]{1,0:T(8,128)}, f32[1024,128]{1,0:T(8,128)}, f32[1024,128]{1,0:T(8,128)}, f32[1024,128]{1,0:T(8,128)}, f32[1024,128]{1,0:T(8,128)}...) custom-call(s32[8]{0:T(128)} %stack.83.info, f32[1024,256]{1,0:T(8,128)} %bitcast.38, ...), custom_call_target="tpu_custom_call" | custom-call | flops 125829120 | bytes 229376 | tf_op jit(solution)/shard_map/pallas_call | solution.py:94
  46.1 7.4 %collective-permute-done.13 = f32[1024,128]{1,0:T(8,128)S(1)} collective-permute-done((f32[1024,128]{1,0:T(8,128)}, f32[1024,128]{1,0:T(8,128)S(1)}, u32[]{:S(2)}, u32[]{:S(2)}) %collective-permute-start.13) | collective-permute-done | bytes 524320 | tf_op jit(solution)/shard_map/ppermute | solution.py:298
  53.5 2.0 collective-permute-start.14
  55.5 4.9 %shard_map.55 = (bf16[512,512]{1,0:T(8,128)(2,1)}, bf16[512,512]{1,0:T(8,128)(2,1)}, bf16[512,512]{1,0:T(8,128)(2,1)}, bf16[512,512]{1,0:T(8,128)(2,1)}, bf16[51...) custom-call(f32[8,3,64,512]{3,2,1,0:T(8,128)} %bitcast.40), custom_call_target="tpu_custom_call" | custom-call | flops 50331648 | bytes 196608 | tf_op jit(solution)/shard_map/pallas_call | solution.py:52
  60.5 0.8 collective-permute-start.12
  61.4 3.3 collective-permute-done.10.refs_8_
  64.7 0.9 collective-permute-done.5.refs_7_
  65.6 10.9 %collective-permute-done.14.refs_10_ = f32[1024,128]{1,0:T(8,128)S(1)} collective-permute-done((f32[1024,128]{1,0:T(8,128)S(1)}, f32[1024,128]{1,0:T(8,128)S(1)}, u32[]{:S(2)}, u32[]{:S(2)}) %collective-permute-start.14) | collective-permute-done | bytes 524320 | tf_op jit(solution)/shard_map/ppermute | solution.py:303
  76.5 0.8 copy-done.16
  77.5 5.6 %shard_map.58 = (f32[1024,512]{1,0:T(8,128)}, f32[1024,256]{1,0:T(8,128)}) custom-call(bf16[512,512]{1,0:T(8,128)(2,1)} %get-tuple-element.45.refs_0_, bf16[512,512]{1,0:T(8,128)(2,1)} %get-tuple-element.46.refs_1_, bf16[512,512]{1,0:T(8,128)(2,1)} %get-tuple-element.47.refs_2_, bf16[512,512]{1,0:T(8,128)(2,1)} %get-tuple-element.48.refs_3_, ...), custom_call_target="tpu_custom_call" | custom-call | flops 37748736 | bytes 294912 | tf_op jit(solution)/shard_map/pallas_call | solution.py:151
  83.2 0.9 collective-permute-start.8
  84.0 1.2 collective-permute-start.6
  85.3 0.8 collective-permute-start.3
  86.0 1.2 collective-permute-start.4
  87.3 11.0 %collective-permute-done.8 = f32[1024,128]{1,0:T(8,128)S(1)} collective-permute-done((f32[1024,128]{1,0:T(8,128)}, f32[1024,128]{1,0:T(8,128)S(1)}, u32[]{:S(2)}, u32[]{:S(2)}) %collective-permute-start.8) | collective-permute-done | bytes 524320 | tf_op jit(solution)/shard_map/ppermute | solution.py:298
  99.1 1.4 collective-permute-start.7
  100.5 9.8 %collective-permute-done.3.refs_7_ = f32[1024,128]{1,0:T(8,128)S(1)} collective-permute-done((f32[1024,128]{1,0:T(8,128)}, f32[1024,128]{1,0:T(8,128)S(1)}, u32[]{:S(2)}, u32[]{:S(2)}) %collective-permute-start.3) | collective-permute-done | bytes 524320 | tf_op jit(solution)/shard_map/ppermute | solution.py:298
  110.3 9.4 %collective-permute-done.9.refs_10_ = f32[1024,128]{1,0:T(8,128)S(1)} collective-permute-done((f32[1024,128]{1,0:T(8,128)S(1)}, f32[1024,128]{1,0:T(8,128)S(1)}, u32[]{:S(2)}, u32[]{:S(2)}) %collective-permute-start.9) | collective-permute-done | bytes 524320 | tf_op jit(solution)/shard_map/ppermute | solution.py:303
  119.7 0.8 copy-done.17
  120.7 5.6 %shard_map.59 = (f32[1024,512]{1,0:T(8,128)}, f32[1024,128]{1,0:T(8,128)}, f32[1024,128]{1,0:T(8,128)}) custom-call(bf16[512,512]{1,0:T(8,128)(2,1)} %get-tuple-element.45.refs_0_, bf16[512,512]{1,0:T(8,128)(2,1)} %get-tuple-element.46.refs_1_, bf16[512,512]{1,0:T(8,128)(2,1)} %get-tuple-element.47.refs_2_, ...), custom_call_target="tpu_custom_call", output_to_operand_aliasing={{0}: (11, {})} | custom-call | flops 37748736 | bytes 294912 | tf_op jit(solution)/shard_map/pallas_call | solution.py:151
  126.3 1.5 collective-permute-start.18
  128.8 1.8 collective-permute-done.16.refs_1_
  130.6 1.4 copy-done.6
  132.0 6.0 %shard_map.60 = (bf16[8,1024,512]{2,1,0:T(8,128)(2,1)}, bf16[8,1024,512]{2,1,0:T(8,128)(2,1)}) custom-call(s32[2]{0:T(128)} %pad_add_fusion.1.place, f32[1024,512]{1,0:T(8,128)} %get-tuple-element.71.refs_0_, f32[1024,512]{1,0:T(8,128)} %copy-done.6), custom_call_target="tpu_custom_call" | custom-call | bytes 262144 | tf_op jit(solution)/shard_map/pallas_call | solution.py:187
  138.1 26.0 %all-gather.13.cloned.1.call-done = f32[4096,256]{1,0:T(8,128)} async-done(((f32[1024,256]{1,0:T(8,128)}), f32[4096,256]{1,0:T(8,128)}) %all-gather.13.cloned.1.call-update) | async-done | bytes 4194320 | tf_op jit(solution)/shard_map/all_gather | solution.py:313
  164.0 4.6 %fusion = (f32[4,1024,128]{2,1,0:T(8,128)}, f32[4,1024,128]{2,1,0:T(8,128)}) fusion(f32[4,1024,256]{2,1,0:T(8,128)} %bitcast.39), kind=kLoop, calls=%fused_computation.10 | loop fusion | bytes 8388608 | tf_op jit(solution)/shard_map/slice | solution.py:327
  168.6 6.0 %collective-permute-done.18.refs_1_ = f32[1024,512]{1,0:T(8,128)} collective-permute-done((f32[1024,512]{1,0:T(8,128)}, f32[1024,512]{1,0:T(8,128)}, u32[]{:S(2)}, u32[]{:S(2)}) %collective-permute-start.18) | collective-permute-done | bytes 2097184 | tf_op jit(solution)/shard_map/ppermute | solution.py:316
  174.6 1.2 collective-permute-done.15.refs_0_
  175.9 2.3 slice.14
  178.1 0.8 collective-permute-start.17
  178.9 2.3 slice.15
  181.2 1.3 collective-permute-start.21
  182.5 3.6 %all-to-all-start.1 = ((f32[4,1024,128]{2,1,0:T(8,128)}), f32[4,1024,128]{2,1,0:T(8,128)S(1)}, u32[]{:S(2)}, u32[]{:S(2)}) async-start(f32[4,1024,128]{2,1,0:T(8,128)} %get-tuple-element.85), calls=%async_computation.1 | async-start | bytes 4194304 | tf_op jit(solution)/shard_map/all_to_all | solution.py:254
  187.0 11.1 %shard_map.61 = (bf16[8,1024,512]{2,1,0:T(8,128)(2,1)}, bf16[8,1024,512]{2,1,0:T(8,128)(2,1)}) custom-call(s32[4]{0:T(128)} %pad_add_fusion.2.place, f32[1024,512]{1,0:T(8,128)} %collective-permute-done.15.refs_0_, f32[1024,512]{1,0:T(8,128)} %collective-permute-done.18.refs_1_, ...), custom_call_target="tpu_custom_call", output_to_operand_aliasing={{0}: (5, {}), {1}: (6, {})} | custom-call | bytes 524288 | tf_op jit(solution)/shard_map/pallas_call | solution.py:187
  198.0 6.3 %collective-permute-done.17 = f32[1024,256]{1,0:T(8,128)} collective-permute-done((f32[1024,256]{1,0:T(8,128)}, f32[1024,256]{1,0:T(8,128)}, u32[]{:S(2)}, u32[]{:S(2)}) %collective-permute-start.17) | collective-permute-done | bytes 1048608 | tf_op jit(solution)/shard_map/ppermute | solution.py:329
  204.4 2.3 constant_dynamic-update-slice_fusion.1
  206.7 0.8 collective-permute-done.21
  207.4 1.0 constant_dynamic-update-slice_fusion.refs_0_
  208.5 20.4 %all-to-all-done.1.pieces = f32[4,1024,128]{2,1,0:T(8,128)S(1)} async-done(((f32[4,1024,128]{2,1,0:T(8,128)}), f32[4,1024,128]{2,1,0:T(8,128)S(1)}, u32[]{:S(2)}, u32[]{:S(2)}) %all-to-all-start.1) | async-done | bytes 2097184 | tf_op jit(solution)/shard_map/all_to_all | solution.py:254
  229.0 1.4 copy-done.2
  230.4 4.5 %all-to-all-start = ((f32[4,1024,128]{2,1,0:T(8,128)}), f32[4,1024,128]{2,1,0:T(8,128)}, u32[]{:S(2)}, u32[]{:S(2)}) async-start(f32[4,1024,128]{2,1,0:T(8,128)} %get-tuple-element.86), calls=%async_computation | async-start | bytes 4194304 | tf_op jit(solution)/shard_map/all_to_all | solution.py:254
  235.5 6.1 %shard_map.62 = (bf16[8,1024,512]{2,1,0:T(8,128)(2,1)}, bf16[8,1024,512]{2,1,0:T(8,128)(2,1)}) custom-call(s32[2]{0:T(128)} %pad_add_fusion.place, f32[1024,512]{1,0:T(8,128)} %constant_dynamic-update-slice_fusion.refs_0_, f32[1024,512]{1,0:T(8,128)} %collective-permute-done.22.refs_1_, ...), custom_call_target="tpu_custom_call", output_to_operand_aliasing={{0}: (3, {}), {1}: (4, {})} | custom-call | bytes 262144 | tf_op jit(solution)/shard_map/pallas_call | solution.py:187
  241.5 18.6 %shard_map.63.refs_0_ = f32[4,512,4096]{2,1,0:T(8,128)} custom-call(f32[4,1024,128]{2,1,0:T(8,128)} %copy-done.2, bf16[8,1024,512]{2,1,0:T(8,128)(2,1)} %get-tuple-element.81.high, bf16[8,1024,512]{2,1,0:T(8,128)(2,1)} %get-tuple-element.82.low), custom_call_target="tpu_custom_call" | custom-call | flops 402653184 | bytes 851968 | tf_op jit(solution)/shard_map/pallas_call | solution.py:230
  260.1 4.1 %all-to-all-start.3 = ((f32[4,1024,128]{2,1,0:T(8,128)}), f32[4,1024,128]{2,1,0:T(8,128)S(1)}, u32[]{:S(2)}, u32[]{:S(2)}) async-start(f32[4,1024,128]{2,1,0:T(8,128)} %bitcast.41), calls=%async_computation.3 | async-start | bytes 4194304 | tf_op jit(solution)/shard_map/all_to_all | solution.py:254
  264.3 18.6 %shard_map.64.refs_0_ = f32[4,512,4096]{2,1,0:T(8,128)} custom-call(f32[4,1024,128]{2,1,0:T(8,128)} %all-to-all-done.pieces, bf16[8,1024,512]{2,1,0:T(8,128)(2,1)} %get-tuple-element.81.high, bf16[8,1024,512]{2,1,0:T(8,128)(2,1)} %get-tuple-element.82.low, f32[4,512,4096]{2,1,0:T(8,128)} %shard_map.63.refs_0_), custom_call_target="tpu_custom_call", output_to_operand_aliasing={{}: (3, {})} | custom-call | flops 402653184 | bytes 851968 | tf_op jit(solution)/shard_map/pallas_call | solution.py:230
  282.8 5.5 %all-to-all-done.3.pieces = f32[4,1024,128]{2,1,0:T(8,128)S(1)} async-done(((f32[4,1024,128]{2,1,0:T(8,128)}), f32[4,1024,128]{2,1,0:T(8,128)S(1)}, u32[]{:S(2)}, u32[]{:S(2)}) %all-to-all-start.3) | async-done | bytes 2097184 | tf_op jit(solution)/shard_map/all_to_all | solution.py:254
  288.4 1.3 copy-done.4
  289.7 4.5 %all-to-all-start.2 = ((f32[4,1024,128]{2,1,0:T(8,128)}), f32[4,1024,128]{2,1,0:T(8,128)}, u32[]{:S(2)}, u32[]{:S(2)}) async-start(f32[4,1024,128]{2,1,0:T(8,128)} %bitcast.42), calls=%async_computation.2 | async-start | bytes 4194304 | tf_op jit(solution)/shard_map/all_to_all | solution.py:254
  294.2 18.6 %shard_map.65.refs_0_ = f32[4,512,4096]{2,1,0:T(8,128)} custom-call(f32[4,1024,128]{2,1,0:T(8,128)} %copy-done.4, bf16[8,1024,512]{2,1,0:T(8,128)(2,1)} %get-tuple-element.81.high, bf16[8,1024,512]{2,1,0:T(8,128)(2,1)} %get-tuple-element.82.low, f32[4,512,4096]{2,1,0:T(8,128)} %shard_map.64.refs_0_), custom_call_target="tpu_custom_call", output_to_operand_aliasing={{}: (3, {})} | custom-call | flops 402653184 | bytes 851968 | tf_op jit(solution)/shard_map/pallas_call | solution.py:230
  312.8 5.9 %all-to-all-done.2.pieces = f32[4,1024,128]{2,1,0:T(8,128)} async-done(((f32[4,1024,128]{2,1,0:T(8,128)}), f32[4,1024,128]{2,1,0:T(8,128)}, u32[]{:S(2)}, u32[]{:S(2)}) %all-to-all-start.2) | async-done | bytes 2097184 | tf_op jit(solution)/shard_map/all_to_all | solution.py:254
  318.7 18.6 %shard_map.66 = f32[4,512,4096]{2,1,0:T(8,128)} custom-call(f32[4,1024,128]{2,1,0:T(8,128)} %all-to-all-done.2.pieces, bf16[8,1024,512]{2,1,0:T(8,128)(2,1)} %get-tuple-element.81.high, bf16[8,1024,512]{2,1,0:T(8,128)(2,1)} %get-tuple-element.82.low, f32[4,512,4096]{2,1,0:T(8,128)} %shard_map.65.refs_0_), custom_call_target="tpu_custom_call", output_to_operand_aliasing={{}: (3, {})} | custom-call | flops 402653184 | bytes 851968 | tf_op jit(solution)/shard_map/pallas_call | solution.py:230
  (76 shorter events, 6.0 us)
Async XLA Ops:
  6.5 49.0 %all-gather.9.cloned.1.call-start = ((), (), s32[]{:S(2)}) async-start(), calls=%async_computation.4 | async-start | bytes 3538944 | tf_op jit(solution)/shard_map/all_gather | solution.py:50
  9.2 154.8 %all-gather.13.cloned.1.call-start = ((), (), s32[]{:S(2)}) async-start(), calls=%async_computation.6 | async-start | bytes 5242880 | tf_op jit(solution)/shard_map/all_gather | solution.py:313
  9.3 3.8 %copy-start.5 = (f32[64,2,4096]{2,1,0:T(2,128)S(1)}, f32[64,2,4096]{2,1,0:T(2,128)}, u32[]{:S(2)}) copy-start(f32[64,2,4096]{2,1,0:T(2,128)} %param.7) | copy-start | bytes 6291460
  12.6 7.4 %collective-permute-start.1 = (f32[256,2048]{1,0:T(8,128)}, f32[256,2048]{1,0:T(8,128)S(1)}, u32[]{:S(2)}, u32[]{:S(2)}) collective-permute-start(f32[256,2048]{1,0:T(8,128)} %constant_dynamic-slice_fusion), channel_id=1, source_target_pairs={{0,4},{4,0},{8,12},{12,8},{16,20},{20,16},{24,28},{28,24},{1,5},{5... | collective-permute-start | bytes 6291464 | tf_op jit(solution)/shard_map/ppermute | solution.py:273
  14.3 2.1 copy-start
  14.3 2.0 copy-start.7
  15.3 3.3 collective-permute-start.2
  16.4 3.6 %copy-start.1 = (f32[2,512,256]{2,1,0:T(8,128)}, f32[2,512,256]{2,1,0:T(8,128)S(1)}, u32[]{:S(2)}) copy-start(f32[2,512,256]{2,1,0:T(8,128)S(1)} %copy.20) | copy-start | bytes 3145732
  16.4 3.6 %collective-permute-start = (f32[1024,256]{1,0:T(8,128)S(1)}, f32[1024,256]{1,0:T(8,128)}, u32[]{:S(2)}, u32[]{:S(2)}) collective-permute-start(f32[1024,256]{1,0:T(8,128)S(1)} %bitcast.36), channel_id=1, source_target_pairs={{0,4},{4,0},{8,12},{12,8},{16,20},{20,16},{24,28},{28,24},{1,5},{5... | collective-permute-start | bytes 3145736 | tf_op jit(solution)/shard_map/ppermute | solution.py:277
  20.0 1.3 copy-start.3
  29.2 24.2 %collective-permute-start.13 = (f32[1024,128]{1,0:T(8,128)}, f32[1024,128]{1,0:T(8,128)S(1)}, u32[]{:S(2)}, u32[]{:S(2)}) collective-permute-start(f32[1024,128]{1,0:T(8,128)} %get-tuple-element.67), channel_id=1, source_target_pairs={{0,16},{4,20},{8,24},{12,28},{16,0},{20,4},{24,8},{28,12},{1,17},{... | collective-permute-start | bytes 1572872 | tf_op jit(solution)/shard_map/ppermute | solution.py:298
  32.1 28.4 %collective-permute-start.11 = (f32[1024,128]{1,0:T(8,128)}, f32[1024,128]{1,0:T(8,128)S(1)}, u32[]{:S(2)}, u32[]{:S(2)}) collective-permute-start(f32[1024,128]{1,0:T(8,128)} %get-tuple-element.64), channel_id=1, source_target_pairs={{0,8},{4,12},{8,0},{12,4},{16,24},{20,28},{24,16},{28,20},{1,9},{5... | collective-permute-start | bytes 1572872 | tf_op jit(solution)/shard_map/ppermute | solution.py:298
  34.2 30.5 %collective-permute-start.10 = (f32[1024,128]{1,0:T(8,128)}, f32[1024,128]{1,0:T(8,128)S(1)}, u32[]{:S(2)}, u32[]{:S(2)}) collective-permute-start(f32[1024,128]{1,0:T(8,128)} %get-tuple-element.62), channel_id=1, source_target_pairs={{0,16},{4,20},{8,24},{12,28},{16,0},{20,4},{24,8},{28,12},{1,17},{... | collective-permute-start | bytes 1572872 | tf_op jit(solution)/shard_map/ppermute | solution.py:298
  34.7 18.8 %copy-start.13 = (f32[1024,128]{1,0:T(8,128)S(1)}, f32[1024,128]{1,0:T(8,128)}, u32[]{:S(2)}) copy-start(f32[1024,128]{1,0:T(8,128)} %get-tuple-element.66) | copy-start | bytes 1572868
  34.7 30.9 %collective-permute-start.5 = (f32[1024,128]{1,0:T(8,128)}, f32[1024,128]{1,0:T(8,128)S(1)}, u32[]{:S(2)}, u32[]{:S(2)}) collective-permute-start(f32[1024,128]{1,0:T(8,128)} %get-tuple-element.56), channel_id=1, source_target_pairs={{0,8},{4,12},{8,0},{12,4},{16,24},{20,28},{24,16},{28,20},{1,9},{5... | collective-permute-start | bytes 1572872 | tf_op jit(solution)/shard_map/ppermute | solution.py:298
  53.5 7.0 %copy-start.10 = (f32[1024,128]{1,0:T(8,128)S(1)}, f32[1024,128]{1,0:T(8,128)}, u32[]{:S(2)}) copy-start(f32[1024,128]{1,0:T(8,128)} %get-tuple-element.63) | copy-start | bytes 1572868
  53.5 22.9 %collective-permute-start.14 = (f32[1024,128]{1,0:T(8,128)S(1)}, f32[1024,128]{1,0:T(8,128)S(1)}, u32[]{:S(2)}, u32[]{:S(2)}) collective-permute-start(f32[1024,128]{1,0:T(8,128)S(1)} %add.66), channel_id=1, source_target_pairs={{0,8},{4,12},{8,0},{12,4},{16,24},{20,28},{24,16},{28,20},{1,9},{5... | collective-permute-start | bytes 1572872 | tf_op jit(solution)/shard_map/ppermute | solution.py:303
  60.5 15.9 %collective-permute-start.12 = (f32[1024,128]{1,0:T(8,128)S(1)}, f32[1024,128]{1,0:T(8,128)S(1)}, u32[]{:S(2)}, u32[]{:S(2)}) collective-permute-start(f32[1024,128]{1,0:T(8,128)S(1)} %add.65), channel_id=1, source_target_pairs={{0,16},{4,20},{8,24},{12,28},{16,0},{20,4},{24,8},{28,12},{1,17},{... | collective-permute-start | bytes 1572872 | tf_op jit(solution)/shard_map/ppermute | solution.py:302
  64.7 11.8 %copy-start.11 = (f32[1024,128]{1,0:T(8,128)}, f32[1024,128]{1,0:T(8,128)S(1)}, u32[]{:S(2)}) copy-start(f32[1024,128]{1,0:T(8,128)S(1)} %collective-permute-done.10.refs_8_) | copy-start | bytes 1572868
  65.6 10.9 %copy-start.12 = (f32[1024,128]{1,0:T(8,128)}, f32[1024,128]{1,0:T(8,128)S(1)}, u32[]{:S(2)}) copy-start(f32[1024,128]{1,0:T(8,128)S(1)} %collective-permute-done.5.refs_7_) | copy-start | bytes 1572868
  76.5 0.8 copy-start.16
  76.5 1.0 copy-start.19
  77.4 8.6 %copy-start.20 = (f32[1024,128]{1,0:T(8,128)S(1)}, f32[1024,128]{1,0:T(8,128)}, u32[]{:S(2)}) copy-start(f32[1024,128]{1,0:T(8,128)} %get-tuple-element.53) | copy-start | bytes 1572868
  77.5 20.8 %copy-start.9 = (f32[1024,128]{1,0:T(8,128)S(1)}, f32[1024,128]{1,0:T(8,128)}, u32[]{:S(2)}) copy-start(f32[1024,128]{1,0:T(8,128)} %get-tuple-element.58) | copy-start | bytes 1572868
  83.1 16.0 %copy-start.8 = (f32[1024,128]{1,0:T(8,128)S(1)}, f32[1024,128]{1,0:T(8,128)}, u32[]{:S(2)}) copy-start(f32[1024,128]{1,0:T(8,128)} %get-tuple-element.54) | copy-start | bytes 1572868
  83.1 152.4 %all-gather.15.cloned.1.call-start = ((), (), s32[]{:S(2)}) async-start(), calls=%async_computation.7 | async-start | bytes 2621440 | tf_op jit(solution)/shard_map/all_gather | solution.py:313
  83.2 15.1 %collective-permute-start.8 = (f32[1024,128]{1,0:T(8,128)}, f32[1024,128]{1,0:T(8,128)S(1)}, u32[]{:S(2)}, u32[]{:S(2)}) collective-permute-start(f32[1024,128]{1,0:T(8,128)} %get-tuple-element.60), channel_id=1, source_target_pairs={{0,16},{4,20},{8,24},{12,28},{16,0},{20,4},{24,8},{28,12},{1,17},{... | collective-permute-start | bytes 1572872 | tf_op jit(solution)/shard_map/ppermute | solution.py:298
  84.0 15.1 %collective-permute-start.6 = (f32[1024,128]{1,0:T(8,128)}, f32[1024,128]{1,0:T(8,128)S(1)}, u32[]{:S(2)}, u32[]{:S(2)}) collective-permute-start(f32[1024,128]{1,0:T(8,128)} %get-tuple-element.57), channel_id=1, source_target_pairs={{0,8},{4,12},{8,0},{12,4},{16,24},{20,28},{24,16},{28,20},{1,9},{5... | collective-permute-start | bytes 1572872 | tf_op jit(solution)/shard_map/ppermute | solution.py:298
  85.3 25.1 %collective-permute-start.3 = (f32[1024,128]{1,0:T(8,128)}, f32[1024,128]{1,0:T(8,128)S(1)}, u32[]{:S(2)}, u32[]{:S(2)}) collective-permute-start(f32[1024,128]{1,0:T(8,128)} %get-tuple-element.52), channel_id=1, source_target_pairs={{0,8},{4,12},{8,0},{12,4},{16,24},{20,28},{24,16},{28,20},{1,9},{5... | collective-permute-start | bytes 1572872 | tf_op jit(solution)/shard_map/ppermute | solution.py:298
  86.0 24.3 %collective-permute-start.4 = (f32[1024,128]{1,0:T(8,128)S(1)}, f32[1024,128]{1,0:T(8,128)S(1)}, u32[]{:S(2)}, u32[]{:S(2)}) collective-permute-start(f32[1024,128]{1,0:T(8,128)S(1)} %copy-done.20), channel_id=1, source_target_pairs={{0,16},{4,20},{8,24},{12,28},{16,0},{20,4},{24,8},{28,12},{1,17},{... | collective-permute-start | bytes 1572872 | tf_op jit(solution)/shard_map/ppermute | solution.py:298
  98.3 21.4 %collective-permute-start.9 = (f32[1024,128]{1,0:T(8,128)S(1)}, f32[1024,128]{1,0:T(8,128)S(1)}, u32[]{:S(2)}, u32[]{:S(2)}) collective-permute-start(f32[1024,128]{1,0:T(8,128)S(1)} %add.64), channel_id=1, source_target_pairs={{0,8},{4,12},{8,0},{12,4},{16,24},{20,28},{24,16},{28,20},{1,9},{5... | collective-permute-start | bytes 1572872 | tf_op jit(solution)/shard_map/ppermute | solution.py:303
  99.1 20.6 %collective-permute-start.7 = (f32[1024,128]{1,0:T(8,128)S(1)}, f32[1024,128]{1,0:T(8,128)S(1)}, u32[]{:S(2)}, u32[]{:S(2)}) collective-permute-start(f32[1024,128]{1,0:T(8,128)S(1)} %add.63), channel_id=1, source_target_pairs={{0,16},{4,20},{8,24},{12,28},{16,0},{20,4},{24,8},{28,12},{1,17},{... | collective-permute-start | bytes 1572872 | tf_op jit(solution)/shard_map/ppermute | solution.py:302
  110.3 9.4 %copy-start.14 = (f32[1024,128]{1,0:T(8,128)}, f32[1024,128]{1,0:T(8,128)S(1)}, u32[]{:S(2)}) copy-start(f32[1024,128]{1,0:T(8,128)S(1)} %collective-permute-done.3.refs_7_) | copy-start | bytes 1572868
  110.3 9.4 %copy-start.15 = (f32[1024,128]{1,0:T(8,128)}, f32[1024,128]{1,0:T(8,128)S(1)}, u32[]{:S(2)}) copy-start(f32[1024,128]{1,0:T(8,128)S(1)} %collective-permute-done.4.refs_8_) | copy-start | bytes 1572868
  119.7 0.8 copy-start.17
  119.7 1.0 copy-start.18
  126.3 4.4 %collective-permute-start.16 = (f32[1024,512]{1,0:T(8,128)}, f32[1024,512]{1,0:T(8,128)S(1)}, u32[]{:S(2)}, u32[]{:S(2)}) collective-permute-start(f32[1024,512]{1,0:T(8,128)} %get-tuple-element.71.refs_0_), channel_id=1, source_target_pairs={{0,4},{4,0},{8,12},{12,8},{16,20},{20,16},{24,28},{28,24},{1,5},{5... | collective-permute-start | bytes 6291464 | tf_op jit(solution)/shard_map/ppermute | solution.py:317
  126.3 48.4 %collective-permute-start.18 = (f32[1024,512]{1,0:T(8,128)}, f32[1024,512]{1,0:T(8,128)}, u32[]{:S(2)}, u32[]{:S(2)}) collective-permute-start(f32[1024,512]{1,0:T(8,128)} %get-tuple-element.71.refs_0_), channel_id=1, source_target_pairs={{0,16},{4,20},{8,24},{12,28},{16,0},{20,4},{24,8},{28,12},{1,17},{... | collective-permute-start | bytes 6291464 | tf_op jit(solution)/shard_map/ppermute | solution.py:316
  127.8 48.1 %collective-permute-start.15 = (f32[1024,512]{1,0:T(8,128)}, f32[1024,512]{1,0:T(8,128)}, u32[]{:S(2)}, u32[]{:S(2)}) collective-permute-start(f32[1024,512]{1,0:T(8,128)} %get-tuple-element.71.refs_0_), channel_id=1, source_target_pairs={{0,8},{4,12},{8,0},{12,4},{16,24},{20,28},{24,16},{28,20},{1,9},{5... | collective-permute-start | bytes 6291464 | tf_op jit(solution)/shard_map/ppermute | solution.py:315
  130.6 1.4 copy-start.6
  174.6 12.3 %collective-permute-start.20 = (f32[1024,512]{1,0:T(8,128)}, f32[1024,512]{1,0:T(8,128)}, u32[]{:S(2)}, u32[]{:S(2)}) collective-permute-start(f32[1024,512]{1,0:T(8,128)} %collective-permute-done.18.refs_1_), channel_id=1, source_target_pairs={{0,4},{4,0},{8,12},{12,8},{16,20},{20,16},{24,28},{28,24},{1,5},{5... | collective-permute-start | bytes 6291464 | tf_op jit(solution)/shard_map/ppermute | solution.py:324
  175.9 11.1 %collective-permute-start.19 = (f32[1024,512]{1,0:T(8,128)}, f32[1024,512]{1,0:T(8,128)}, u32[]{:S(2)}, u32[]{:S(2)}) collective-permute-start(f32[1024,512]{1,0:T(8,128)} %collective-permute-done.15.refs_0_), channel_id=1, source_target_pairs={{0,4},{4,0},{8,12},{12,8},{16,20},{20,16},{24,28},{28,24},{1,5},{5... | collective-permute-start | bytes 6291464 | tf_op jit(solution)/shard_map/ppermute | solution.py:324
  178.1 26.3 %collective-permute-start.17 = (f32[1024,256]{1,0:T(8,128)}, f32[1024,256]{1,0:T(8,128)}, u32[]{:S(2)}, u32[]{:S(2)}) collective-permute-start(f32[1024,256]{1,0:T(8,128)} %slice.14), channel_id=1, source_target_pairs={{0,16},{4,20},{8,24},{12,28},{16,0},{20,4},{24,8},{28,12},{1,17},{... | collective-permute-start | bytes 3145736 | tf_op jit(solution)/shard_map/ppermute | solution.py:329
  181.2 26.2 %collective-permute-start.21 = (f32[1024,256]{1,0:T(8,128)}, f32[1024,256]{1,0:T(8,128)S(1)}, u32[]{:S(2)}, u32[]{:S(2)}) collective-permute-start(f32[1024,256]{1,0:T(8,128)} %slice.15), channel_id=1, source_target_pairs={{0,8},{4,12},{8,0},{12,4},{16,24},{20,28},{24,16},{28,20},{1,9},{5... | collective-permute-start | bytes 3145736 | tf_op jit(solution)/shard_map/ppermute | solution.py:330
  182.5 46.5 %all-to-all-start.1 = ((f32[4,1024,128]{2,1,0:T(8,128)}), f32[4,1024,128]{2,1,0:T(8,128)S(1)}, u32[]{:S(2)}, u32[]{:S(2)}) async-start(f32[4,1024,128]{2,1,0:T(8,128)} %get-tuple-element.85), calls=%async_computation.1 | async-start | bytes 4194304 | tf_op jit(solution)/shard_map/all_to_all | solution.py:254
  186.1 96.8 %all-gather.11.cloned.1.call-start = ((), (), s32[]{:S(2)}) async-start(), calls=%async_computation.5 | async-start | bytes 2621440 | tf_op jit(solution)/shard_map/all_gather | solution.py:313
  208.5 27.0 %collective-permute-start.22 = (f32[1024,512]{1,0:T(8,128)}, f32[1024,512]{1,0:T(8,128)}, u32[]{:S(2)}, u32[]{:S(2)}) collective-permute-start(f32[1024,512]{1,0:T(8,128)} %constant_dynamic-update-slice_fusion.refs_0_), channel_id=1, source_target_pairs={{0,4},{4,0},{8,12},{12,8},{16,20},{20,16},{24,28},{28,24},{1,5},{5... | collective-permute-start | bytes 6291464 | tf_op jit(solution)/shard_map/ppermute | solution.py:324
  229.0 1.4 copy-start.2
  230.4 29.8 %all-to-all-start = ((f32[4,1024,128]{2,1,0:T(8,128)}), f32[4,1024,128]{2,1,0:T(8,128)}, u32[]{:S(2)}, u32[]{:S(2)}) async-start(f32[4,1024,128]{2,1,0:T(8,128)} %get-tuple-element.86), calls=%async_computation | async-start | bytes 4194304 | tf_op jit(solution)/shard_map/all_to_all | solution.py:254
  260.1 28.2 %all-to-all-start.3 = ((f32[4,1024,128]{2,1,0:T(8,128)}), f32[4,1024,128]{2,1,0:T(8,128)S(1)}, u32[]{:S(2)}, u32[]{:S(2)}) async-start(f32[4,1024,128]{2,1,0:T(8,128)} %bitcast.41), calls=%async_computation.3 | async-start | bytes 4194304 | tf_op jit(solution)/shard_map/all_to_all | solution.py:254
  288.4 1.4 copy-start.4
  289.7 28.9 %all-to-all-start.2 = ((f32[4,1024,128]{2,1,0:T(8,128)}), f32[4,1024,128]{2,1,0:T(8,128)}, u32[]{:S(2)}, u32[]{:S(2)}) async-start(f32[4,1024,128]{2,1,0:T(8,128)} %bitcast.42), calls=%async_computation.2 | async-start | bytes 4194304 | tf_op jit(solution)/shard_map/all_to_all | solution.py:254
Sparse Core Ops, SparseCore 0:
  9.4 43.4 all-gather.8
  83.2 80.7 all-gather.12
  165.6 44.4 all-gather.14
  211.5 44.6 all-gather.10

commit v3 on v2

--- a/solution.py
+++ b/solution.py
@@ -32,7 +32,7 @@
     return pl.CostEstimate(flops=flops // 32, bytes_accessed=moved // 32, transcendentals=0)
 
 
-def roomy(limit=56):
+def roomy(limit=62):
     return pltpu.CompilerParams(vmem_limit_bytes=limit << 20)
 
 

time: 346 us -> 343 us (level)
  local copies, waits for them, and re-layouts: 28.8 us -> 21.9 us
  starting transfers between devices: 35.5 us -> 39.3 us
    unnamed x45 -> x33, local copies, waits for them, and re-layouts: 12.8 us -> 6.8 us
  transfers between devices with their start and end apart: 31 -> 31, of which waited for: 19 -> 18; matrix products, arithmetic and copies ran while one was open for 6% -> 6% of each run, Pallas kernels for 32% -> 32%
where the time goes in v3:
time: 343 us; the launch traced here: 341 us
  Pallas kernels  133 us (39%)
  waiting for transfers between devices  128 us (37%)
  starting transfers between devices  39.3 us (11%)
  local copies, waits for them, and re-layouts  21.9 us (6%)
  between operations  13.4 us (4%)
  other arithmetic  5.74 us (2%)
    pallas_call x4, Pallas kernels, downdate_part(): pl.pallas_call(downdate_kernel, grid=(8,), in_specs=specs, out_specs=pl.B...  74.4 us
    all_to_all x4, waiting for transfers between devices, to_chips(): return lax.all_to_all(blocks, 'row', 0, 0, axis_index_groups=SAME_CORE)  33.8 us
    all_gather x3, waiting for transfers between devices, local(): blocks = [lax.all_gather(x, 'col', axis=0) for x in (chunk, *chunks)]  28.2 us
    pallas_call x3, Pallas kernels, split_blocks(): pl.pallas_call(functools.partial(split_kernel, parts, count), grid_spec=p...  23.3 us
    ppermute x2, waiting for transfers between devices, arrivals(): b_last = lax.ppermute(b_on + first[1], 'row', ALONG_X)  19.7 us
    pallas_call x2, Pallas kernels, update_blocks(): pl.pallas_call(lambda info, *refs: partial_updates(steps, [info[count + n...  19 us
    ppermute x4, waiting for transfers between devices, passed(): lax.ppermute(b_pass, 'row', ALONG_Y)  18.6 us
    all_to_all x4, starting transfers between devices, to_chips(): return lax.all_to_all(blocks, 'row', 0, 0, axis_index_groups=SAME_CORE)  18 us
  transfers between devices with their start and end apart: 31, of which 18 were waited for; matrix products, arithmetic and copies ran while one was open for 6% of the time, Pallas kernels for 32%

profile of v3, /device:TPU:0, one launch (start us, length us, event | category | flops | bytes accessed | tf_op | source)
XLA Modules:
  0.0 340.9 jit_solution(4454229174523516205)
XLA Ops:
  6.5 1.0 copy.26
  7.5 1.7 pad_maximum_fusion
  9.3 3.3 constant_dynamic-slice_fusion
  13.1 1.2 copy.27
  14.3 1.1 dynamic-slice_bitcast_fusion
  15.5 0.8 copy-done.5
  16.5 0.8 stack.87.info
  17.3 1.3 collective-permute-done.2.refs_5_
  18.6 1.4 collective-permute-done.refs_1_
  20.0 7.9 %shard_map.57 = (f32[1024,128]{1,0:T(8,128)}, f32[1024,128]{1,0:T(8,128)}, f32[1024,128]{1,0:T(8,128)}, f32[1024,128]{1,0:T(8,128)}, f32[1024,128]{1,0:T(8,128)}, /*index=5*/f32[1024,128]{1,0:T(8,128)}) custom-call(s32[6]{0:T(128)} %stack.87.info, f32[1024,256]{1,0:T(8,128)} %bitcast.37, f32[1024,256]{1,0:T(8,128)} %collective-permute-done.refs_1_, ...), custom_call_target="tpu_custom_call" | custom-call | flops 75497472 | bytes 163840 | tf_op jit(solution)/shard_map/pallas_call | solution.py:94
  27.9 2.9 collective-permute-start.13
  30.8 1.5 collective-permute-start.11
  32.3 0.6 stack.83.info
  33.5 11.1 %shard_map.56 = (f32[1024,128]{1,0:T(8,128)}, f32[1024,128]{1,0:T(8,128)}, f32[1024,128]{1,0:T(8,128)}, f32[1024,128]{1,0:T(8,128)}, f32[1024,128]{1,0:T(8,128)}...) custom-call(s32[8]{0:T(128)} %stack.83.info, f32[1024,256]{1,0:T(8,128)} %bitcast.38, ...), custom_call_target="tpu_custom_call" | custom-call | flops 125829120 | bytes 229376 | tf_op jit(solution)/shard_map/pallas_call | solution.py:94
  44.6 7.6 %collective-permute-done.13 = f32[1024,128]{1,0:T(8,128)S(1)} collective-permute-done((f32[1024,128]{1,0:T(8,128)}, f32[1024,128]{1,0:T(8,128)S(1)}, u32[]{:S(2)}, u32[]{:S(2)}) %collective-permute-start.13) | collective-permute-done | bytes 524320 | tf_op jit(solution)/shard_map/ppermute | solution.py:298
  52.2 0.8 copy-done.12
  53.0 2.1 add.66
  55.1 2.0 collective-permute-start.14
  57.1 4.9 %shard_map.55 = (bf16[512,512]{1,0:T(8,128)(2,1)}, bf16[512,512]{1,0:T(8,128)(2,1)}, bf16[512,512]{1,0:T(8,128)(2,1)}, bf16[512,512]{1,0:T(8,128)(2,1)}, bf16[51...) custom-call(f32[8,3,64,512]{3,2,1,0:T(8,128)} %bitcast.40), custom_call_target="tpu_custom_call" | custom-call | flops 50331648 | bytes 196608 | tf_op jit(solution)/shard_map/pallas_call | solution.py:52
  62.2 1.6 collective-permute-start.12
  63.8 1.5 collective-permute-done.5.refs_7_
  65.3 10.4 %collective-permute-done.14.refs_10_ = f32[1024,128]{1,0:T(8,128)} collective-permute-done((f32[1024,128]{1,0:T(8,128)}, f32[1024,128]{1,0:T(8,128)}, u32[]{:S(2)}, u32[]{:S(2)}) %collective-permute-start.14) | collective-permute-done | bytes 524320 | tf_op jit(solution)/shard_map/ppermute | solution.py:303
  75.7 0.8 copy-done.14
  76.5 5.6 %shard_map.58 = (f32[1024,512]{1,0:T(8,128)}, f32[1024,256]{1,0:T(8,128)}) custom-call(bf16[512,512]{1,0:T(8,128)(2,1)} %get-tuple-element.45.refs_0_, bf16[512,512]{1,0:T(8,128)(2,1)} %get-tuple-element.46.refs_1_, bf16[512,512]{1,0:T(8,128)(2,1)} %get-tuple-element.47.refs_2_, bf16[512,512]{1,0:T(8,128)(2,1)} %get-tuple-element.48.refs_3_, ...), custom_call_target="tpu_custom_call" | custom-call | flops 37748736 | bytes 294912 | tf_op jit(solution)/shard_map/pallas_call | solution.py:151
  82.6 1.6 collective-permute-start.6
  84.6 1.7 collective-permute-start.4
  86.3 11.0 %collective-permute-done.8 = f32[1024,128]{1,0:T(8,128)S(1)} collective-permute-done((f32[1024,128]{1,0:T(8,128)}, f32[1024,128]{1,0:T(8,128)S(1)}, u32[]{:S(2)}, u32[]{:S(2)}) %collective-permute-start.8) | collective-permute-done | bytes 524320 | tf_op jit(solution)/shard_map/ppermute | solution.py:298
  97.4 1.2 collective-permute-start.9
  98.6 0.9 collective-permute-start.7
  99.6 9.3 %collective-permute-done.3.refs_7_ = f32[1024,128]{1,0:T(8,128)S(1)} collective-permute-done((f32[1024,128]{1,0:T(8,128)}, f32[1024,128]{1,0:T(8,128)S(1)}, u32[]{:S(2)}, u32[]{:S(2)}) %collective-permute-start.3) | collective-permute-done | bytes 524320 | tf_op jit(solution)/shard_map/ppermute | solution.py:298
  108.9 9.2 %collective-permute-done.9.refs_10_ = f32[1024,128]{1,0:T(8,128)S(1)} collective-permute-done((f32[1024,128]{1,0:T(8,128)S(1)}, f32[1024,128]{1,0:T(8,128)S(1)}, u32[]{:S(2)}, u32[]{:S(2)}) %collective-permute-start.9) | collective-permute-done | bytes 524320 | tf_op jit(solution)/shard_map/ppermute | solution.py:303
  118.2 0.8 copy-done.13
  118.9 5.6 %shard_map.59 = (f32[1024,512]{1,0:T(8,128)}, f32[1024,128]{1,0:T(8,128)}, f32[1024,128]{1,0:T(8,128)}) custom-call(bf16[512,512]{1,0:T(8,128)(2,1)} %get-tuple-element.45.refs_0_, bf16[512,512]{1,0:T(8,128)(2,1)} %get-tuple-element.46.refs_1_, bf16[512,512]{1,0:T(8,128)(2,1)} %get-tuple-element.47.refs_2_, ...), custom_call_target="tpu_custom_call", output_to_operand_aliasing={{0}: (11, {})} | custom-call | flops 37748736 | bytes 294912 | tf_op jit(solution)/shard_map/pallas_call | solution.py:151
  124.5 1.7 collective-permute-start.18
  126.2 1.6 collective-permute-start.15
  127.7 0.6 pad_add_fusion.1.place
  128.4 0.6 collective-permute-done.16.refs_1_
  129.0 6.1 %shard_map.60 = (bf16[8,1024,512]{2,1,0:T(8,128)(2,1)}, bf16[8,1024,512]{2,1,0:T(8,128)(2,1)}) custom-call(s32[2]{0:T(128)} %pad_add_fusion.1.place, f32[1024,512]{1,0:T(8,128)} %get-tuple-element.71.refs_0_, f32[1024,512]{1,0:T(8,128)} %collective-permute-done.16.refs_1_), custom_call_target="tpu_custom_call" | custom-call | bytes 262144 | tf_op jit(solution)/shard_map/pallas_call | solution.py:187
  135.1 28.2 %all-gather.13.cloned.1.call-done = f32[4096,256]{1,0:T(8,128)} async-done(((f32[1024,256]{1,0:T(8,128)}), f32[4096,256]{1,0:T(8,128)}) %all-gather.13.cloned.1.call-update) | async-done | bytes 4194320 | tf_op jit(solution)/shard_map/all_gather | solution.py:313
  163.3 4.5 %fusion = (f32[4,1024,128]{2,1,0:T(8,128)}, f32[4,1024,128]{2,1,0:T(8,128)}) fusion(f32[4,1024,256]{2,1,0:T(8,128)} %bitcast.39), kind=kLoop, calls=%fused_computation.10 | loop fusion | bytes 8388608 | tf_op jit(solution)/shard_map/slice | solution.py:327
  167.8 5.0 %collective-permute-done.18.refs_1_ = f32[1024,512]{1,0:T(8,128)} collective-permute-done((f32[1024,512]{1,0:T(8,128)}, f32[1024,512]{1,0:T(8,128)}, u32[]{:S(2)}, u32[]{:S(2)}) %collective-permute-start.18) | collective-permute-done | bytes 2097184 | tf_op jit(solution)/shard_map/ppermute | solution.py:316
  172.9 1.4 collective-permute-done.15.refs_0_
  174.3 2.3 slice.14
  176.5 0.8 collective-permute-start.17
  177.3 2.3 slice.15
  179.6 1.6 collective-permute-start.21
  181.2 4.6 %all-to-all-start.1 = ((f32[4,1024,128]{2,1,0:T(8,128)}), f32[4,1024,128]{2,1,0:T(8,128)}, u32[]{:S(2)}, u32[]{:S(2)}) async-start(f32[4,1024,128]{2,1,0:T(8,128)} %get-tuple-element.85), calls=%async_computation.1 | async-start | bytes 4194304 | tf_op jit(solution)/shard_map/all_to_all | solution.py:254
  185.9 0.6 pad_add_fusion.2.place
  186.5 11.1 %shard_map.61 = (bf16[8,1024,512]{2,1,0:T(8,128)(2,1)}, bf16[8,1024,512]{2,1,0:T(8,128)(2,1)}) custom-call(s32[4]{0:T(128)} %pad_add_fusion.2.place, f32[1024,512]{1,0:T(8,128)} %collective-permute-done.15.refs_0_, f32[1024,512]{1,0:T(8,128)} %collective-permute-done.18.refs_1_, ...), custom_call_target="tpu_custom_call", output_to_operand_aliasing={{0}: (5, {}), {1}: (6, {})} | custom-call | bytes 524288 | tf_op jit(solution)/shard_map/pallas_call | solution.py:187
  197.6 5.2 %collective-permute-done.17 = f32[1024,256]{1,0:T(8,128)} collective-permute-done((f32[1024,256]{1,0:T(8,128)}, f32[1024,256]{1,0:T(8,128)}, u32[]{:S(2)}, u32[]{:S(2)}) %collective-permute-start.17) | collective-permute-done | bytes 1048608 | tf_op jit(solution)/shard_map/ppermute | solution.py:329
  202.8 1.4 constant_dynamic-update-slice_fusion.1
  204.2 1.7 collective-permute-done.21
  206.1 21.2 %all-to-all-done.1.pieces = f32[4,1024,128]{2,1,0:T(8,128)} async-done(((f32[4,1024,128]{2,1,0:T(8,128)}), f32[4,1024,128]{2,1,0:T(8,128)}, u32[]{:S(2)}, u32[]{:S(2)}) %all-to-all-start.1) | async-done | bytes 2097184 | tf_op jit(solution)/shard_map/all_to_all | solution.py:254
  227.3 4.4 %all-to-all-start = ((f32[4,1024,128]{2,1,0:T(8,128)}), f32[4,1024,128]{2,1,0:T(8,128)}, u32[]{:S(2)}, u32[]{:S(2)}) async-start(f32[4,1024,128]{2,1,0:T(8,128)} %get-tuple-element.86), calls=%async_computation | async-start | bytes 4194304 | tf_op jit(solution)/shard_map/all_to_all | solution.py:254
  231.7 0.6 pad_add_fusion.place
  232.3 6.1 %shard_map.62 = (bf16[8,1024,512]{2,1,0:T(8,128)(2,1)}, bf16[8,1024,512]{2,1,0:T(8,128)(2,1)}) custom-call(s32[2]{0:T(128)} %pad_add_fusion.place, f32[1024,512]{1,0:T(8,128)} %copy-done.2, f32[1024,512]{1,0:T(8,128)} %collective-permute-done.22.refs_1_, ...), custom_call_target="tpu_custom_call", output_to_operand_aliasing={{0}: (3, {}), {1}: (4, {})} | custom-call | bytes 262144 | tf_op jit(solution)/shard_map/pallas_call | solution.py:187
  238.4 18.6 %shard_map.63.refs_0_ = f32[4,512,4096]{2,1,0:T(8,128)} custom-call(f32[4,1024,128]{2,1,0:T(8,128)} %all-to-all-done.1.pieces, bf16[8,1024,512]{2,1,0:T(8,128)(2,1)} %get-tuple-element.81.high, bf16[8,1024,512]{2,1,0:T(8,128)(2,1)} %get-tuple-element.82.low), custom_call_target="tpu_custom_call" | custom-call | flops 402653184 | bytes 851968 | tf_op jit(solution)/shard_map/pallas_call | solution.py:230
  257.4 4.4 %all-to-all-start.3 = ((f32[4,1024,128]{2,1,0:T(8,128)}), f32[4,1024,128]{2,1,0:T(8,128)}, u32[]{:S(2)}, u32[]{:S(2)}) async-start(f32[4,1024,128]{2,1,0:T(8,128)} %bitcast.41), calls=%async_computation.3 | async-start | bytes 4194304 | tf_op jit(solution)/shard_map/all_to_all | solution.py:254
  261.8 18.6 %shard_map.64.refs_0_ = f32[4,512,4096]{2,1,0:T(8,128)} custom-call(f32[4,1024,128]{2,1,0:T(8,128)} %all-to-all-done.pieces, bf16[8,1024,512]{2,1,0:T(8,128)(2,1)} %get-tuple-element.81.high, bf16[8,1024,512]{2,1,0:T(8,128)(2,1)} %get-tuple-element.82.low, f32[4,512,4096]{2,1,0:T(8,128)} %shard_map.63.refs_0_), custom_call_target="tpu_custom_call", output_to_operand_aliasing={{}: (3, {})} | custom-call | flops 402653184 | bytes 851968 | tf_op jit(solution)/shard_map/pallas_call | solution.py:230
  280.4 6.7 %all-to-all-done.3.pieces = f32[4,1024,128]{2,1,0:T(8,128)} async-done(((f32[4,1024,128]{2,1,0:T(8,128)}), f32[4,1024,128]{2,1,0:T(8,128)}, u32[]{:S(2)}, u32[]{:S(2)}) %all-to-all-start.3) | async-done | bytes 2097184 | tf_op jit(solution)/shard_map/all_to_all | solution.py:254
  287.1 4.4 %all-to-all-start.2 = ((f32[4,1024,128]{2,1,0:T(8,128)}), f32[4,1024,128]{2,1,0:T(8,128)}, u32[]{:S(2)}, u32[]{:S(2)}) async-start(f32[4,1024,128]{2,1,0:T(8,128)} %bitcast.42), calls=%async_computation.2 | async-start | bytes 4194304 | tf_op jit(solution)/shard_map/all_to_all | solution.py:254
  291.6 18.6 %shard_map.65.refs_0_ = f32[4,512,4096]{2,1,0:T(8,128)} custom-call(f32[4,1024,128]{2,1,0:T(8,128)} %all-to-all-done.3.pieces, bf16[8,1024,512]{2,1,0:T(8,128)(2,1)} %get-tuple-element.81.high, bf16[8,1024,512]{2,1,0:T(8,128)(2,1)} %get-tuple-element.82.low, f32[4,512,4096]{2,1,0:T(8,128)} %shard_map.64.refs_0_), custom_call_target="tpu_custom_call", output_to_operand_aliasing={{}: (3, {})} | custom-call | flops 402653184 | bytes 851968 | tf_op jit(solution)/shard_map/pallas_call | solution.py:230
  310.2 5.6 %all-to-all-done.2.pieces = f32[4,1024,128]{2,1,0:T(8,128)} async-done(((f32[4,1024,128]{2,1,0:T(8,128)}), f32[4,1024,128]{2,1,0:T(8,128)}, u32[]{:S(2)}, u32[]{:S(2)}) %all-to-all-start.2) | async-done | bytes 2097184 | tf_op jit(solution)/shard_map/all_to_all | solution.py:254
  315.7 18.6 %shard_map.66 = f32[4,512,4096]{2,1,0:T(8,128)} custom-call(f32[4,1024,128]{2,1,0:T(8,128)} %all-to-all-done.2.pieces, bf16[8,1024,512]{2,1,0:T(8,128)(2,1)} %get-tuple-element.81.high, bf16[8,1024,512]{2,1,0:T(8,128)(2,1)} %get-tuple-element.82.low, f32[4,512,4096]{2,1,0:T(8,128)} %shard_map.65.refs_0_), custom_call_target="tpu_custom_call", output_to_operand_aliasing={{}: (3, {})} | custom-call | flops 402653184 | bytes 851968 | tf_op jit(solution)/shard_map/pallas_call | solution.py:230
  (64 shorter events, 3.2 us)
Async XLA Ops:
  6.5 50.6 %all-gather.9.cloned.1.call-start = ((), (), s32[]{:S(2)}) async-start(), calls=%async_computation.4 | async-start | bytes 3538944 | tf_op jit(solution)/shard_map/all_gather | solution.py:50
  9.2 154.0 %all-gather.13.cloned.1.call-start = ((), (), s32[]{:S(2)}) async-start(), calls=%async_computation.6 | async-start | bytes 5242880 | tf_op jit(solution)/shard_map/all_gather | solution.py:313
  9.3 3.8 %copy-start.4 = (f32[64,2,4096]{2,1,0:T(2,128)S(1)}, f32[64,2,4096]{2,1,0:T(2,128)}, u32[]{:S(2)}) copy-start(f32[64,2,4096]{2,1,0:T(2,128)} %param.7) | copy-start | bytes 6291460
  12.6 7.4 %collective-permute-start.1 = (f32[256,2048]{1,0:T(8,128)}, f32[256,2048]{1,0:T(8,128)}, u32[]{:S(2)}, u32[]{:S(2)}) collective-permute-start(f32[256,2048]{1,0:T(8,128)} %constant_dynamic-slice_fusion), channel_id=1, source_target_pairs={{0,4},{4,0},{8,12},{12,8},{16,20},{20,16},{24,28},{28,24},{1,5},{5... | collective-permute-start | bytes 6291464 | tf_op jit(solution)/shard_map/ppermute | solution.py:273
  14.3 2.1 copy-start
  14.3 2.0 copy-start.5
  15.4 3.1 collective-permute-start.2
  16.4 3.6 %copy-start.1 = (f32[2,512,256]{2,1,0:T(8,128)}, f32[2,512,256]{2,1,0:T(8,128)S(1)}, u32[]{:S(2)}) copy-start(f32[2,512,256]{2,1,0:T(8,128)S(1)} %copy.20) | copy-start | bytes 3145732
  16.4 3.6 %collective-permute-start = (f32[1024,256]{1,0:T(8,128)S(1)}, f32[1024,256]{1,0:T(8,128)}, u32[]{:S(2)}, u32[]{:S(2)}) collective-permute-start(f32[1024,256]{1,0:T(8,128)S(1)} %bitcast.36), channel_id=1, source_target_pairs={{0,4},{4,0},{8,12},{12,8},{16,20},{20,16},{24,28},{28,24},{1,5},{5... | collective-permute-start | bytes 3145736 | tf_op jit(solution)/shard_map/ppermute | solution.py:277
  18.6 1.4 copy-start.3
  27.9 24.2 %collective-permute-start.13 = (f32[1024,128]{1,0:T(8,128)}, f32[1024,128]{1,0:T(8,128)S(1)}, u32[]{:S(2)}, u32[]{:S(2)}) collective-permute-start(f32[1024,128]{1,0:T(8,128)} %get-tuple-element.67), channel_id=1, source_target_pairs={{0,16},{4,20},{8,24},{12,28},{16,0},{20,4},{24,8},{28,12},{1,17},{... | collective-permute-start | bytes 1572872 | tf_op jit(solution)/shard_map/ppermute | solution.py:298
  30.8 31.3 %collective-permute-start.11 = (f32[1024,128]{1,0:T(8,128)}, f32[1024,128]{1,0:T(8,128)S(1)}, u32[]{:S(2)}, u32[]{:S(2)}) collective-permute-start(f32[1024,128]{1,0:T(8,128)} %get-tuple-element.64), channel_id=1, source_target_pairs={{0,8},{4,12},{8,0},{12,4},{16,24},{20,28},{24,16},{28,20},{1,9},{5... | collective-permute-start | bytes 1572872 | tf_op jit(solution)/shard_map/ppermute | solution.py:298
  32.9 30.8 %collective-permute-start.10 = (f32[1024,128]{1,0:T(8,128)}, f32[1024,128]{1,0:T(8,128)S(1)}, u32[]{:S(2)}, u32[]{:S(2)}) collective-permute-start(f32[1024,128]{1,0:T(8,128)} %get-tuple-element.62), channel_id=1, source_target_pairs={{0,16},{4,20},{8,24},{12,28},{16,0},{20,4},{24,8},{28,12},{1,17},{... | collective-permute-start | bytes 1572872 | tf_op jit(solution)/shard_map/ppermute | solution.py:298
  33.4 31.9 %collective-permute-start.5 = (f32[1024,128]{1,0:T(8,128)}, f32[1024,128]{1,0:T(8,128)}, u32[]{:S(2)}, u32[]{:S(2)}) collective-permute-start(f32[1024,128]{1,0:T(8,128)} %get-tuple-element.56), channel_id=1, source_target_pairs={{0,8},{4,12},{8,0},{12,4},{16,24},{20,28},{24,16},{28,20},{1,9},{5... | collective-permute-start | bytes 1572872 | tf_op jit(solution)/shard_map/ppermute | solution.py:298
  52.2 0.8 copy-start.12
  53.0 9.1 %copy-start.8 = (f32[1024,128]{1,0:T(8,128)S(1)}, f32[1024,128]{1,0:T(8,128)}, u32[]{:S(2)}) copy-start(f32[1024,128]{1,0:T(8,128)} %get-tuple-element.63) | copy-start | bytes 1572868
  55.1 20.6 %collective-permute-start.14 = (f32[1024,128]{1,0:T(8,128)}, f32[1024,128]{1,0:T(8,128)}, u32[]{:S(2)}, u32[]{:S(2)}) collective-permute-start(f32[1024,128]{1,0:T(8,128)} %add.66), channel_id=1, source_target_pairs={{0,8},{4,12},{8,0},{12,4},{16,24},{20,28},{24,16},{28,20},{1,9},{5... | collective-permute-start | bytes 1572872 | tf_op jit(solution)/shard_map/ppermute | solution.py:303
  62.2 13.6 %collective-permute-start.12 = (f32[1024,128]{1,0:T(8,128)S(1)}, f32[1024,128]{1,0:T(8,128)S(1)}, u32[]{:S(2)}, u32[]{:S(2)}) collective-permute-start(f32[1024,128]{1,0:T(8,128)S(1)} %add.65), channel_id=1, source_target_pairs={{0,16},{4,20},{8,24},{12,28},{16,0},{20,4},{24,8},{28,12},{1,17},{... | collective-permute-start | bytes 1572872 | tf_op jit(solution)/shard_map/ppermute | solution.py:302
  63.8 12.0 %copy-start.9 = (f32[1024,128]{1,0:T(8,128)}, f32[1024,128]{1,0:T(8,128)S(1)}, u32[]{:S(2)}) copy-start(f32[1024,128]{1,0:T(8,128)S(1)} %collective-permute-done.10.refs_8_) | copy-start | bytes 1572868
  75.7 0.8 copy-start.14
  76.5 20.8 %copy-start.7 = (f32[1024,128]{1,0:T(8,128)S(1)}, f32[1024,128]{1,0:T(8,128)}, u32[]{:S(2)}) copy-start(f32[1024,128]{1,0:T(8,128)} %get-tuple-element.58) | copy-start | bytes 1572868
  82.1 16.5 %copy-start.6 = (f32[1024,128]{1,0:T(8,128)S(1)}, f32[1024,128]{1,0:T(8,128)}, u32[]{:S(2)}) copy-start(f32[1024,128]{1,0:T(8,128)} %get-tuple-element.54) | copy-start | bytes 1572868
  82.1 150.2 %all-gather.15.cloned.1.call-start = ((), (), s32[]{:S(2)}) async-start(), calls=%async_computation.7 | async-start | bytes 2621440 | tf_op jit(solution)/shard_map/all_gather | solution.py:313
  82.2 15.1 %collective-permute-start.8 = (f32[1024,128]{1,0:T(8,128)}, f32[1024,128]{1,0:T(8,128)S(1)}, u32[]{:S(2)}, u32[]{:S(2)}) collective-permute-start(f32[1024,128]{1,0:T(8,128)} %get-tuple-element.60), channel_id=1, source_target_pairs={{0,16},{4,20},{8,24},{12,28},{16,0},{20,4},{24,8},{28,12},{1,17},{... | collective-permute-start | bytes 1572872 | tf_op jit(solution)/shard_map/ppermute | solution.py:298
  82.6 16.0 %collective-permute-start.6 = (f32[1024,128]{1,0:T(8,128)}, f32[1024,128]{1,0:T(8,128)S(1)}, u32[]{:S(2)}, u32[]{:S(2)}) collective-permute-start(f32[1024,128]{1,0:T(8,128)} %get-tuple-element.57), channel_id=1, source_target_pairs={{0,8},{4,12},{8,0},{12,4},{16,24},{20,28},{24,16},{28,20},{1,9},{5... | collective-permute-start | bytes 1572872 | tf_op jit(solution)/shard_map/ppermute | solution.py:298
  84.2 24.7 %collective-permute-start.3 = (f32[1024,128]{1,0:T(8,128)}, f32[1024,128]{1,0:T(8,128)S(1)}, u32[]{:S(2)}, u32[]{:S(2)}) collective-permute-start(f32[1024,128]{1,0:T(8,128)} %get-tuple-element.52), channel_id=1, source_target_pairs={{0,8},{4,12},{8,0},{12,4},{16,24},{20,28},{24,16},{28,20},{1,9},{5... | collective-permute-start | bytes 1572872 | tf_op jit(solution)/shard_map/ppermute | solution.py:298
  84.6 24.3 %collective-permute-start.4 = (f32[1024,128]{1,0:T(8,128)}, f32[1024,128]{1,0:T(8,128)S(1)}, u32[]{:S(2)}, u32[]{:S(2)}) collective-permute-start(f32[1024,128]{1,0:T(8,128)} %get-tuple-element.53), channel_id=1, source_target_pairs={{0,16},{4,20},{8,24},{12,28},{16,0},{20,4},{24,8},{28,12},{1,17},{... | collective-permute-start | bytes 1572872 | tf_op jit(solution)/shard_map/ppermute | solution.py:298
  97.4 20.7 %collective-permute-start.9 = (f32[1024,128]{1,0:T(8,128)S(1)}, f32[1024,128]{1,0:T(8,128)S(1)}, u32[]{:S(2)}, u32[]{:S(2)}) collective-permute-start(f32[1024,128]{1,0:T(8,128)S(1)} %add.64), channel_id=1, source_target_pairs={{0,8},{4,12},{8,0},{12,4},{16,24},{20,28},{24,16},{28,20},{1,9},{5... | collective-permute-start | bytes 1572872 | tf_op jit(solution)/shard_map/ppermute | solution.py:303
  98.6 19.5 %collective-permute-start.7 = (f32[1024,128]{1,0:T(8,128)S(1)}, f32[1024,128]{1,0:T(8,128)}, u32[]{:S(2)}, u32[]{:S(2)}) collective-permute-start(f32[1024,128]{1,0:T(8,128)S(1)} %add.63), channel_id=1, source_target_pairs={{0,16},{4,20},{8,24},{12,28},{16,0},{20,4},{24,8},{28,12},{1,17},{... | collective-permute-start | bytes 1572872 | tf_op jit(solution)/shard_map/ppermute | solution.py:302
  108.9 9.3 %copy-start.10 = (f32[1024,128]{1,0:T(8,128)}, f32[1024,128]{1,0:T(8,128)S(1)}, u32[]{:S(2)}) copy-start(f32[1024,128]{1,0:T(8,128)S(1)} %collective-permute-done.3.refs_7_) | copy-start | bytes 1572868
  108.9 9.3 %copy-start.11 = (f32[1024,128]{1,0:T(8,128)}, f32[1024,128]{1,0:T(8,128)S(1)}, u32[]{:S(2)}) copy-start(f32[1024,128]{1,0:T(8,128)S(1)} %collective-permute-done.4.refs_8_) | copy-start | bytes 1572868
  118.1 0.8 copy-start.13
  124.5 4.5 %collective-permute-start.16 = (f32[1024,512]{1,0:T(8,128)}, f32[1024,512]{1,0:T(8,128)}, u32[]{:S(2)}, u32[]{:S(2)}) collective-permute-start(f32[1024,512]{1,0:T(8,128)} %get-tuple-element.71.refs_0_), channel_id=1, source_target_pairs={{0,4},{4,0},{8,12},{12,8},{16,20},{20,16},{24,28},{28,24},{1,5},{5... | collective-permute-start | bytes 6291464 | tf_op jit(solution)/shard_map/ppermute | solution.py:317
  124.5 48.4 %collective-permute-start.18 = (f32[1024,512]{1,0:T(8,128)}, f32[1024,512]{1,0:T(8,128)}, u32[]{:S(2)}, u32[]{:S(2)}) collective-permute-start(f32[1024,512]{1,0:T(8,128)} %get-tuple-element.71.refs_0_), channel_id=1, source_target_pairs={{0,16},{4,20},{8,24},{12,28},{16,0},{20,4},{24,8},{28,12},{1,17},{... | collective-permute-start | bytes 6291464 | tf_op jit(solution)/shard_map/ppermute | solution.py:316
  126.2 48.1 %collective-permute-start.15 = (f32[1024,512]{1,0:T(8,128)}, f32[1024,512]{1,0:T(8,128)}, u32[]{:S(2)}, u32[]{:S(2)}) collective-permute-start(f32[1024,512]{1,0:T(8,128)} %get-tuple-element.71.refs_0_), channel_id=1, source_target_pairs={{0,8},{4,12},{8,0},{12,4},{16,24},{20,28},{24,16},{28,20},{1,9},{5... | collective-permute-start | bytes 6291464 | tf_op jit(solution)/shard_map/ppermute | solution.py:315
  172.9 13.6 %collective-permute-start.20 = (f32[1024,512]{1,0:T(8,128)}, f32[1024,512]{1,0:T(8,128)}, u32[]{:S(2)}, u32[]{:S(2)}) collective-permute-start(f32[1024,512]{1,0:T(8,128)} %collective-permute-done.18.refs_1_), channel_id=1, source_target_pairs={{0,4},{4,0},{8,12},{12,8},{16,20},{20,16},{24,28},{28,24},{1,5},{5... | collective-permute-start | bytes 6291464 | tf_op jit(solution)/shard_map/ppermute | solution.py:324
  174.3 12.2 %collective-permute-start.19 = (f32[1024,512]{1,0:T(8,128)}, f32[1024,512]{1,0:T(8,128)}, u32[]{:S(2)}, u32[]{:S(2)}) collective-permute-start(f32[1024,512]{1,0:T(8,128)} %collective-permute-done.15.refs_0_), channel_id=1, source_target_pairs={{0,4},{4,0},{8,12},{12,8},{16,20},{20,16},{24,28},{28,24},{1,5},{5... | collective-permute-start | bytes 6291464 | tf_op jit(solution)/shard_map/ppermute | solution.py:324
  176.5 26.3 %collective-permute-start.17 = (f32[1024,256]{1,0:T(8,128)}, f32[1024,256]{1,0:T(8,128)}, u32[]{:S(2)}, u32[]{:S(2)}) collective-permute-start(f32[1024,256]{1,0:T(8,128)} %slice.14), channel_id=1, source_target_pairs={{0,16},{4,20},{8,24},{12,28},{16,0},{20,4},{24,8},{28,12},{1,17},{... | collective-permute-start | bytes 3145736 | tf_op jit(solution)/shard_map/ppermute | solution.py:329
  179.6 26.3 %collective-permute-start.21 = (f32[1024,256]{1,0:T(8,128)}, f32[1024,256]{1,0:T(8,128)S(1)}, u32[]{:S(2)}, u32[]{:S(2)}) collective-permute-start(f32[1024,256]{1,0:T(8,128)} %slice.15), channel_id=1, source_target_pairs={{0,8},{4,12},{8,0},{12,4},{16,24},{20,28},{24,16},{28,20},{1,9},{5... | collective-permute-start | bytes 3145736 | tf_op jit(solution)/shard_map/ppermute | solution.py:330
  181.2 46.1 %all-to-all-start.1 = ((f32[4,1024,128]{2,1,0:T(8,128)}), f32[4,1024,128]{2,1,0:T(8,128)}, u32[]{:S(2)}, u32[]{:S(2)}) async-start(f32[4,1024,128]{2,1,0:T(8,128)} %get-tuple-element.85), calls=%async_computation.1 | async-start | bytes 4194304 | tf_op jit(solution)/shard_map/all_to_all | solution.py:254
  185.8 94.6 %all-gather.11.cloned.1.call-start = ((), (), s32[]{:S(2)}) async-start(), calls=%async_computation.5 | async-start | bytes 2621440 | tf_op jit(solution)/shard_map/all_gather | solution.py:313
  206.0 21.3 %copy-start.2 = (f32[1024,512]{1,0:T(8,128)}, f32[1024,512]{1,0:T(8,128)S(1)}, u32[]{:S(2)}) copy-start(f32[1024,512]{1,0:T(8,128)S(1)} %constant_dynamic-update-slice_fusion.refs_0_) | copy-start | bytes 6291460
  206.0 26.3 %collective-permute-start.22 = (f32[1024,512]{1,0:T(8,128)S(1)}, f32[1024,512]{1,0:T(8,128)}, u32[]{:S(2)}, u32[]{:S(2)}) collective-permute-start(f32[1024,512]{1,0:T(8,128)S(1)} %constant_dynamic-update-slice_fusion.refs_0_), channel_id=1, source_target_pairs={{0,4},{4,0},{8,12},{12,8},{16,20},{20,16},{24,28},{28,24},{1,5},{5... | collective-permute-start | bytes 6291464 | tf_op jit(solution)/shard_map/ppermute | solution.py:324
  227.3 30.1 %all-to-all-start = ((f32[4,1024,128]{2,1,0:T(8,128)}), f32[4,1024,128]{2,1,0:T(8,128)}, u32[]{:S(2)}, u32[]{:S(2)}) async-start(f32[4,1024,128]{2,1,0:T(8,128)} %get-tuple-element.86), calls=%async_computation | async-start | bytes 4194304 | tf_op jit(solution)/shard_map/all_to_all | solution.py:254
  257.4 29.7 %all-to-all-start.3 = ((f32[4,1024,128]{2,1,0:T(8,128)}), f32[4,1024,128]{2,1,0:T(8,128)}, u32[]{:S(2)}, u32[]{:S(2)}) async-start(f32[4,1024,128]{2,1,0:T(8,128)} %bitcast.41), calls=%async_computation.3 | async-start | bytes 4194304 | tf_op jit(solution)/shard_map/all_to_all | solution.py:254
  287.1 28.6 %all-to-all-start.2 = ((f32[4,1024,128]{2,1,0:T(8,128)}), f32[4,1024,128]{2,1,0:T(8,128)}, u32[]{:S(2)}, u32[]{:S(2)}) async-start(f32[4,1024,128]{2,1,0:T(8,128)} %bitcast.42), calls=%async_computation.2 | async-start | bytes 4194304 | tf_op jit(solution)/shard_map/all_to_all | solution.py:254
Sparse Core Ops, SparseCore 0:
  9.4 43.5 all-gather.8
  82.2 80.9 all-gather.12
  164.9 44.4 all-gather.14
  210.8 44.6 all-gather.10

commit v4 on v3

--- a/solution.py
+++ b/solution.py
@@ -131,8 +131,10 @@
     low = three(corner, upper) + three(second, lower)
     solved[:panel, :] = top
     solved[panel:, :] = low
-    for n, chunk in enumerate(chunks):
-        cut = slice(n * chunk.shape[1], (n + 1) * chunk.shape[1])
+    start = 0
+    for chunk in chunks:
+        cut = slice(start % (2 * half), start % (2 * half) + chunk.shape[1])
+        start = cut.stop
         chunk[:panel, :] = top[:, cut]
         chunk[panel:, :] = low[:, cut]
 
@@ -171,19 +173,22 @@
             high[0], low[0] = halves(block[...])
 
 
-def split_blocks(place, blocks, held, weight=1):
+def split_blocks(place, blocks, held):
     depth, width = blocks[0].shape
     count, parts = len(blocks), 2
     rows = depth // parts
-    shape = jax.ShapeDtypeStruct((8, depth, width), jnp.bfloat16)
-    spec = pl.BlockSpec((1, rows, width), lambda i, place: (place[i // parts], i % parts, 0))
+    held = list(held)
+    wide = held[0].shape[2] if held else width
+    shape = jax.ShapeDtypeStruct((8, depth, wide), jnp.bfloat16)
+    spec = pl.BlockSpec(
+        (1, rows, width), lambda i, place: (place[0, i // parts], i % parts, place[1, i // parts])
+    )
 
     def taken(m):
         return pl.BlockSpec(
             (rows, width), lambda i, place: (jnp.clip(i - parts * m, 0, parts - 1), 0)
         )
 
-    held = list(held)
     return pl.pallas_call(
         functools.partial(split_kernel, parts, count),
         grid_spec=pltpu.PrefetchScalarGridSpec(
@@ -196,7 +201,7 @@
         out_shape=[shape, shape],
         input_output_aliases={count + 1: 0, count + 2: 1} if held else {},
         compiler_params=roomy(),
-        cost_estimate=cost(0, 8 * count * depth * width * weight),
+        cost_estimate=cost(0, 8 * count * depth * width),
     )(place, *blocks, *held)
 
 
@@ -287,7 +292,9 @@
         spots = [(chip ^ across) * 2 + side for across, side in places]
         return update_blocks(ints(*spots, core, rank, rank ^ 1), steps, widths, sources)
 
-    early = updates(((3, 0), (1, 0), (2, 0)), away, (quarter,) * 6)
+    shifted = tuple(tuple((out - 2, *rest) for out, *rest in step) for step in away[1:])
+    early = updates(((3, 0),), away[:1], (quarter,) * 2)
+    early += updates(((1, 0), (2, 0)), shifted, (quarter,) * 4)
     *late, keep, late_keep = updates(
         ((3, 1), (1, 1), (2, 1), (0, 0), (0, 1)),
         (*away, ((6, 0, 0, half),), ((7, 0, 0, half),)),
@@ -304,36 +311,41 @@
         return a_got, b_got, a_last, b_last
 
     first = passed(*early[:2])
-    first = after(first[0], late_keep, matrix[0]), first[1]
+    first = after(first[0], late_keep), first[1]
     terms = arrivals(first, *early[2:])
     first = passed(*[after(x, terms[0]) for x in late[:2]])
     solved, chunk = solve(matrix, (keep, *terms), (half,), None)
     late_terms = arrivals(first, *late[2:])
-    solved, *chunks = solve(matrix, (late_keep, *late_terms), (quarter, quarter), solved)
+    solved, late_half, *chunks = solve(
+        matrix, (late_keep, *late_terms), (half, quarter, quarter), solved
+    )
     blocks = [lax.all_gather(x, "col", axis=0) for x in (chunk, *chunks)]
 
-    from_x = lax.ppermute(solved, "row", ALONG_X)
-    from_y = lax.ppermute(solved, "row", ALONG_Y)
+    x_early = lax.ppermute(after(chunk, late_half), "row", ALONG_X)
+    y_late = lax.ppermute(late_half, "row", ALONG_Y)
+    x_late = lax.ppermute(late_half, "row", ALONG_X)
+    y_early = lax.ppermute(after(chunk, late_half), "row", ALONG_Y)
     twin = lax.ppermute(solved, "row", CORE)
 
-    def split(blocks, pair, group, held, weight=1):
-        places = [c * 4 + (chip ^ m) for c in (core, 1 - core) for m in group]
-        return split_blocks(ints(*places), [*blocks, *pair], held, weight)
+    def split(blocks, pair, spots, held):
+        places = [c * 4 + (chip ^ m) for c in (core, 1 - core) for m, _ in spots]
+        sides = [side for _, side in spots] * 2
+        return split_blocks(jnp.stack([ints(*places), ints(*sides)]), [*blocks, *pair], held)
 
     def given(*arrays):
         return [lax.ppermute(x, "row", CORE) for x in arrays]
 
-    held = split([solved], [twin], (0,), ())
+    held = split([solved], [twin], ((0, 0),), ())
     first_chunk = blocks[0][:, :, :quarter]
-    from_x, from_y = after(from_x, first_chunk, *held), after(from_y, first_chunk, *held)
-    far_a = lax.ppermute(from_x[:, :half], "row", ALONG_Y)
-    far_b = lax.ppermute(from_y[:, half:], "row", ALONG_X)
-
-    held = split([from_x, from_y], given(from_x, from_y), (1, 2), held)
+    x_early, y_late = after(x_early, first_chunk, *held), after(y_late, first_chunk, *held)
+    far_a = lax.ppermute(x_early, "row", ALONG_Y)
+    far_b = lax.ppermute(y_late, "row", ALONG_X)
+    sides = [x_early, x_late, y_early, y_late]
+    held = split(sides, given(*sides), ((1, 0), (1, 1), (2, 0), (2, 1)), held)
     far = jnp.concatenate([after(far_a, *held), far_b], axis=1)
     pieces = to_chips(first_chunk)
     twin = given(far)
-    held = split([after(far, pieces, blocks[1])], twin, (3,), held)
+    held = split([after(far, pieces, blocks[1])], twin, ((3, 0),), held)
     out = before = downdate_part(pieces, held, None, 0)
     pieces = to_chips(blocks[0][:, :, quarter:])
     out = downdate_part(pieces, held, out, 1)

time: 343 us -> 336 us (0.980)
  waiting for transfers between devices: 128 us -> 115 us
  Pallas kernels: 133 us -> 140 us
    all_gather x3, waiting for transfers between devices: 28.2 us -> 4.43 us  [local(): blocks = [lax.all_gather(x, 'col', axis=0) for x in (chunk, *chunks)]]
    ppermute x4 -> x6, waiting for transfers between devices: 13.3 us -> 34.1 us  [the longest x1 22 us: local(): y_early = lax.ppermute(after(chunk, late_half), 'row', ALONG_Y)]
    ppermute x4, waiting for transfers between devices: 18.6 us -> 11 us  [passed(): lax.ppermute(b_pass, 'row', ALONG_Y)]
    slice x2 -> x0, local copies, waits for them, and re-layouts: 4.53 us -> none  [the longest x1 2.27 us: local(): far_b = lax.ppermute(from_y[:, half:], 'row', ALONG_X)]
    pallas_call x2 -> x3, Pallas kernels: 19 us -> 22.3 us  [update_blocks(): pl.pallas_call(lambda info, *refs: partial_updates(steps, [info[count + n...]
    unnamed x33 -> x35, local copies, waits for them, and re-layouts: 6.8 us -> 7.14 us
  transfers between devices with their start and end apart: 31 -> 35, of which waited for: 18 -> 16; matrix products, arithmetic and copies ran while one was open for 6% -> 6% of each run, Pallas kernels for 32% -> 35%
where the time goes in v4:
time: 336 us; the launch traced here: 334 us
  Pallas kernels  140 us (42%)
  waiting for transfers between devices  115 us (34%)
  starting transfers between devices  39.9 us (12%)
  local copies, waits for them, and re-layouts  18.9 us (6%)
  between operations  13.4 us (4%)
  other arithmetic  7.18 us (2%)
    pallas_call x4, Pallas kernels, downdate_part(): pl.pallas_call(downdate_kernel, grid=(8,), in_specs=specs, out_specs=pl.B...  74.4 us
    all_to_all x4, waiting for transfers between devices, to_chips(): return lax.all_to_all(blocks, 'row', 0, 0, axis_index_groups=SAME_CORE)  33.1 us
    pallas_call x3, Pallas kernels, split_blocks(): pl.pallas_call(functools.partial(split_kernel, parts, count), grid_spec=p...  26.5 us
    pallas_call x3, Pallas kernels, update_blocks(): pl.pallas_call(lambda info, *refs: partial_updates(steps, [info[count + n...  22.3 us
    ppermute x1, waiting for transfers between devices, local(): y_early = lax.ppermute(after(chunk, late_half), 'row', ALONG_Y)  22 us
    ppermute x2, waiting for transfers between devices, arrivals(): b_last = lax.ppermute(b_on + first[1], 'row', ALONG_X)  19.5 us
    all_to_all x4, starting transfers between devices, to_chips(): return lax.all_to_all(blocks, 'row', 0, 0, axis_index_groups=SAME_CORE)  17.8 us
    pallas_call x2, Pallas kernels, solve(): pl.pallas_call(kernel, grid=(1,), in_specs=specs, out_specs=[pl.BlockSpec...  11.5 us
  transfers between devices with their start and end apart: 35, of which 16 were waited for; matrix products, arithmetic and copies ran while one was open for 6% of the time, Pallas kernels for 35%

profile of v4, /device:TPU:0, one launch (start us, length us, event | category | flops | bytes accessed | tf_op | source)
XLA Modules:
  0.0 334.0 jit_solution(12820220864364488687)
XLA Ops:
  6.5 1.0 copy.26
  7.5 1.7 pad_maximum_fusion
  9.3 3.3 constant_dynamic-slice_fusion
  13.1 1.2 copy.27
  14.3 1.1 dynamic-slice_bitcast_fusion
  15.4 0.9 copy-done.6
  16.6 0.7 pad_add_fusion.1.info
  17.2 1.5 collective-permute-done.2.refs_5_
  18.7 1.2 collective-permute-done.refs_1_
  19.9 1.0 copy-done.2
  20.9 4.4 %shard_map.58 = (f32[1024,128]{1,0:T(8,128)}, f32[1024,128]{1,0:T(8,128)}) custom-call(s32[4]{0:T(128)} %pad_add_fusion.1.info, f32[1024,256]{1,0:T(8,128)} %bitcast.43, f32[1024,256]{1,0:T(8,128)} %copy-done.2, f32[256,4096]{1,0:T(8,128)} %refs_2_.5, f32[256,2048]{1,0:T(8,128)} %collective-permute-done.1.refs_3_, f32[2,64,4096]{2,1,0:T(8,128)} %bitcast.39, ...), custom_call_target="tpu_custom_call" | custom-call | flops 25165824 | bytes 98304 | tf_op jit(solution)/shard_map/pallas_call | solution.py:94
  25.3 2.9 collective-permute-start.13
  28.2 1.5 collective-permute-start.11
  29.7 0.7 stack.114.info
  30.3 0.6 stack.111.info
  31.0 6.7 %shard_map.57 = (f32[1024,128]{1,0:T(8,128)}, f32[1024,128]{1,0:T(8,128)}, f32[1024,128]{1,0:T(8,128)}, f32[1024,128]{1,0:T(8,128)}) custom-call(s32[5]{0:T(128)} %stack.114.info, f32[1024,256]{1,0:T(8,128)} %bitcast.44, f32[1024,256]{1,0:T(8,128)} %copy-done.2, f32[256,4096]{1,0:T(8,128)} %refs_2_.5, f32[256,2048]{1,0:T(8,128)} %collective-permute-done.1.refs_3_, ...), custom_call_target="tpu_custom_call" | custom-call | flops 50331648 | bytes 131072 | tf_op jit(solution)/shard_map/pallas_call | solution.py:94
  38.0 11.1 %shard_map.56 = (f32[1024,128]{1,0:T(8,128)}, f32[1024,128]{1,0:T(8,128)}, f32[1024,128]{1,0:T(8,128)}, f32[1024,128]{1,0:T(8,128)}, f32[1024,128]{1,0:T(8,128)}...) custom-call(s32[8]{0:T(128)} %stack.111.info, f32[1024,256]{1,0:T(8,128)} %bitcast.45, ...), custom_call_target="tpu_custom_call" | custom-call | flops 125829120 | bytes 229376 | tf_op jit(solution)/shard_map/pallas_call | solution.py:94
  49.1 2.1 add.74
  51.2 1.9 collective-permute-start.14
  53.1 1.9 add.73
  55.0 1.9 collective-permute-start.12
  56.9 5.0 %shard_map.55 = (bf16[512,512]{1,0:T(8,128)(2,1)}, bf16[512,512]{1,0:T(8,128)(2,1)}, bf16[512,512]{1,0:T(8,128)(2,1)}, bf16[512,512]{1,0:T(8,128)(2,1)}, bf16[51...) custom-call(f32[8,3,64,512]{3,2,1,0:T(8,128)} %bitcast.47), custom_call_target="tpu_custom_call" | custom-call | flops 50331648 | bytes 196608 | tf_op jit(solution)/shard_map/pallas_call | solution.py:52
  61.9 1.0 collective-permute-done.5.refs_7_
  62.8 10.2 %collective-permute-done.14.refs_10_ = f32[1024,128]{1,0:T(8,128)} collective-permute-done((f32[1024,128]{1,0:T(8,128)}, f32[1024,128]{1,0:T(8,128)}, u32[]{:S(2)}, u32[]{:S(2)}) %collective-permute-start.14) | collective-permute-done | bytes 524320 | tf_op jit(solution)/shard_map/ppermute | solution.py:310
  73.1 0.8 copy-done.14
  73.9 5.6 %shard_map.59 = (f32[1024,512]{1,0:T(8,128)}, f32[1024,256]{1,0:T(8,128)}) custom-call(bf16[512,512]{1,0:T(8,128)(2,1)} %get-tuple-element.47.refs_0_, bf16[512,512]{1,0:T(8,128)(2,1)} %get-tuple-element.48.refs_1_, bf16[512,512]{1,0:T(8,128)(2,1)} %get-tuple-element.49.refs_2_, bf16[512,512]{1,0:T(8,128)(2,1)} %get-tuple-element.50.refs_3_, ...), custom_call_target="tpu_custom_call" | custom-call | flops 37748736 | bytes 294912 | tf_op jit(solution)/shard_map/pallas_call | solution.py:153
  80.1 1.7 collective-permute-start.6
  82.1 1.7 collective-permute-start.4
  83.9 11.0 %collective-permute-done.8 = f32[1024,128]{1,0:T(8,128)S(1)} collective-permute-done((f32[1024,128]{1,0:T(8,128)}, f32[1024,128]{1,0:T(8,128)S(1)}, u32[]{:S(2)}, u32[]{:S(2)}) %collective-permute-start.8) | collective-permute-done | bytes 524320 | tf_op jit(solution)/shard_map/ppermute | solution.py:305
  95.0 1.5 collective-permute-start.9
  96.6 0.6 collective-permute-start.7
  97.2 9.3 %collective-permute-done.3.refs_7_ = f32[1024,128]{1,0:T(8,128)S(1)} collective-permute-done((f32[1024,128]{1,0:T(8,128)}, f32[1024,128]{1,0:T(8,128)S(1)}, u32[]{:S(2)}, u32[]{:S(2)}) %collective-permute-start.3) | collective-permute-done | bytes 524320 | tf_op jit(solution)/shard_map/ppermute | solution.py:305
  106.4 9.3 %collective-permute-done.9.refs_10_ = f32[1024,128]{1,0:T(8,128)S(1)} collective-permute-done((f32[1024,128]{1,0:T(8,128)S(1)}, f32[1024,128]{1,0:T(8,128)S(1)}, u32[]{:S(2)}, u32[]{:S(2)}) %collective-permute-start.9) | collective-permute-done | bytes 524320 | tf_op jit(solution)/shard_map/ppermute | solution.py:310
  115.7 0.8 copy-done.13
  116.5 5.9 %shard_map.60 = (f32[1024,512]{1,0:T(8,128)}, f32[1024,256]{1,0:T(8,128)}, f32[1024,128]{1,0:T(8,128)}, f32[1024,128]{1,0:T(8,128)}) custom-call(bf16[512,512]{1,0:T(8,128)(2,1)} %get-tuple-element.47.refs_0_, bf16[512,512]{1,0:T(8,128)(2,1)} %get-tuple-element.48.refs_1_, ...), custom_call_target="tpu_custom_call", output_to_operand_aliasing={{0}: (11, {})} | custom-call | flops 37748736 | bytes 294912 | tf_op jit(solution)/shard_map/pallas_call | solution.py:153
  122.5 1.5 collective-permute-start.19
  123.9 1.4 collective-permute-start.18
  125.3 0.7 collective-permute-start.20
  126.0 0.6 collective-permute-start.15
  126.6 22.0 %collective-permute-done.19.refs_2_ = f32[1024,256]{1,0:T(8,128)S(1)} collective-permute-done((f32[1024,256]{1,0:T(8,128)}, f32[1024,256]{1,0:T(8,128)S(1)}, u32[]{:S(2)}, u32[]{:S(2)}) %collective-permute-start.19) | collective-permute-done | bytes 1048608 | tf_op jit(solution)/shard_map/ppermute | solution.py:327
  148.7 0.7 stack.126.place
  149.4 0.8 collective-permute-done.18.refs_1_
  150.2 6.1 %shard_map.61 = (bf16[8,1024,512]{2,1,0:T(8,128)(2,1)}, bf16[8,1024,512]{2,1,0:T(8,128)(2,1)}) custom-call(s32[2,2]{1,0:T(2,128)} %stack.126.place, f32[1024,512]{1,0:T(8,128)} %get-tuple-element.75.refs_0_, f32[1024,512]{1,0:T(8,128)} %collective-permute-done.16.refs_1_), custom_call_target="tpu_custom_call" | custom-call | bytes 262144 | tf_op jit(solution)/shard_map/pallas_call | solution.py:192
  156.3 4.4 %all-gather.13.cloned.1.call-done = f32[4096,256]{1,0:T(8,128)} async-done(((f32[1024,256]{1,0:T(8,128)}), f32[4096,256]{1,0:T(8,128)}) %all-gather.13.cloned.1.call-update) | async-done | bytes 4194320 | tf_op jit(solution)/shard_map/all_gather | solution.py:322
  160.7 4.5 %fusion = (f32[4,1024,128]{2,1,0:T(8,128)}, f32[4,1024,128]{2,1,0:T(8,128)}) fusion(f32[4,1024,256]{2,1,0:T(8,128)} %bitcast.46), kind=kLoop, calls=%fused_computation.11 | loop fusion | bytes 8388608 | tf_op jit(solution)/shard_map/slice | solution.py:339
  165.3 5.5 %collective-permute-done.20.refs_3_ = f32[1024,256]{1,0:T(8,128)} collective-permute-done((f32[1024,256]{1,0:T(8,128)}, f32[1024,256]{1,0:T(8,128)}, u32[]{:S(2)}, u32[]{:S(2)}) %collective-permute-start.20) | collective-permute-done | bytes 1048608 | tf_op jit(solution)/shard_map/ppermute | solution.py:325
  170.8 1.1 collective-permute-done.15.refs_0_
  172.0 0.8 collective-permute-start.17
  172.8 1.4 collective-permute-start.25
  174.2 4.5 %all-to-all-start.1 = ((f32[4,1024,128]{2,1,0:T(8,128)}), f32[4,1024,128]{2,1,0:T(8,128)}, u32[]{:S(2)}, u32[]{:S(2)}) async-start(f32[4,1024,128]{2,1,0:T(8,128)} %get-tuple-element.89), calls=%async_computation.1 | async-start | bytes 4194304 | tf_op jit(solution)/shard_map/all_to_all | solution.py:259
  179.4 14.3 %shard_map.62 = (bf16[8,1024,512]{2,1,0:T(8,128)(2,1)}, bf16[8,1024,512]{2,1,0:T(8,128)(2,1)}) custom-call(s32[2,8]{1,0:T(2,128)} %pad_add_fusion.place, f32[1024,256]{1,0:T(8,128)} %collective-permute-done.15.refs_0_, f32[1024,256]{1,0:T(8,128)} %collective-permute-done.18.refs_1_, ...), custom_call_target="tpu_custom_call", output_to_operand_aliasing={{0}: (9, {}), {1}: (10, {})} | custom-call | bytes 524288 | tf_op jit(solution)/shard_map/pallas_call | solution.py:192
  193.7 4.6 %collective-permute-done.17 = f32[1024,256]{1,0:T(8,128)} collective-permute-done((f32[1024,256]{1,0:T(8,128)}, f32[1024,256]{1,0:T(8,128)}, u32[]{:S(2)}, u32[]{:S(2)}) %collective-permute-start.17) | collective-permute-done | bytes 1048608 | tf_op jit(solution)/shard_map/ppermute | solution.py:341
  198.2 1.4 constant_dynamic-update-slice_fusion.1
  199.9 20.8 %all-to-all-done.1.pieces = f32[4,1024,128]{2,1,0:T(8,128)} async-done(((f32[4,1024,128]{2,1,0:T(8,128)}), f32[4,1024,128]{2,1,0:T(8,128)}, u32[]{:S(2)}, u32[]{:S(2)}) %all-to-all-start.1) | async-done | bytes 2097184 | tf_op jit(solution)/shard_map/all_to_all | solution.py:259
  220.7 4.5 %all-to-all-start = ((f32[4,1024,128]{2,1,0:T(8,128)}), f32[4,1024,128]{2,1,0:T(8,128)}, u32[]{:S(2)}, u32[]{:S(2)}) async-start(f32[4,1024,128]{2,1,0:T(8,128)} %get-tuple-element.90), calls=%async_computation | async-start | bytes 4194304 | tf_op jit(solution)/shard_map/all_to_all | solution.py:259
  225.8 6.1 %shard_map.63 = (bf16[8,1024,512]{2,1,0:T(8,128)(2,1)}, bf16[8,1024,512]{2,1,0:T(8,128)(2,1)}) custom-call(s32[2,2]{1,0:T(2,128)} %stack.121.place, f32[1024,512]{1,0:T(8,128)} %copy-done.3, f32[1024,512]{1,0:T(8,128)} %collective-permute-done.26.refs_1_, ...), custom_call_target="tpu_custom_call", output_to_operand_aliasing={{0}: (3, {}), {1}: (4, {})} | custom-call | bytes 262144 | tf_op jit(solution)/shard_map/pallas_call | solution.py:192
  231.9 18.6 %shard_map.64.refs_0_ = f32[4,512,4096]{2,1,0:T(8,128)} custom-call(f32[4,1024,128]{2,1,0:T(8,128)} %all-to-all-done.1.pieces, bf16[8,1024,512]{2,1,0:T(8,128)(2,1)} %get-tuple-element.85.high, bf16[8,1024,512]{2,1,0:T(8,128)(2,1)} %get-tuple-element.86.low), custom_call_target="tpu_custom_call" | custom-call | flops 402653184 | bytes 851968 | tf_op jit(solution)/shard_map/pallas_call | solution.py:235
  250.5 4.4 %all-to-all-start.3 = ((f32[4,1024,128]{2,1,0:T(8,128)}), f32[4,1024,128]{2,1,0:T(8,128)}, u32[]{:S(2)}, u32[]{:S(2)}) async-start(f32[4,1024,128]{2,1,0:T(8,128)} %bitcast.48), calls=%async_computation.3 | async-start | bytes 4194304 | tf_op jit(solution)/shard_map/all_to_all | solution.py:259
  255.0 18.6 %shard_map.65.refs_0_ = f32[4,512,4096]{2,1,0:T(8,128)} custom-call(f32[4,1024,128]{2,1,0:T(8,128)} %all-to-all-done.pieces, bf16[8,1024,512]{2,1,0:T(8,128)(2,1)} %get-tuple-element.85.high, bf16[8,1024,512]{2,1,0:T(8,128)(2,1)} %get-tuple-element.86.low, f32[4,512,4096]{2,1,0:T(8,128)} %shard_map.64.refs_0_), custom_call_target="tpu_custom_call", output_to_operand_aliasing={{}: (3, {})} | custom-call | flops 402653184 | bytes 851968 | tf_op jit(solution)/shard_map/pallas_call | solution.py:235
  273.6 6.7 %all-to-all-done.3.pieces = f32[4,1024,128]{2,1,0:T(8,128)} async-done(((f32[4,1024,128]{2,1,0:T(8,128)}), f32[4,1024,128]{2,1,0:T(8,128)}, u32[]{:S(2)}, u32[]{:S(2)}) %all-to-all-start.3) | async-done | bytes 2097184 | tf_op jit(solution)/shard_map/all_to_all | solution.py:259
  280.3 4.5 %all-to-all-start.2 = ((f32[4,1024,128]{2,1,0:T(8,128)}), f32[4,1024,128]{2,1,0:T(8,128)}, u32[]{:S(2)}, u32[]{:S(2)}) async-start(f32[4,1024,128]{2,1,0:T(8,128)} %bitcast.49), calls=%async_computation.2 | async-start | bytes 4194304 | tf_op jit(solution)/shard_map/all_to_all | solution.py:259
  284.7 18.6 %shard_map.66.refs_0_ = f32[4,512,4096]{2,1,0:T(8,128)} custom-call(f32[4,1024,128]{2,1,0:T(8,128)} %all-to-all-done.3.pieces, bf16[8,1024,512]{2,1,0:T(8,128)(2,1)} %get-tuple-element.85.high, bf16[8,1024,512]{2,1,0:T(8,128)(2,1)} %get-tuple-element.86.low, f32[4,512,4096]{2,1,0:T(8,128)} %shard_map.65.refs_0_), custom_call_target="tpu_custom_call", output_to_operand_aliasing={{}: (3, {})} | custom-call | flops 402653184 | bytes 851968 | tf_op jit(solution)/shard_map/pallas_call | solution.py:235
  303.3 5.6 %all-to-all-done.2.pieces = f32[4,1024,128]{2,1,0:T(8,128)} async-done(((f32[4,1024,128]{2,1,0:T(8,128)}), f32[4,1024,128]{2,1,0:T(8,128)}, u32[]{:S(2)}, u32[]{:S(2)}) %all-to-all-start.2) | async-done | bytes 2097184 | tf_op jit(solution)/shard_map/all_to_all | solution.py:259
  308.9 18.6 %shard_map.67 = f32[4,512,4096]{2,1,0:T(8,128)} custom-call(f32[4,1024,128]{2,1,0:T(8,128)} %all-to-all-done.2.pieces, bf16[8,1024,512]{2,1,0:T(8,128)(2,1)} %get-tuple-element.85.high, bf16[8,1024,512]{2,1,0:T(8,128)(2,1)} %get-tuple-element.86.low, f32[4,512,4096]{2,1,0:T(8,128)} %shard_map.66.refs_0_), custom_call_target="tpu_custom_call", output_to_operand_aliasing={{}: (3, {})} | custom-call | flops 402653184 | bytes 851968 | tf_op jit(solution)/shard_map/pallas_call | solution.py:235
  (77 shorter events, 3.9 us)
Async XLA Ops:
  6.5 50.4 %all-gather.9.cloned.1.call-start = ((), (), s32[]{:S(2)}) async-start(), calls=%async_computation.4 | async-start | bytes 3538944 | tf_op jit(solution)/shard_map/all_gather | solution.py:50
  9.3 151.5 %all-gather.13.cloned.1.call-start = ((), (), s32[]{:S(2)}) async-start(), calls=%async_computation.6 | async-start | bytes 5242880 | tf_op jit(solution)/shard_map/all_gather | solution.py:322
  9.3 3.8 %copy-start.4 = (f32[64,2,4096]{2,1,0:T(2,128)S(1)}, f32[64,2,4096]{2,1,0:T(2,128)}, u32[]{:S(2)}) copy-start(f32[64,2,4096]{2,1,0:T(2,128)} %param.7) | copy-start | bytes 6291460
  12.6 8.2 %collective-permute-start.1 = (f32[256,2048]{1,0:T(8,128)}, f32[256,2048]{1,0:T(8,128)}, u32[]{:S(2)}, u32[]{:S(2)}) collective-permute-start(f32[256,2048]{1,0:T(8,128)} %constant_dynamic-slice_fusion), channel_id=1, source_target_pairs={{0,4},{4,0},{8,12},{12,8},{16,20},{20,16},{24,28},{28,24},{1,5},{5... | collective-permute-start | bytes 6291464 | tf_op jit(solution)/shard_map/ppermute | solution.py:278
  14.3 2.1 copy-start
  14.3 2.0 copy-start.6
  15.4 3.3 collective-permute-start.2
  16.4 4.4 %copy-start.1 = (f32[2,512,256]{2,1,0:T(8,128)}, f32[2,512,256]{2,1,0:T(8,128)S(1)}, u32[]{:S(2)}) copy-start(f32[2,512,256]{2,1,0:T(8,128)S(1)} %copy.20) | copy-start | bytes 3145732
  16.4 3.4 %collective-permute-start = (f32[1024,256]{1,0:T(8,128)S(1)}, f32[1024,256]{1,0:T(8,128)S(1)}, u32[]{:S(2)}, u32[]{:S(2)}) collective-permute-start(f32[1024,256]{1,0:T(8,128)S(1)} %bitcast.42), channel_id=1, source_target_pairs={{0,4},{4,0},{8,12},{12,8},{16,20},{20,16},{24,28},{28,24},{1,5},{5... | collective-permute-start | bytes 3145736 | tf_op jit(solution)/shard_map/ppermute | solution.py:282
  19.9 1.0 copy-start.2
  25.3 23.8 %collective-permute-start.13 = (f32[1024,128]{1,0:T(8,128)}, f32[1024,128]{1,0:T(8,128)}, u32[]{:S(2)}, u32[]{:S(2)}) collective-permute-start(f32[1024,128]{1,0:T(8,128)} %get-tuple-element.69), channel_id=1, source_target_pairs={{0,16},{4,20},{8,24},{12,28},{16,0},{20,4},{24,8},{28,12},{1,17},{... | collective-permute-start | bytes 1572872 | tf_op jit(solution)/shard_map/ppermute | solution.py:305
  28.2 24.9 %collective-permute-start.11 = (f32[1024,128]{1,0:T(8,128)}, f32[1024,128]{1,0:T(8,128)S(1)}, u32[]{:S(2)}, u32[]{:S(2)}) collective-permute-start(f32[1024,128]{1,0:T(8,128)} %get-tuple-element.66), channel_id=1, source_target_pairs={{0,8},{4,12},{8,0},{12,4},{16,24},{20,28},{24,16},{28,20},{1,9},{5... | collective-permute-start | bytes 1572872 | tf_op jit(solution)/shard_map/ppermute | solution.py:305
  37.7 24.2 %collective-permute-start.10 = (f32[1024,128]{1,0:T(8,128)}, f32[1024,128]{1,0:T(8,128)S(1)}, u32[]{:S(2)}, u32[]{:S(2)}) collective-permute-start(f32[1024,128]{1,0:T(8,128)} %get-tuple-element.64), channel_id=1, source_target_pairs={{0,16},{4,20},{8,24},{12,28},{16,0},{20,4},{24,8},{28,12},{1,17},{... | collective-permute-start | bytes 1572872 | tf_op jit(solution)/shard_map/ppermute | solution.py:305
  37.9 25.0 %collective-permute-start.5 = (f32[1024,128]{1,0:T(8,128)}, f32[1024,128]{1,0:T(8,128)S(1)}, u32[]{:S(2)}, u32[]{:S(2)}) collective-permute-start(f32[1024,128]{1,0:T(8,128)} %get-tuple-element.58), channel_id=1, source_target_pairs={{0,8},{4,12},{8,0},{12,4},{16,24},{20,28},{24,16},{28,20},{1,9},{5... | collective-permute-start | bytes 1572872 | tf_op jit(solution)/shard_map/ppermute | solution.py:305
  51.2 21.9 %collective-permute-start.14 = (f32[1024,128]{1,0:T(8,128)}, f32[1024,128]{1,0:T(8,128)}, u32[]{:S(2)}, u32[]{:S(2)}) collective-permute-start(f32[1024,128]{1,0:T(8,128)} %add.74), channel_id=1, source_target_pairs={{0,8},{4,12},{8,0},{12,4},{16,24},{20,28},{24,16},{28,20},{1,9},{5... | collective-permute-start | bytes 1572872 | tf_op jit(solution)/shard_map/ppermute | solution.py:310
  55.0 18.1 %collective-permute-start.12 = (f32[1024,128]{1,0:T(8,128)}, f32[1024,128]{1,0:T(8,128)S(1)}, u32[]{:S(2)}, u32[]{:S(2)}) collective-permute-start(f32[1024,128]{1,0:T(8,128)} %add.73), channel_id=1, source_target_pairs={{0,16},{4,20},{8,24},{12,28},{16,0},{20,4},{24,8},{28,12},{1,17},{... | collective-permute-start | bytes 1572872 | tf_op jit(solution)/shard_map/ppermute | solution.py:309
  61.9 12.0 %copy-start.9 = (f32[1024,128]{1,0:T(8,128)}, f32[1024,128]{1,0:T(8,128)S(1)}, u32[]{:S(2)}) copy-start(f32[1024,128]{1,0:T(8,128)S(1)} %collective-permute-done.10.refs_8_) | copy-start | bytes 1572868
  62.8 11.1 %copy-start.10 = (f32[1024,128]{1,0:T(8,128)}, f32[1024,128]{1,0:T(8,128)S(1)}, u32[]{:S(2)}) copy-start(f32[1024,128]{1,0:T(8,128)S(1)} %collective-permute-done.5.refs_7_) | copy-start | bytes 1572868
  73.1 0.8 copy-start.14
  73.9 21.0 %copy-start.8 = (f32[1024,128]{1,0:T(8,128)S(1)}, f32[1024,128]{1,0:T(8,128)}, u32[]{:S(2)}) copy-start(f32[1024,128]{1,0:T(8,128)} %get-tuple-element.60) | copy-start | bytes 1572868
  79.5 17.0 %copy-start.7 = (f32[1024,128]{1,0:T(8,128)S(1)}, f32[1024,128]{1,0:T(8,128)}, u32[]{:S(2)}) copy-start(f32[1024,128]{1,0:T(8,128)} %get-tuple-element.56) | copy-start | bytes 1572868
  79.5 146.3 %all-gather.15.cloned.1.call-start = ((), (), s32[]{:S(2)}) async-start(), calls=%async_computation.7 | async-start | bytes 2621440 | tf_op jit(solution)/shard_map/all_gather | solution.py:322
  79.8 15.1 %collective-permute-start.8 = (f32[1024,128]{1,0:T(8,128)}, f32[1024,128]{1,0:T(8,128)S(1)}, u32[]{:S(2)}, u32[]{:S(2)}) collective-permute-start(f32[1024,128]{1,0:T(8,128)} %get-tuple-element.62), channel_id=1, source_target_pairs={{0,16},{4,20},{8,24},{12,28},{16,0},{20,4},{24,8},{28,12},{1,17},{... | collective-permute-start | bytes 1572872 | tf_op jit(solution)/shard_map/ppermute | solution.py:305
  80.1 16.4 %collective-permute-start.6 = (f32[1024,128]{1,0:T(8,128)}, f32[1024,128]{1,0:T(8,128)S(1)}, u32[]{:S(2)}, u32[]{:S(2)}) collective-permute-start(f32[1024,128]{1,0:T(8,128)} %get-tuple-element.59), channel_id=1, source_target_pairs={{0,8},{4,12},{8,0},{12,4},{16,24},{20,28},{24,16},{28,20},{1,9},{5... | collective-permute-start | bytes 1572872 | tf_op jit(solution)/shard_map/ppermute | solution.py:305
  81.8 24.6 %collective-permute-start.3 = (f32[1024,128]{1,0:T(8,128)}, f32[1024,128]{1,0:T(8,128)S(1)}, u32[]{:S(2)}, u32[]{:S(2)}) collective-permute-start(f32[1024,128]{1,0:T(8,128)} %get-tuple-element.54), channel_id=1, source_target_pairs={{0,8},{4,12},{8,0},{12,4},{16,24},{20,28},{24,16},{28,20},{1,9},{5... | collective-permute-start | bytes 1572872 | tf_op jit(solution)/shard_map/ppermute | solution.py:305
  82.1 24.3 %collective-permute-start.4 = (f32[1024,128]{1,0:T(8,128)}, f32[1024,128]{1,0:T(8,128)S(1)}, u32[]{:S(2)}, u32[]{:S(2)}) collective-permute-start(f32[1024,128]{1,0:T(8,128)} %get-tuple-element.55), channel_id=1, source_target_pairs={{0,16},{4,20},{8,24},{12,28},{16,0},{20,4},{24,8},{28,12},{1,17},{... | collective-permute-start | bytes 1572872 | tf_op jit(solution)/shard_map/ppermute | solution.py:305
  95.0 20.7 %collective-permute-start.9 = (f32[1024,128]{1,0:T(8,128)S(1)}, f32[1024,128]{1,0:T(8,128)S(1)}, u32[]{:S(2)}, u32[]{:S(2)}) collective-permute-start(f32[1024,128]{1,0:T(8,128)S(1)} %add.72), channel_id=1, source_target_pairs={{0,8},{4,12},{8,0},{12,4},{16,24},{20,28},{24,16},{28,20},{1,9},{5... | collective-permute-start | bytes 1572872 | tf_op jit(solution)/shard_map/ppermute | solution.py:310
  96.6 19.1 %collective-permute-start.7 = (f32[1024,128]{1,0:T(8,128)S(1)}, f32[1024,128]{1,0:T(8,128)}, u32[]{:S(2)}, u32[]{:S(2)}) collective-permute-start(f32[1024,128]{1,0:T(8,128)S(1)} %add.71), channel_id=1, source_target_pairs={{0,16},{4,20},{8,24},{12,28},{16,0},{20,4},{24,8},{28,12},{1,17},{... | collective-permute-start | bytes 1572872 | tf_op jit(solution)/shard_map/ppermute | solution.py:309
  106.4 9.3 %copy-start.11 = (f32[1024,128]{1,0:T(8,128)}, f32[1024,128]{1,0:T(8,128)S(1)}, u32[]{:S(2)}) copy-start(f32[1024,128]{1,0:T(8,128)S(1)} %collective-permute-done.3.refs_7_) | copy-start | bytes 1572868
  106.4 9.3 %copy-start.12 = (f32[1024,128]{1,0:T(8,128)}, f32[1024,128]{1,0:T(8,128)S(1)}, u32[]{:S(2)}) copy-start(f32[1024,128]{1,0:T(8,128)S(1)} %collective-permute-done.4.refs_8_) | copy-start | bytes 1572868
  115.7 0.9 copy-start.13
  122.5 27.8 %collective-permute-start.16 = (f32[1024,512]{1,0:T(8,128)}, f32[1024,512]{1,0:T(8,128)}, u32[]{:S(2)}, u32[]{:S(2)}) collective-permute-start(f32[1024,512]{1,0:T(8,128)} %get-tuple-element.75.refs_0_), channel_id=1, source_target_pairs={{0,4},{4,0},{8,12},{12,8},{16,20},{20,16},{24,28},{28,24},{1,5},{5... | collective-permute-start | bytes 6291464 | tf_op jit(solution)/shard_map/ppermute | solution.py:328
  122.5 26.2 %collective-permute-start.19 = (f32[1024,256]{1,0:T(8,128)}, f32[1024,256]{1,0:T(8,128)S(1)}, u32[]{:S(2)}, u32[]{:S(2)}) collective-permute-start(f32[1024,256]{1,0:T(8,128)} %get-tuple-element.74), channel_id=1, source_target_pairs={{0,16},{4,20},{8,24},{12,28},{16,0},{20,4},{24,8},{28,12},{1,17},{... | collective-permute-start | bytes 3145736 | tf_op jit(solution)/shard_map/ppermute | solution.py:327
  123.9 26.3 %collective-permute-start.18 = (f32[1024,256]{1,0:T(8,128)}, f32[1024,256]{1,0:T(8,128)}, u32[]{:S(2)}, u32[]{:S(2)}) collective-permute-start(f32[1024,256]{1,0:T(8,128)} %get-tuple-element.73), channel_id=1, source_target_pairs={{0,8},{4,12},{8,0},{12,4},{16,24},{20,28},{24,16},{28,20},{1,9},{5... | collective-permute-start | bytes 3145736 | tf_op jit(solution)/shard_map/ppermute | solution.py:326
  125.3 45.5 %collective-permute-start.20 = (f32[1024,256]{1,0:T(8,128)}, f32[1024,256]{1,0:T(8,128)}, u32[]{:S(2)}, u32[]{:S(2)}) collective-permute-start(f32[1024,256]{1,0:T(8,128)} %get-tuple-element.73), channel_id=1, source_target_pairs={{0,16},{4,20},{8,24},{12,28},{16,0},{20,4},{24,8},{28,12},{1,17},{... | collective-permute-start | bytes 3145736 | tf_op jit(solution)/shard_map/ppermute | solution.py:325
  126.0 46.0 %collective-permute-start.15 = (f32[1024,256]{1,0:T(8,128)}, f32[1024,256]{1,0:T(8,128)}, u32[]{:S(2)}, u32[]{:S(2)}) collective-permute-start(f32[1024,256]{1,0:T(8,128)} %get-tuple-element.74), channel_id=1, source_target_pairs={{0,8},{4,12},{8,0},{12,4},{16,24},{20,28},{24,16},{28,20},{1,9},{5... | collective-permute-start | bytes 3145736 | tf_op jit(solution)/shard_map/ppermute | solution.py:324
  148.7 7.6 %copy-start.5 = (f32[1024,256]{1,0:T(8,128)}, f32[1024,256]{1,0:T(8,128)S(1)}, u32[]{:S(2)}) copy-start(f32[1024,256]{1,0:T(8,128)S(1)} %collective-permute-done.19.refs_2_) | copy-start | bytes 3145732
  148.7 24.1 %collective-permute-start.23 = (f32[1024,256]{1,0:T(8,128)S(1)}, f32[1024,256]{1,0:T(8,128)}, u32[]{:S(2)}, u32[]{:S(2)}) collective-permute-start(f32[1024,256]{1,0:T(8,128)S(1)} %collective-permute-done.19.refs_2_), channel_id=1, source_target_pairs={{0,4},{4,0},{8,12},{12,8},{16,20},{20,16},{24,28},{28,24},{1,5},{5... | collective-permute-start | bytes 3145736 | tf_op jit(solution)/shard_map/ppermute | solution.py:336
  150.2 29.1 %collective-permute-start.22 = (f32[1024,256]{1,0:T(8,128)}, f32[1024,256]{1,0:T(8,128)}, u32[]{:S(2)}, u32[]{:S(2)}) collective-permute-start(f32[1024,256]{1,0:T(8,128)} %collective-permute-done.18.refs_1_), channel_id=1, source_target_pairs={{0,4},{4,0},{8,12},{12,8},{16,20},{20,16},{24,28},{28,24},{1,5},{5... | collective-permute-start | bytes 3145736 | tf_op jit(solution)/shard_map/ppermute | solution.py:336
  170.8 8.0 %copy-start.15 = (s32[1,8]{1,0:T(1,128)S(1)}, s32[1,8]{1,0:T(1,128)}, u32[]{:S(2)}) copy-start(s32[1,8]{1,0:T(1,128)} %constant.42.clone.1) | copy-start | bytes 100
  170.8 8.5 %collective-permute-start.24 = (f32[1024,256]{1,0:T(8,128)}, f32[1024,256]{1,0:T(8,128)}, u32[]{:S(2)}, u32[]{:S(2)}) collective-permute-start(f32[1024,256]{1,0:T(8,128)} %collective-permute-done.20.refs_3_), channel_id=1, source_target_pairs={{0,4},{4,0},{8,12},{12,8},{16,20},{20,16},{24,28},{28,24},{1,5},{5... | collective-permute-start | bytes 3145736 | tf_op jit(solution)/shard_map/ppermute | solution.py:336
  172.0 7.4 %collective-permute-start.21 = (f32[1024,256]{1,0:T(8,128)}, f32[1024,256]{1,0:T(8,128)}, u32[]{:S(2)}, u32[]{:S(2)}) collective-permute-start(f32[1024,256]{1,0:T(8,128)} %collective-permute-done.15.refs_0_), channel_id=1, source_target_pairs={{0,4},{4,0},{8,12},{12,8},{16,20},{20,16},{24,28},{28,24},{1,5},{5... | collective-permute-start | bytes 3145736 | tf_op jit(solution)/shard_map/ppermute | solution.py:336
  172.0 26.3 %collective-permute-start.17 = (f32[1024,256]{1,0:T(8,128)}, f32[1024,256]{1,0:T(8,128)}, u32[]{:S(2)}, u32[]{:S(2)}) collective-permute-start(f32[1024,256]{1,0:T(8,128)} %collective-permute-done.15.refs_0_), channel_id=1, source_target_pairs={{0,16},{4,20},{8,24},{12,28},{16,0},{20,4},{24,8},{28,12},{1,17},{... | collective-permute-start | bytes 3145736 | tf_op jit(solution)/shard_map/ppermute | solution.py:341
  172.8 26.9 %collective-permute-start.25 = (f32[1024,256]{1,0:T(8,128)}, f32[1024,256]{1,0:T(8,128)S(1)}, u32[]{:S(2)}, u32[]{:S(2)}) collective-permute-start(f32[1024,256]{1,0:T(8,128)} %collective-permute-done.20.refs_3_), channel_id=1, source_target_pairs={{0,8},{4,12},{8,0},{12,4},{16,24},{20,28},{24,16},{28,20},{1,9},{5... | collective-permute-start | bytes 3145736 | tf_op jit(solution)/shard_map/ppermute | solution.py:342
  174.2 46.5 %all-to-all-start.1 = ((f32[4,1024,128]{2,1,0:T(8,128)}), f32[4,1024,128]{2,1,0:T(8,128)}, u32[]{:S(2)}, u32[]{:S(2)}) async-start(f32[4,1024,128]{2,1,0:T(8,128)} %get-tuple-element.89), calls=%async_computation.1 | async-start | bytes 4194304 | tf_op jit(solution)/shard_map/all_to_all | solution.py:259
  178.6 94.9 %all-gather.11.cloned.1.call-start = ((), (), s32[]{:S(2)}) async-start(), calls=%async_computation.5 | async-start | bytes 2621440 | tf_op jit(solution)/shard_map/all_gather | solution.py:322
  199.8 20.9 %copy-start.3 = (f32[1024,512]{1,0:T(8,128)}, f32[1024,512]{1,0:T(8,128)S(1)}, u32[]{:S(2)}) copy-start(f32[1024,512]{1,0:T(8,128)S(1)} %constant_dynamic-update-slice_fusion.refs_0_) | copy-start | bytes 6291460
  199.8 26.0 %collective-permute-start.26 = (f32[1024,512]{1,0:T(8,128)S(1)}, f32[1024,512]{1,0:T(8,128)}, u32[]{:S(2)}, u32[]{:S(2)}) collective-permute-start(f32[1024,512]{1,0:T(8,128)S(1)} %constant_dynamic-update-slice_fusion.refs_0_), channel_id=1, source_target_pairs={{0,4},{4,0},{8,12},{12,8},{16,20},{20,16},{24,28},{28,24},{1,5},{5... | collective-permute-start | bytes 6291464 | tf_op jit(solution)/shard_map/ppermute | solution.py:336
  220.7 29.8 %all-to-all-start = ((f32[4,1024,128]{2,1,0:T(8,128)}), f32[4,1024,128]{2,1,0:T(8,128)}, u32[]{:S(2)}, u32[]{:S(2)}) async-start(f32[4,1024,128]{2,1,0:T(8,128)} %get-tuple-element.90), calls=%async_computation | async-start | bytes 4194304 | tf_op jit(solution)/shard_map/all_to_all | solution.py:259
  250.5 29.7 %all-to-all-start.3 = ((f32[4,1024,128]{2,1,0:T(8,128)}), f32[4,1024,128]{2,1,0:T(8,128)}, u32[]{:S(2)}, u32[]{:S(2)}) async-start(f32[4,1024,128]{2,1,0:T(8,128)} %bitcast.48), calls=%async_computation.3 | async-start | bytes 4194304 | tf_op jit(solution)/shard_map/all_to_all | solution.py:259
  280.3 28.7 %all-to-all-start.2 = ((f32[4,1024,128]{2,1,0:T(8,128)}), f32[4,1024,128]{2,1,0:T(8,128)}, u32[]{:S(2)}, u32[]{:S(2)}) async-start(f32[4,1024,128]{2,1,0:T(8,128)} %bitcast.49), calls=%async_computation.2 | async-start | bytes 4194304 | tf_op jit(solution)/shard_map/all_to_all | solution.py:259
Sparse Core Ops, SparseCore 0:
  9.4 43.5 all-gather.8
  79.7 81.0 all-gather.12
  162.3 44.4 all-gather.14
  208.2 44.6 all-gather.10

commit v5 on v4

--- a/solution.py
+++ b/solution.py
@@ -319,7 +319,7 @@
     solved, late_half, *chunks = solve(
         matrix, (late_keep, *late_terms), (half, quarter, quarter), solved
     )
-    blocks = [lax.all_gather(x, "col", axis=0) for x in (chunk, *chunks)]
+    blocks = [lax.all_gather(x, "col", axis=0) for x in (after(chunk, *first), *chunks)]
 
     x_early = lax.ppermute(after(chunk, late_half), "row", ALONG_X)
     y_late = lax.ppermute(late_half, "row", ALONG_Y)
@@ -337,17 +337,19 @@
 
     held = split([solved], [twin], ((0, 0),), ())
     first_chunk = blocks[0][:, :, :quarter]
-    x_early, y_late = after(x_early, first_chunk, *held), after(y_late, first_chunk, *held)
+    x_early, y_late = after(x_early, *held), after(y_late, *held)
+    x_late, y_early = after(x_late, first_chunk), after(y_early, first_chunk)
     far_a = lax.ppermute(x_early, "row", ALONG_Y)
     far_b = lax.ppermute(y_late, "row", ALONG_X)
     sides = [x_early, x_late, y_early, y_late]
     held = split(sides, given(*sides), ((1, 0), (1, 1), (2, 0), (2, 1)), held)
+    second_chunk = after(blocks[0], *held)[:, :, quarter:]
     far = jnp.concatenate([after(far_a, *held), far_b], axis=1)
     pieces = to_chips(first_chunk)
     twin = given(far)
     held = split([after(far, pieces, blocks[1])], twin, ((3, 0),), held)
     out = before = downdate_part(pieces, held, None, 0)
-    pieces = to_chips(blocks[0][:, :, quarter:])
+    pieces = to_chips(second_chunk)
     out = downdate_part(pieces, held, out, 1)
     pieces = to_chips(after(blocks[1], before))
     before, out = out, downdate_part(pieces, held, out, 2)

time: 336 us -> 333 us (level)
  waiting for transfers between devices: 115 us -> 106 us
    ppermute x1, waiting for transfers between devices: 22 us -> 0.01 us  [local(): y_early = lax.ppermute(after(chunk, late_half), 'row', ALONG_Y)]
    all_gather x3, waiting for transfers between devices: 4.43 us -> 22.3 us  [local(): lax.all_gather(x, 'col', axis=0)]
    ppermute x1, waiting for transfers between devices: 5.54 us -> 15.3 us  [local(): y_late = lax.ppermute(late_half, 'row', ALONG_Y)]
    ppermute x2, waiting for transfers between devices: 19.5 us -> 12 us  [arrivals(): b_last = lax.ppermute(b_on + first[1], 'row', ALONG_X)]
    ppermute x4, waiting for transfers between devices: 11 us -> 4.49 us  [passed(): lax.ppermute(b_pass, 'row', ALONG_Y)]
    all_to_all x4, waiting for transfers between devices: 33.1 us -> 26.7 us  [to_chips(): return lax.all_to_all(blocks, 'row', 0, 0, axis_index_groups=SAME_CORE)]
    ppermute x4, waiting for transfers between devices: 10.2 us -> 16.1 us  [passed(): lax.ppermute(a_pass, 'row', ALONG_X)]
    slice x0 -> x1, local copies, waits for them, and re-layouts: none -> 3.69 us  [local(): second_chunk = after(blocks[0], *held)[:, :, quarter:]]
  transfers between devices with their start and end apart: 35 -> 35, of which waited for: 16 -> 18; matrix products, arithmetic and copies ran while one was open for 6% -> 8% of each run, Pallas kernels for 35% -> 37%
where the time goes in v5:
time: 333 us; the launch traced here: 331 us
  Pallas kernels  139 us (42%)
  waiting for transfers between devices  106 us (32%)
  starting transfers between devices  41.5 us (12%)
  local copies, waits for them, and re-layouts  21.5 us (6%)
  between operations  13.4 us (4%)
  other arithmetic  9.21 us (3%)
    pallas_call x4, Pallas kernels, downdate_part(): pl.pallas_call(downdate_kernel, grid=(8,), in_specs=specs, out_specs=pl.B...  74.4 us
    all_to_all x4, waiting for transfers between devices, to_chips(): return lax.all_to_all(blocks, 'row', 0, 0, axis_index_groups=SAME_CORE)  26.7 us
    pallas_call x3, Pallas kernels, split_blocks(): pl.pallas_call(functools.partial(split_kernel, parts, count), grid_spec=p...  26.5 us
    all_gather x3, waiting for transfers between devices, local(): lax.all_gather(x, 'col', axis=0)  22.3 us
    pallas_call x3, Pallas kernels, update_blocks(): pl.pallas_call(lambda info, *refs: partial_updates(steps, [info[count + n...  21.9 us
    all_to_all x4, starting transfers between devices, to_chips(): return lax.all_to_all(blocks, 'row', 0, 0, axis_index_groups=SAME_CORE)  17.9 us
    ppermute x4, waiting for transfers between devices, passed(): lax.ppermute(a_pass, 'row', ALONG_X)  16.1 us
    ppermute x1, waiting for transfers between devices, local(): y_late = lax.ppermute(late_half, 'row', ALONG_Y)  15.3 us
  transfers between devices with their start and end apart: 35, of which 18 were waited for; matrix products, arithmetic and copies ran while one was open for 8% of the time, Pallas kernels for 37%

profile of v5, /device:TPU:0, one launch (start us, length us, event | category | flops | bytes accessed | tf_op | source)
XLA Modules:
  0.0 330.8 jit_solution(15533926348240810544)
XLA Ops:
  6.5 1.0 copy.26
  7.5 1.7 pad_maximum_fusion
  9.3 3.3 constant_dynamic-slice_fusion
  13.1 1.2 copy.27
  14.3 1.1 dynamic-slice_bitcast_fusion
  15.5 0.8 copy-done.7
  16.5 0.7 stack.114.info
  17.9 0.8 collective-permute-done.2.refs_5_
  18.7 1.2 collective-permute-done.refs_1_
  19.9 1.0 copy-done.2
  20.9 4.4 %shard_map.58 = (f32[1024,128]{1,0:T(8,128)}, f32[1024,128]{1,0:T(8,128)}) custom-call(s32[4]{0:T(128)} %pad_add_fusion.1.info, f32[1024,256]{1,0:T(8,128)} %bitcast.43, f32[1024,256]{1,0:T(8,128)} %copy-done.2, f32[256,4096]{1,0:T(8,128)} %refs_2_.5, f32[256,2048]{1,0:T(8,128)} %collective-permute-done.1.refs_3_, f32[2,64,4096]{2,1,0:T(8,128)} %bitcast.39, ...), custom_call_target="tpu_custom_call" | custom-call | flops 25165824 | bytes 98304 | tf_op jit(solution)/shard_map/pallas_call | solution.py:94
  25.3 2.9 collective-permute-start.13
  28.2 1.5 collective-permute-start.11
  29.7 6.4 %shard_map.57 = (f32[1024,128]{1,0:T(8,128)}, f32[1024,128]{1,0:T(8,128)}, f32[1024,128]{1,0:T(8,128)}, f32[1024,128]{1,0:T(8,128)}) custom-call(s32[5]{0:T(128)} %stack.114.info, f32[1024,256]{1,0:T(8,128)} %bitcast.44, f32[1024,256]{1,0:T(8,128)} %copy-done.2, f32[256,4096]{1,0:T(8,128)} %refs_2_.5, f32[256,2048]{1,0:T(8,128)} %collective-permute-done.1.refs_3_, ...), custom_call_target="tpu_custom_call" | custom-call | flops 50331648 | bytes 131072 | tf_op jit(solution)/shard_map/pallas_call | solution.py:94
  37.2 11.1 %shard_map.56 = (f32[1024,128]{1,0:T(8,128)}, f32[1024,128]{1,0:T(8,128)}, f32[1024,128]{1,0:T(8,128)}, f32[1024,128]{1,0:T(8,128)}, f32[1024,128]{1,0:T(8,128)}...) custom-call(s32[8]{0:T(128)} %stack.111.info, f32[1024,256]{1,0:T(8,128)} %bitcast.45, ...), custom_call_target="tpu_custom_call" | custom-call | flops 125829120 | bytes 229376 | tf_op jit(solution)/shard_map/pallas_call | solution.py:94
  48.3 0.9 collective-permute-done.13
  49.2 2.0 add.74
  51.2 1.2 collective-permute-start.14
  52.5 1.9 add.73
  54.4 2.5 collective-permute-start.12
  56.9 6.0 %collective-permute-done.5.refs_7_ = f32[1024,128]{1,0:T(8,128)S(1)} collective-permute-done((f32[1024,128]{1,0:T(8,128)}, f32[1024,128]{1,0:T(8,128)S(1)}, u32[]{:S(2)}, u32[]{:S(2)}) %collective-permute-start.5) | collective-permute-done | bytes 524320 | tf_op jit(solution)/shard_map/ppermute | solution.py:305
  62.9 2.0 collective-permute-start.6
  64.8 5.0 %shard_map.55 = (bf16[512,512]{1,0:T(8,128)(2,1)}, bf16[512,512]{1,0:T(8,128)(2,1)}, bf16[512,512]{1,0:T(8,128)(2,1)}, bf16[512,512]{1,0:T(8,128)(2,1)}, bf16[51...) custom-call(f32[8,3,64,512]{3,2,1,0:T(8,128)} %bitcast.48), custom_call_target="tpu_custom_call" | custom-call | flops 50331648 | bytes 196608 | tf_op jit(solution)/shard_map/pallas_call | solution.py:52
  69.9 4.3 %collective-permute-done.14.refs_10_ = f32[1024,128]{1,0:T(8,128)} collective-permute-done((f32[1024,128]{1,0:T(8,128)}, f32[1024,128]{1,0:T(8,128)}, u32[]{:S(2)}, u32[]{:S(2)}) %collective-permute-start.14) | collective-permute-done | bytes 524320 | tf_op jit(solution)/shard_map/ppermute | solution.py:310
  74.2 0.8 copy-done.14
  75.0 5.7 %shard_map.59 = (f32[1024,512]{1,0:T(8,128)}, f32[1024,256]{1,0:T(8,128)}) custom-call(bf16[512,512]{1,0:T(8,128)(2,1)} %get-tuple-element.51.refs_0_, bf16[512,512]{1,0:T(8,128)(2,1)} %get-tuple-element.52.refs_1_, bf16[512,512]{1,0:T(8,128)(2,1)} %get-tuple-element.53.refs_2_, bf16[512,512]{1,0:T(8,128)(2,1)} %get-tuple-element.54.refs_3_, ...), custom_call_target="tpu_custom_call" | custom-call | flops 37748736 | bytes 294912 | tf_op jit(solution)/shard_map/pallas_call | solution.py:153
  80.7 2.1 collective-permute-done.8
  82.8 1.5 collective-permute-done.6
  84.6 1.6 collective-permute-start.3
  86.6 1.1 add.72
  88.1 1.1 add.71
  89.2 1.8 collective-permute-start.7
  91.0 8.7 %collective-permute-done.3.refs_7_ = f32[1024,128]{1,0:T(8,128)S(1)} collective-permute-done((f32[1024,128]{1,0:T(8,128)}, f32[1024,128]{1,0:T(8,128)S(1)}, u32[]{:S(2)}, u32[]{:S(2)}) %collective-permute-start.3) | collective-permute-done | bytes 524320 | tf_op jit(solution)/shard_map/ppermute | solution.py:305
  99.7 1.5 collective-permute-done.4.refs_8_
  101.2 7.7 %collective-permute-done.9.refs_10_ = f32[1024,128]{1,0:T(8,128)S(1)} collective-permute-done((f32[1024,128]{1,0:T(8,128)S(1)}, f32[1024,128]{1,0:T(8,128)S(1)}, u32[]{:S(2)}, u32[]{:S(2)}) %collective-permute-start.9) | collective-permute-done | bytes 524320 | tf_op jit(solution)/shard_map/ppermute | solution.py:310
  108.9 1.3 collective-permute-done.7.refs_9_
  110.2 6.0 %shard_map.60 = (f32[1024,512]{1,0:T(8,128)}, f32[1024,256]{1,0:T(8,128)}, f32[1024,128]{1,0:T(8,128)}, f32[1024,128]{1,0:T(8,128)}) custom-call(bf16[512,512]{1,0:T(8,128)(2,1)} %get-tuple-element.51.refs_0_, bf16[512,512]{1,0:T(8,128)(2,1)} %get-tuple-element.52.refs_1_, ...), custom_call_target="tpu_custom_call", output_to_operand_aliasing={{0}: (11, {})} | custom-call | flops 37748736 | bytes 294912 | tf_op jit(solution)/shard_map/pallas_call | solution.py:153
  116.8 1.0 collective-permute-start.15
  117.8 1.4 collective-permute-start.18
  119.3 1.1 collective-permute-start.17
  121.0 6.1 %shard_map.61 = (bf16[8,1024,512]{2,1,0:T(8,128)(2,1)}, bf16[8,1024,512]{2,1,0:T(8,128)(2,1)}) custom-call(s32[2,2]{1,0:T(2,128)} %stack.128.place, f32[1024,512]{1,0:T(8,128)} %get-tuple-element.80.refs_0_, f32[1024,512]{1,0:T(8,128)} %collective-permute-done.16.refs_1_), custom_call_target="tpu_custom_call" | custom-call | bytes 262144 | tf_op jit(solution)/shard_map/pallas_call | solution.py:192
  127.1 15.3 %collective-permute-done.19.refs_3_ = f32[1024,256]{1,0:T(8,128)S(1)} collective-permute-done((f32[1024,256]{1,0:T(8,128)}, f32[1024,256]{1,0:T(8,128)S(1)}, u32[]{:S(2)}, u32[]{:S(2)}) %collective-permute-start.19) | collective-permute-done | bytes 1048608 | tf_op jit(solution)/shard_map/ppermute | solution.py:325
  142.4 0.8 collective-permute-done.15.refs_0_
  143.2 22.3 %all-gather.13.cloned.1.call-done = f32[4096,256]{1,0:T(8,128)} async-done(((f32[1024,256]{1,0:T(8,128)}), f32[4096,256]{1,0:T(8,128)}) %all-gather.13.cloned.1.call-update) | async-done | bytes 4194320 | tf_op jit(solution)/shard_map/all_gather | solution.py:322
  165.5 3.0 slice.8
  169.1 1.5 collective-permute-start.24
  170.6 1.5 collective-permute-start.25
  172.1 4.5 %all-to-all-start.1 = ((f32[4,1024,128]{2,1,0:T(8,128)}), f32[4,1024,128]{2,1,0:T(8,128)}, u32[]{:S(2)}, u32[]{:S(2)}) async-start(f32[4,1024,128]{2,1,0:T(8,128)} %slice.8), calls=%async_computation.1 | async-start | bytes 4194304 | tf_op jit(solution)/shard_map/all_to_all | solution.py:259
  177.4 14.3 %shard_map.62 = (bf16[8,1024,512]{2,1,0:T(8,128)(2,1)}, bf16[8,1024,512]{2,1,0:T(8,128)(2,1)}) custom-call(s32[2,8]{1,0:T(2,128)} %pad_add_fusion.place, f32[1024,256]{1,0:T(8,128)} %collective-permute-done.15.refs_0_, f32[1024,256]{1,0:T(8,128)} %collective-permute-done.17.refs_1_, ...), custom_call_target="tpu_custom_call", output_to_operand_aliasing={{0}: (9, {}), {1}: (10, {})} | custom-call | bytes 524288 | tf_op jit(solution)/shard_map/pallas_call | solution.py:192
  191.7 4.7 %collective-permute-done.24 = f32[1024,256]{1,0:T(8,128)} collective-permute-done((f32[1024,256]{1,0:T(8,128)}, f32[1024,256]{1,0:T(8,128)}, u32[]{:S(2)}, u32[]{:S(2)}) %collective-permute-start.24) | collective-permute-done | bytes 1048608 | tf_op jit(solution)/shard_map/ppermute | solution.py:342
  196.4 1.4 constant_dynamic-update-slice_fusion.1
  197.8 1.4 constant_dynamic-update-slice_fusion.refs_0_
  199.3 3.7 %slice.7 = f32[4,1024,128]{2,1,0:T(8,128)} slice(f32[4,1024,256]{2,1,0:T(8,128)} %bitcast.47), slice={[0:4], [0:1024], [128:256]} | slice | bytes 4194304 | tf_op jit(solution)/shard_map/slice | solution.py:346
  203.0 15.1 %all-to-all-done.1.pieces = f32[4,1024,128]{2,1,0:T(8,128)} async-done(((f32[4,1024,128]{2,1,0:T(8,128)}), f32[4,1024,128]{2,1,0:T(8,128)}, u32[]{:S(2)}, u32[]{:S(2)}) %all-to-all-start.1) | async-done | bytes 2097184 | tf_op jit(solution)/shard_map/all_to_all | solution.py:259
  218.2 4.5 %all-to-all-start = ((f32[4,1024,128]{2,1,0:T(8,128)}), f32[4,1024,128]{2,1,0:T(8,128)}, u32[]{:S(2)}, u32[]{:S(2)}) async-start(f32[4,1024,128]{2,1,0:T(8,128)} %slice.7), calls=%async_computation | async-start | bytes 4194304 | tf_op jit(solution)/shard_map/all_to_all | solution.py:259
  223.3 6.1 %shard_map.63 = (bf16[8,1024,512]{2,1,0:T(8,128)(2,1)}, bf16[8,1024,512]{2,1,0:T(8,128)(2,1)}) custom-call(s32[2,2]{1,0:T(2,128)} %stack.133.place, f32[1024,512]{1,0:T(8,128)} %copy-done.3, f32[1024,512]{1,0:T(8,128)} %collective-permute-done.26.refs_1_, ...), custom_call_target="tpu_custom_call", output_to_operand_aliasing={{0}: (3, {}), {1}: (4, {})} | custom-call | bytes 262144 | tf_op jit(solution)/shard_map/pallas_call | solution.py:192
  229.4 18.6 %shard_map.64.refs_0_ = f32[4,512,4096]{2,1,0:T(8,128)} custom-call(f32[4,1024,128]{2,1,0:T(8,128)} %all-to-all-done.1.pieces, bf16[8,1024,512]{2,1,0:T(8,128)(2,1)} %get-tuple-element.93.high, bf16[8,1024,512]{2,1,0:T(8,128)(2,1)} %get-tuple-element.94.low), custom_call_target="tpu_custom_call" | custom-call | flops 402653184 | bytes 851968 | tf_op jit(solution)/shard_map/pallas_call | solution.py:235
  248.0 4.5 %all-to-all-start.3 = ((f32[4,1024,128]{2,1,0:T(8,128)}), f32[4,1024,128]{2,1,0:T(8,128)}, u32[]{:S(2)}, u32[]{:S(2)}) async-start(f32[4,1024,128]{2,1,0:T(8,128)} %bitcast.49), calls=%async_computation.3 | async-start | bytes 4194304 | tf_op jit(solution)/shard_map/all_to_all | solution.py:259
  252.5 18.6 %shard_map.65.refs_0_ = f32[4,512,4096]{2,1,0:T(8,128)} custom-call(f32[4,1024,128]{2,1,0:T(8,128)} %all-to-all-done.pieces, bf16[8,1024,512]{2,1,0:T(8,128)(2,1)} %get-tuple-element.93.high, bf16[8,1024,512]{2,1,0:T(8,128)(2,1)} %get-tuple-element.94.low, f32[4,512,4096]{2,1,0:T(8,128)} %shard_map.64.refs_0_), custom_call_target="tpu_custom_call", output_to_operand_aliasing={{}: (3, {})} | custom-call | flops 402653184 | bytes 851968 | tf_op jit(solution)/shard_map/pallas_call | solution.py:235
  271.1 5.7 %all-to-all-done.3.pieces = f32[4,1024,128]{2,1,0:T(8,128)} async-done(((f32[4,1024,128]{2,1,0:T(8,128)}), f32[4,1024,128]{2,1,0:T(8,128)}, u32[]{:S(2)}, u32[]{:S(2)}) %all-to-all-start.3) | async-done | bytes 2097184 | tf_op jit(solution)/shard_map/all_to_all | solution.py:259
  276.8 4.5 %all-to-all-start.2 = ((f32[4,1024,128]{2,1,0:T(8,128)}), f32[4,1024,128]{2,1,0:T(8,128)}, u32[]{:S(2)}, u32[]{:S(2)}) async-start(f32[4,1024,128]{2,1,0:T(8,128)} %bitcast.50), calls=%async_computation.2 | async-start | bytes 4194304 | tf_op jit(solution)/shard_map/all_to_all | solution.py:259
  281.3 18.6 %shard_map.66.refs_0_ = f32[4,512,4096]{2,1,0:T(8,128)} custom-call(f32[4,1024,128]{2,1,0:T(8,128)} %all-to-all-done.3.pieces, bf16[8,1024,512]{2,1,0:T(8,128)(2,1)} %get-tuple-element.93.high, bf16[8,1024,512]{2,1,0:T(8,128)(2,1)} %get-tuple-element.94.low, f32[4,512,4096]{2,1,0:T(8,128)} %shard_map.65.refs_0_), custom_call_target="tpu_custom_call", output_to_operand_aliasing={{}: (3, {})} | custom-call | flops 402653184 | bytes 851968 | tf_op jit(solution)/shard_map/pallas_call | solution.py:235
  299.9 5.8 %all-to-all-done.2.pieces = f32[4,1024,128]{2,1,0:T(8,128)} async-done(((f32[4,1024,128]{2,1,0:T(8,128)}), f32[4,1024,128]{2,1,0:T(8,128)}, u32[]{:S(2)}, u32[]{:S(2)}) %all-to-all-start.2) | async-done | bytes 2097184 | tf_op jit(solution)/shard_map/all_to_all | solution.py:259
  305.7 18.6 %shard_map.67 = f32[4,512,4096]{2,1,0:T(8,128)} custom-call(f32[4,1024,128]{2,1,0:T(8,128)} %all-to-all-done.2.pieces, bf16[8,1024,512]{2,1,0:T(8,128)(2,1)} %get-tuple-element.93.high, bf16[8,1024,512]{2,1,0:T(8,128)(2,1)} %get-tuple-element.94.low, f32[4,512,4096]{2,1,0:T(8,128)} %shard_map.66.refs_0_), custom_call_target="tpu_custom_call", output_to_operand_aliasing={{}: (3, {})} | custom-call | flops 402653184 | bytes 851968 | tf_op jit(solution)/shard_map/pallas_call | solution.py:235
  (80 shorter events, 7.0 us)
Async XLA Ops:
  6.5 58.3 %all-gather.9.cloned.1.call-start = ((), (), s32[]{:S(2)}) async-start(), calls=%async_computation.4 | async-start | bytes 3538944 | tf_op jit(solution)/shard_map/all_gather | solution.py:50
  9.2 156.3 %all-gather.13.cloned.1.call-start = ((), (), s32[]{:S(2)}) async-start(), calls=%async_computation.6 | async-start | bytes 5242880 | tf_op jit(solution)/shard_map/all_gather | solution.py:322
  9.3 3.8 %copy-start.4 = (f32[64,2,4096]{2,1,0:T(2,128)S(1)}, f32[64,2,4096]{2,1,0:T(2,128)}, u32[]{:S(2)}) copy-start(f32[64,2,4096]{2,1,0:T(2,128)} %param.7) | copy-start | bytes 6291460
  12.6 8.3 %collective-permute-start.1 = (f32[256,2048]{1,0:T(8,128)}, f32[256,2048]{1,0:T(8,128)}, u32[]{:S(2)}, u32[]{:S(2)}) collective-permute-start(f32[256,2048]{1,0:T(8,128)} %constant_dynamic-slice_fusion), channel_id=1, source_target_pairs={{0,4},{4,0},{8,12},{12,8},{16,20},{20,16},{24,28},{28,24},{1,5},{5... | collective-permute-start | bytes 6291464 | tf_op jit(solution)/shard_map/ppermute | solution.py:278
  14.3 2.1 copy-start
  14.3 2.0 copy-start.7
  15.5 3.2 collective-permute-start.2
  16.4 4.5 %copy-start.1 = (f32[2,512,256]{2,1,0:T(8,128)}, f32[2,512,256]{2,1,0:T(8,128)S(1)}, u32[]{:S(2)}) copy-start(f32[2,512,256]{2,1,0:T(8,128)S(1)} %copy.20) | copy-start | bytes 3145732
  16.4 3.4 %collective-permute-start = (f32[1024,256]{1,0:T(8,128)S(1)}, f32[1024,256]{1,0:T(8,128)S(1)}, u32[]{:S(2)}, u32[]{:S(2)}) collective-permute-start(f32[1024,256]{1,0:T(8,128)S(1)} %bitcast.42), channel_id=1, source_target_pairs={{0,4},{4,0},{8,12},{12,8},{16,20},{20,16},{24,28},{28,24},{1,5},{5... | collective-permute-start | bytes 3145736 | tf_op jit(solution)/shard_map/ppermute | solution.py:282
  19.9 1.0 copy-start.2
  25.3 23.9 %collective-permute-start.13 = (f32[1024,128]{1,0:T(8,128)}, f32[1024,128]{1,0:T(8,128)}, u32[]{:S(2)}, u32[]{:S(2)}) collective-permute-start(f32[1024,128]{1,0:T(8,128)} %get-tuple-element.73), channel_id=1, source_target_pairs={{0,16},{4,20},{8,24},{12,28},{16,0},{20,4},{24,8},{28,12},{1,17},{... | collective-permute-start | bytes 1572872 | tf_op jit(solution)/shard_map/ppermute | solution.py:305
  28.2 24.3 %collective-permute-start.11 = (f32[1024,128]{1,0:T(8,128)}, f32[1024,128]{1,0:T(8,128)S(1)}, u32[]{:S(2)}, u32[]{:S(2)}) collective-permute-start(f32[1024,128]{1,0:T(8,128)} %get-tuple-element.70), channel_id=1, source_target_pairs={{0,8},{4,12},{8,0},{12,4},{16,24},{20,28},{24,16},{28,20},{1,9},{5... | collective-permute-start | bytes 1572872 | tf_op jit(solution)/shard_map/ppermute | solution.py:305
  36.1 26.8 %collective-permute-start.5 = (f32[1024,128]{1,0:T(8,128)}, f32[1024,128]{1,0:T(8,128)S(1)}, u32[]{:S(2)}, u32[]{:S(2)}) collective-permute-start(f32[1024,128]{1,0:T(8,128)} %get-tuple-element.62), channel_id=1, source_target_pairs={{0,8},{4,12},{8,0},{12,4},{16,24},{20,28},{24,16},{28,20},{1,9},{5... | collective-permute-start | bytes 1572872 | tf_op jit(solution)/shard_map/ppermute | solution.py:305
  37.2 32.7 %collective-permute-start.10 = (f32[1024,128]{1,0:T(8,128)}, f32[1024,128]{1,0:T(8,128)S(1)}, u32[]{:S(2)}, u32[]{:S(2)}) collective-permute-start(f32[1024,128]{1,0:T(8,128)} %get-tuple-element.68), channel_id=1, source_target_pairs={{0,16},{4,20},{8,24},{12,28},{16,0},{20,4},{24,8},{28,12},{1,17},{... | collective-permute-start | bytes 1572872 | tf_op jit(solution)/shard_map/ppermute | solution.py:305
  51.2 23.0 %collective-permute-start.14 = (f32[1024,128]{1,0:T(8,128)}, f32[1024,128]{1,0:T(8,128)}, u32[]{:S(2)}, u32[]{:S(2)}) collective-permute-start(f32[1024,128]{1,0:T(8,128)} %add.74), channel_id=1, source_target_pairs={{0,8},{4,12},{8,0},{12,4},{16,24},{20,28},{24,16},{28,20},{1,9},{5... | collective-permute-start | bytes 1572872 | tf_op jit(solution)/shard_map/ppermute | solution.py:310
  54.4 19.8 %collective-permute-start.12 = (f32[1024,128]{1,0:T(8,128)}, f32[1024,128]{1,0:T(8,128)S(1)}, u32[]{:S(2)}, u32[]{:S(2)}) collective-permute-start(f32[1024,128]{1,0:T(8,128)} %add.73), channel_id=1, source_target_pairs={{0,16},{4,20},{8,24},{12,28},{16,0},{20,4},{24,8},{28,12},{1,17},{... | collective-permute-start | bytes 1572872 | tf_op jit(solution)/shard_map/ppermute | solution.py:309
  62.9 12.2 %copy-start.10 = (f32[1024,128]{1,0:T(8,128)}, f32[1024,128]{1,0:T(8,128)S(1)}, u32[]{:S(2)}) copy-start(f32[1024,128]{1,0:T(8,128)S(1)} %collective-permute-done.5.refs_7_) | copy-start | bytes 1572868
  62.9 20.0 %collective-permute-start.8 = (f32[1024,128]{1,0:T(8,128)}, f32[1024,128]{1,0:T(8,128)}, u32[]{:S(2)}, u32[]{:S(2)}) collective-permute-start(f32[1024,128]{1,0:T(8,128)} %get-tuple-element.66), channel_id=1, source_target_pairs={{0,16},{4,20},{8,24},{12,28},{16,0},{20,4},{24,8},{28,12},{1,17},{... | collective-permute-start | bytes 1572872 | tf_op jit(solution)/shard_map/ppermute | solution.py:305
  62.9 21.4 %collective-permute-start.6 = (f32[1024,128]{1,0:T(8,128)}, f32[1024,128]{1,0:T(8,128)}, u32[]{:S(2)}, u32[]{:S(2)}) collective-permute-start(f32[1024,128]{1,0:T(8,128)} %get-tuple-element.63), channel_id=1, source_target_pairs={{0,8},{4,12},{8,0},{12,4},{16,24},{20,28},{24,16},{28,20},{1,9},{5... | collective-permute-start | bytes 1572872 | tf_op jit(solution)/shard_map/ppermute | solution.py:305
  69.9 5.1 %copy-start.11 = (f32[1024,128]{1,0:T(8,128)}, f32[1024,128]{1,0:T(8,128)S(1)}, u32[]{:S(2)}) copy-start(f32[1024,128]{1,0:T(8,128)S(1)} %collective-permute-done.10.refs_8_) | copy-start | bytes 1572868
  74.2 0.8 copy-start.14
  75.0 11.6 %copy-start.9 = (f32[1024,128]{1,0:T(8,128)S(1)}, f32[1024,128]{1,0:T(8,128)}, u32[]{:S(2)}) copy-start(f32[1024,128]{1,0:T(8,128)} %get-tuple-element.64) | copy-start | bytes 1572868
  80.7 7.4 %copy-start.8 = (f32[1024,128]{1,0:T(8,128)S(1)}, f32[1024,128]{1,0:T(8,128)}, u32[]{:S(2)}) copy-start(f32[1024,128]{1,0:T(8,128)} %get-tuple-element.60) | copy-start | bytes 1572868
  84.3 139.0 %all-gather.15.cloned.1.call-start = ((), (), s32[]{:S(2)}) async-start(), calls=%async_computation.7 | async-start | bytes 2621440 | tf_op jit(solution)/shard_map/all_gather | solution.py:322
  84.6 15.1 %collective-permute-start.3 = (f32[1024,128]{1,0:T(8,128)}, f32[1024,128]{1,0:T(8,128)S(1)}, u32[]{:S(2)}, u32[]{:S(2)}) collective-permute-start(f32[1024,128]{1,0:T(8,128)} %get-tuple-element.58), channel_id=1, source_target_pairs={{0,8},{4,12},{8,0},{12,4},{16,24},{20,28},{24,16},{28,20},{1,9},{5... | collective-permute-start | bytes 1572872 | tf_op jit(solution)/shard_map/ppermute | solution.py:305
  86.1 15.1 %collective-permute-start.4 = (f32[1024,128]{1,0:T(8,128)}, f32[1024,128]{1,0:T(8,128)S(1)}, u32[]{:S(2)}, u32[]{:S(2)}) collective-permute-start(f32[1024,128]{1,0:T(8,128)} %get-tuple-element.59), channel_id=1, source_target_pairs={{0,16},{4,20},{8,24},{12,28},{16,0},{20,4},{24,8},{28,12},{1,17},{... | collective-permute-start | bytes 1572872 | tf_op jit(solution)/shard_map/ppermute | solution.py:305
  87.7 21.2 %collective-permute-start.9 = (f32[1024,128]{1,0:T(8,128)S(1)}, f32[1024,128]{1,0:T(8,128)S(1)}, u32[]{:S(2)}, u32[]{:S(2)}) collective-permute-start(f32[1024,128]{1,0:T(8,128)S(1)} %add.72), channel_id=1, source_target_pairs={{0,8},{4,12},{8,0},{12,4},{16,24},{20,28},{24,16},{28,20},{1,9},{5... | collective-permute-start | bytes 1572872 | tf_op jit(solution)/shard_map/ppermute | solution.py:310
  89.2 21.0 %collective-permute-start.7 = (f32[1024,128]{1,0:T(8,128)S(1)}, f32[1024,128]{1,0:T(8,128)}, u32[]{:S(2)}, u32[]{:S(2)}) collective-permute-start(f32[1024,128]{1,0:T(8,128)S(1)} %add.71), channel_id=1, source_target_pairs={{0,16},{4,20},{8,24},{12,28},{16,0},{20,4},{24,8},{28,12},{1,17},{... | collective-permute-start | bytes 1572872 | tf_op jit(solution)/shard_map/ppermute | solution.py:309
  99.7 10.5 %copy-start.12 = (f32[1024,128]{1,0:T(8,128)}, f32[1024,128]{1,0:T(8,128)S(1)}, u32[]{:S(2)}) copy-start(f32[1024,128]{1,0:T(8,128)S(1)} %collective-permute-done.3.refs_7_) | copy-start | bytes 1572868
  101.2 9.0 %copy-start.13 = (f32[1024,128]{1,0:T(8,128)}, f32[1024,128]{1,0:T(8,128)S(1)}, u32[]{:S(2)}) copy-start(f32[1024,128]{1,0:T(8,128)S(1)} %collective-permute-done.4.refs_8_) | copy-start | bytes 1572868
  108.9 1.3 copy-start.15
  116.2 4.8 %collective-permute-start.16 = (f32[1024,512]{1,0:T(8,128)}, f32[1024,512]{1,0:T(8,128)}, u32[]{:S(2)}, u32[]{:S(2)}) collective-permute-start(f32[1024,512]{1,0:T(8,128)} %get-tuple-element.80.refs_0_), channel_id=1, source_target_pairs={{0,4},{4,0},{8,12},{12,8},{16,20},{20,16},{24,28},{28,24},{1,5},{5... | collective-permute-start | bytes 6291464 | tf_op jit(solution)/shard_map/ppermute | solution.py:328
  116.2 26.2 %collective-permute-start.19 = (f32[1024,256]{1,0:T(8,128)}, f32[1024,256]{1,0:T(8,128)S(1)}, u32[]{:S(2)}, u32[]{:S(2)}) collective-permute-start(f32[1024,256]{1,0:T(8,128)} %get-tuple-element.78), channel_id=1, source_target_pairs={{0,16},{4,20},{8,24},{12,28},{16,0},{20,4},{24,8},{28,12},{1,17},{... | collective-permute-start | bytes 3145736 | tf_op jit(solution)/shard_map/ppermute | solution.py:325
  116.8 26.4 %collective-permute-start.15 = (f32[1024,256]{1,0:T(8,128)}, f32[1024,256]{1,0:T(8,128)}, u32[]{:S(2)}, u32[]{:S(2)}) collective-permute-start(f32[1024,256]{1,0:T(8,128)} %get-tuple-element.79), channel_id=1, source_target_pairs={{0,8},{4,12},{8,0},{12,4},{16,24},{20,28},{24,16},{28,20},{1,9},{5... | collective-permute-start | bytes 3145736 | tf_op jit(solution)/shard_map/ppermute | solution.py:324
  117.8 50.8 %collective-permute-start.18 = (f32[1024,256]{1,0:T(8,128)}, f32[1024,256]{1,0:T(8,128)}, u32[]{:S(2)}, u32[]{:S(2)}) collective-permute-start(f32[1024,256]{1,0:T(8,128)} %get-tuple-element.79), channel_id=1, source_target_pairs={{0,16},{4,20},{8,24},{12,28},{16,0},{20,4},{24,8},{28,12},{1,17},{... | collective-permute-start | bytes 3145736 | tf_op jit(solution)/shard_map/ppermute | solution.py:327
  119.3 49.3 %collective-permute-start.17 = (f32[1024,256]{1,0:T(8,128)}, f32[1024,256]{1,0:T(8,128)}, u32[]{:S(2)}, u32[]{:S(2)}) collective-permute-start(f32[1024,256]{1,0:T(8,128)} %get-tuple-element.78), channel_id=1, source_target_pairs={{0,8},{4,12},{8,0},{12,4},{16,24},{20,28},{24,16},{28,20},{1,9},{5... | collective-permute-start | bytes 3145736 | tf_op jit(solution)/shard_map/ppermute | solution.py:326
  142.4 28.2 %copy-start.5 = (f32[1024,256]{1,0:T(8,128)}, f32[1024,256]{1,0:T(8,128)S(1)}, u32[]{:S(2)}) copy-start(f32[1024,256]{1,0:T(8,128)S(1)} %collective-permute-done.19.refs_3_) | copy-start | bytes 3145732
  142.4 28.2 %collective-permute-start.23 = (f32[1024,256]{1,0:T(8,128)S(1)}, f32[1024,256]{1,0:T(8,128)S(1)}, u32[]{:S(2)}, u32[]{:S(2)}) collective-permute-start(f32[1024,256]{1,0:T(8,128)S(1)} %collective-permute-done.19.refs_3_), channel_id=1, source_target_pairs={{0,4},{4,0},{8,12},{12,8},{16,20},{20,16},{24,28},{28,24},{1,5},{5... | collective-permute-start | bytes 3145736 | tf_op jit(solution)/shard_map/ppermute | solution.py:336
  143.2 34.2 %collective-permute-start.20 = (f32[1024,256]{1,0:T(8,128)}, f32[1024,256]{1,0:T(8,128)}, u32[]{:S(2)}, u32[]{:S(2)}) collective-permute-start(f32[1024,256]{1,0:T(8,128)} %collective-permute-done.15.refs_0_), channel_id=1, source_target_pairs={{0,4},{4,0},{8,12},{12,8},{16,20},{20,16},{24,28},{28,24},{1,5},{5... | collective-permute-start | bytes 3145736 | tf_op jit(solution)/shard_map/ppermute | solution.py:336
  168.6 8.2 %copy-start.16 = (s32[1,8]{1,0:T(1,128)S(1)}, s32[1,8]{1,0:T(1,128)}, u32[]{:S(2)}) copy-start(s32[1,8]{1,0:T(1,128)} %constant.42.clone.1) | copy-start | bytes 100
  168.6 8.8 %collective-permute-start.22 = (f32[1024,256]{1,0:T(8,128)}, f32[1024,256]{1,0:T(8,128)}, u32[]{:S(2)}, u32[]{:S(2)}) collective-permute-start(f32[1024,256]{1,0:T(8,128)} %collective-permute-done.18.refs_2_), channel_id=1, source_target_pairs={{0,4},{4,0},{8,12},{12,8},{16,20},{20,16},{24,28},{28,24},{1,5},{5... | collective-permute-start | bytes 3145736 | tf_op jit(solution)/shard_map/ppermute | solution.py:336
  168.6 8.8 %collective-permute-start.21 = (f32[1024,256]{1,0:T(8,128)}, f32[1024,256]{1,0:T(8,128)}, u32[]{:S(2)}, u32[]{:S(2)}) collective-permute-start(f32[1024,256]{1,0:T(8,128)} %collective-permute-done.17.refs_1_), channel_id=1, source_target_pairs={{0,4},{4,0},{8,12},{12,8},{16,20},{20,16},{24,28},{28,24},{1,5},{5... | collective-permute-start | bytes 3145736 | tf_op jit(solution)/shard_map/ppermute | solution.py:336
  169.1 27.3 %collective-permute-start.24 = (f32[1024,256]{1,0:T(8,128)}, f32[1024,256]{1,0:T(8,128)}, u32[]{:S(2)}, u32[]{:S(2)}) collective-permute-start(f32[1024,256]{1,0:T(8,128)} %collective-permute-done.15.refs_0_), channel_id=1, source_target_pairs={{0,16},{4,20},{8,24},{12,28},{16,0},{20,4},{24,8},{28,12},{1,17},{... | collective-permute-start | bytes 3145736 | tf_op jit(solution)/shard_map/ppermute | solution.py:342
  170.6 1.5 copy-start.6
  170.6 27.2 %collective-permute-start.25 = (f32[1024,256]{1,0:T(8,128)S(1)}, f32[1024,256]{1,0:T(8,128)}, u32[]{:S(2)}, u32[]{:S(2)}) collective-permute-start(f32[1024,256]{1,0:T(8,128)S(1)} %collective-permute-done.19.refs_3_), channel_id=1, source_target_pairs={{0,8},{4,12},{8,0},{12,4},{16,24},{20,28},{24,16},{28,20},{1,9},{5... | collective-permute-start | bytes 3145736 | tf_op jit(solution)/shard_map/ppermute | solution.py:343
  172.1 46.0 %all-to-all-start.1 = ((f32[4,1024,128]{2,1,0:T(8,128)}), f32[4,1024,128]{2,1,0:T(8,128)}, u32[]{:S(2)}, u32[]{:S(2)}) async-start(f32[4,1024,128]{2,1,0:T(8,128)} %slice.8), calls=%async_computation.1 | async-start | bytes 4194304 | tf_op jit(solution)/shard_map/all_to_all | solution.py:259
  176.6 94.5 %all-gather.11.cloned.1.call-start = ((), (), s32[]{:S(2)}) async-start(), calls=%async_computation.5 | async-start | bytes 2621440 | tf_op jit(solution)/shard_map/all_gather | solution.py:322
  199.2 3.8 %copy-start.3 = (f32[1024,512]{1,0:T(8,128)}, f32[1024,512]{1,0:T(8,128)S(1)}, u32[]{:S(2)}) copy-start(f32[1024,512]{1,0:T(8,128)S(1)} %constant_dynamic-update-slice_fusion.refs_0_) | copy-start | bytes 6291460
  199.2 24.1 %collective-permute-start.26 = (f32[1024,512]{1,0:T(8,128)S(1)}, f32[1024,512]{1,0:T(8,128)}, u32[]{:S(2)}, u32[]{:S(2)}) collective-permute-start(f32[1024,512]{1,0:T(8,128)S(1)} %constant_dynamic-update-slice_fusion.refs_0_), channel_id=1, source_target_pairs={{0,4},{4,0},{8,12},{12,8},{16,20},{20,16},{24,28},{28,24},{1,5},{5... | collective-permute-start | bytes 6291464 | tf_op jit(solution)/shard_map/ppermute | solution.py:336
  218.2 29.9 %all-to-all-start = ((f32[4,1024,128]{2,1,0:T(8,128)}), f32[4,1024,128]{2,1,0:T(8,128)}, u32[]{:S(2)}, u32[]{:S(2)}) async-start(f32[4,1024,128]{2,1,0:T(8,128)} %slice.7), calls=%async_computation | async-start | bytes 4194304 | tf_op jit(solution)/shard_map/all_to_all | solution.py:259
  248.0 28.8 %all-to-all-start.3 = ((f32[4,1024,128]{2,1,0:T(8,128)}), f32[4,1024,128]{2,1,0:T(8,128)}, u32[]{:S(2)}, u32[]{:S(2)}) async-start(f32[4,1024,128]{2,1,0:T(8,128)} %bitcast.49), calls=%async_computation.3 | async-start | bytes 4194304 | tf_op jit(solution)/shard_map/all_to_all | solution.py:259
  276.8 28.8 %all-to-all-start.2 = ((f32[4,1024,128]{2,1,0:T(8,128)}), f32[4,1024,128]{2,1,0:T(8,128)}, u32[]{:S(2)}, u32[]{:S(2)}) async-start(f32[4,1024,128]{2,1,0:T(8,128)} %bitcast.50), calls=%async_computation.2 | async-start | bytes 4194304 | tf_op jit(solution)/shard_map/all_to_all | solution.py:259
Sparse Core Ops, SparseCore 0:
  9.4 43.5 all-gather.8
  84.5 81.0 all-gather.12
  167.1 44.4 all-gather.14
  213.0 44.6 all-gather.10

commit v6 on v5

--- a/solution.py
+++ b/solution.py
@@ -295,10 +295,9 @@
     shifted = tuple(tuple((out - 2, *rest) for out, *rest in step) for step in away[1:])
     early = updates(((3, 0),), away[:1], (quarter,) * 2)
     early += updates(((1, 0), (2, 0)), shifted, (quarter,) * 4)
-    *late, keep, late_keep = updates(
-        ((3, 1), (1, 1), (2, 1), (0, 0), (0, 1)),
-        (*away, ((6, 0, 0, half),), ((7, 0, 0, half),)),
-        (*(quarter,) * 6, half, half),
+    late = updates(((3, 1), (1, 1), (2, 1)), away, (quarter,) * 6)
+    keep, late_keep = updates(
+        ((0, 0), (0, 1)), (((0, 0, 0, half),), ((1, 0, 0, half),)), (half, half)
     )
 
     def passed(a_pass, b_pass):
@@ -311,7 +310,7 @@
         return a_got, b_got, a_last, b_last
 
     first = passed(*early[:2])
-    first = after(first[0], late_keep), first[1]
+    first = after(first[0], late[0]), first[1]
     terms = arrivals(first, *early[2:])
     first = passed(*[after(x, terms[0]) for x in late[:2]])
     solved, chunk = solve(matrix, (keep, *terms), (half,), None)

time: 333 us -> 333 us (level)
  Pallas kernels: 139 us -> 143 us
  waiting for transfers between devices: 106 us -> 102 us
    ppermute x2, waiting for transfers between devices: 12 us -> 7.78 us  [arrivals(): b_last = lax.ppermute(b_on + first[1], 'row', ALONG_X)]
    pallas_call x3 -> x4, Pallas kernels: 21.9 us -> 25.3 us  [update_blocks(): pl.pallas_call(lambda info, *refs: partial_updates(steps, [info[count + n...]
  transfers between devices with their start and end apart: 35 -> 35, of which waited for: 18 -> 16; matrix products, arithmetic and copies ran while one was open for 8% -> 8% of each run, Pallas kernels for 37% -> 38%
where the time goes in v6:
time: 333 us; the launch traced here: 331 us
  Pallas kernels  143 us (43%)
  waiting for transfers between devices  102 us (31%)
  starting transfers between devices  41.5 us (12%)
  local copies, waits for them, and re-layouts  22.2 us (7%)
  between operations  13.4 us (4%)
  other arithmetic  9.16 us (3%)
    pallas_call x4, Pallas kernels, downdate_part(): pl.pallas_call(downdate_kernel, grid=(8,), in_specs=specs, out_specs=pl.B...  74.4 us
    all_to_all x4, waiting for transfers between devices, to_chips(): return lax.all_to_all(blocks, 'row', 0, 0, axis_index_groups=SAME_CORE)  26.7 us
    pallas_call x3, Pallas kernels, split_blocks(): pl.pallas_call(functools.partial(split_kernel, parts, count), grid_spec=p...  26.5 us
    pallas_call x4, Pallas kernels, update_blocks(): pl.pallas_call(lambda info, *refs: partial_updates(steps, [info[count + n...  25.3 us
    all_gather x3, waiting for transfers between devices, local(): lax.all_gather(x, 'col', axis=0)  22.4 us
    all_to_all x4, starting transfers between devices, to_chips(): return lax.all_to_all(blocks, 'row', 0, 0, axis_index_groups=SAME_CORE)  17.9 us
    ppermute x4, waiting for transfers between devices, passed(): lax.ppermute(a_pass, 'row', ALONG_X)  15.4 us
    ppermute x1, waiting for transfers between devices, local(): y_late = lax.ppermute(late_half, 'row', ALONG_Y)  15.3 us
  transfers between devices with their start and end apart: 35, of which 16 were waited for; matrix products, arithmetic and copies ran while one was open for 8% of the time, Pallas kernels for 38%

profile of v6, /device:TPU:0, one launch (start us, length us, event | category | flops | bytes accessed | tf_op | source)
XLA Modules:
  0.0 330.8 jit_solution(10378513022265809414)
XLA Ops:
  6.5 1.0 copy.26
  7.5 1.7 pad_maximum_fusion
  9.3 3.3 constant_dynamic-slice_fusion
  13.1 1.2 copy.27
  14.3 1.1 dynamic-slice_bitcast_fusion
  15.4 0.9 copy-done.7
  16.5 0.7 stack.121.info
  17.9 0.8 collective-permute-done.2.refs_5_
  18.7 1.2 collective-permute-done.refs_1_
  19.9 1.0 copy-done.2
  20.8 4.4 %shard_map.59 = (f32[1024,128]{1,0:T(8,128)}, f32[1024,128]{1,0:T(8,128)}) custom-call(s32[4]{0:T(128)} %pad_add_fusion.1.info, f32[1024,256]{1,0:T(8,128)} %bitcast.44, f32[1024,256]{1,0:T(8,128)} %copy-done.2, f32[256,4096]{1,0:T(8,128)} %refs_2_.7, f32[256,2048]{1,0:T(8,128)} %collective-permute-done.1.refs_3_, f32[2,64,4096]{2,1,0:T(8,128)} %bitcast.39, ...), custom_call_target="tpu_custom_call" | custom-call | flops 25165824 | bytes 98304 | tf_op jit(solution)/shard_map/pallas_call | solution.py:94
  25.2 2.9 collective-permute-start.13
  28.1 1.5 collective-permute-start.11
  29.7 6.4 %shard_map.58 = (f32[1024,128]{1,0:T(8,128)}, f32[1024,128]{1,0:T(8,128)}, f32[1024,128]{1,0:T(8,128)}, f32[1024,128]{1,0:T(8,128)}) custom-call(s32[5]{0:T(128)} %stack.121.info, f32[1024,256]{1,0:T(8,128)} %bitcast.45, f32[1024,256]{1,0:T(8,128)} %copy-done.2, f32[256,4096]{1,0:T(8,128)} %refs_2_.7, f32[256,2048]{1,0:T(8,128)} %collective-permute-done.1.refs_3_, ...), custom_call_target="tpu_custom_call" | custom-call | flops 50331648 | bytes 131072 | tf_op jit(solution)/shard_map/pallas_call | solution.py:94
  37.2 7.9 %shard_map.57 = (f32[1024,128]{1,0:T(8,128)}, f32[1024,128]{1,0:T(8,128)}, f32[1024,128]{1,0:T(8,128)}, f32[1024,128]{1,0:T(8,128)}, f32[1024,128]{1,0:T(8,128)}, /*index=5*/f32[1024,128]{1,0:T(8,128)}) custom-call(s32[6]{0:T(128)} %stack.118.info, f32[1024,256]{1,0:T(8,128)} %bitcast.46, f32[1024,256]{1,0:T(8,128)} %copy-done.2, f32[256,4096]{1,0:T(8,128)} %refs_2_.7, ...), custom_call_target="tpu_custom_call" | custom-call | flops 75497472 | bytes 163840 | tf_op jit(solution)/shard_map/pallas_call | solution.py:94
  45.1 3.9 %collective-permute-done.13 = f32[1024,128]{1,0:T(8,128)S(1)} collective-permute-done((f32[1024,128]{1,0:T(8,128)}, f32[1024,128]{1,0:T(8,128)S(1)}, u32[]{:S(2)}, u32[]{:S(2)}) %collective-permute-start.13) | collective-permute-done | bytes 524320 | tf_op jit(solution)/shard_map/ppermute | solution.py:304
  49.1 1.9 add.74
  51.0 1.4 collective-permute-start.14
  52.4 2.0 add.73
  54.4 2.4 collective-permute-start.12
  56.8 6.0 %collective-permute-done.5.refs_7_ = f32[1024,128]{1,0:T(8,128)S(1)} collective-permute-done((f32[1024,128]{1,0:T(8,128)}, f32[1024,128]{1,0:T(8,128)S(1)}, u32[]{:S(2)}, u32[]{:S(2)}) %collective-permute-start.5) | collective-permute-done | bytes 524320 | tf_op jit(solution)/shard_map/ppermute | solution.py:304
  62.8 2.0 collective-permute-start.6
  64.8 0.7 stack.114.info
  65.5 6.5 %shard_map.56 = (f32[1024,256]{1,0:T(8,128)}, f32[1024,256]{1,0:T(8,128)}) custom-call(s32[5]{0:T(128)} %stack.114.info, f32[1024,256]{1,0:T(8,128)} %bitcast.47, f32[1024,256]{1,0:T(8,128)} %copy-done.2, f32[256,4096]{1,0:T(8,128)} %refs_2_.7, f32[256,2048]{1,0:T(8,128)} %collective-permute-done.1.refs_3_, f32[2,64,4096]{2,1,0:T(8,128)} %bitcast.42, ...), custom_call_target="tpu_custom_call" | custom-call | flops 50331648 | bytes 131072 | tf_op jit(solution)/shard_map/pallas_call | solution.py:94
  72.0 5.0 %shard_map.55 = (bf16[512,512]{1,0:T(8,128)(2,1)}, bf16[512,512]{1,0:T(8,128)(2,1)}, bf16[512,512]{1,0:T(8,128)(2,1)}, bf16[512,512]{1,0:T(8,128)(2,1)}, bf16[51...) custom-call(f32[8,3,64,512]{3,2,1,0:T(8,128)} %bitcast.50), custom_call_target="tpu_custom_call" | custom-call | flops 50331648 | bytes 196608 | tf_op jit(solution)/shard_map/pallas_call | solution.py:52
  77.0 0.8 copy-done.12
  78.0 5.6 %shard_map.60 = (f32[1024,512]{1,0:T(8,128)}, f32[1024,256]{1,0:T(8,128)}) custom-call(bf16[512,512]{1,0:T(8,128)(2,1)} %get-tuple-element.51.refs_0_, bf16[512,512]{1,0:T(8,128)(2,1)} %get-tuple-element.52.refs_1_, bf16[512,512]{1,0:T(8,128)(2,1)} %get-tuple-element.53.refs_2_, bf16[512,512]{1,0:T(8,128)(2,1)} %get-tuple-element.54.refs_3_, ...), custom_call_target="tpu_custom_call" | custom-call | flops 37748736 | bytes 294912 | tf_op jit(solution)/shard_map/pallas_call | solution.py:153
  84.6 1.5 collective-permute-start.3
  86.6 1.1 add.72
  87.7 1.0 collective-permute-start.9
  88.7 1.1 add.71
  89.8 1.2 collective-permute-start.7
  91.0 8.7 %collective-permute-done.3.refs_7_ = f32[1024,128]{1,0:T(8,128)S(1)} collective-permute-done((f32[1024,128]{1,0:T(8,128)}, f32[1024,128]{1,0:T(8,128)S(1)}, u32[]{:S(2)}, u32[]{:S(2)}) %collective-permute-start.3) | collective-permute-done | bytes 524320 | tf_op jit(solution)/shard_map/ppermute | solution.py:304
  99.7 1.5 collective-permute-done.4.refs_8_
  101.2 7.8 %collective-permute-done.9.refs_10_ = f32[1024,128]{1,0:T(8,128)S(1)} collective-permute-done((f32[1024,128]{1,0:T(8,128)S(1)}, f32[1024,128]{1,0:T(8,128)S(1)}, u32[]{:S(2)}, u32[]{:S(2)}) %collective-permute-start.9) | collective-permute-done | bytes 524320 | tf_op jit(solution)/shard_map/ppermute | solution.py:309
  108.9 1.2 collective-permute-done.7.refs_9_
  110.2 6.0 %shard_map.61 = (f32[1024,512]{1,0:T(8,128)}, f32[1024,256]{1,0:T(8,128)}, f32[1024,128]{1,0:T(8,128)}, f32[1024,128]{1,0:T(8,128)}) custom-call(bf16[512,512]{1,0:T(8,128)(2,1)} %get-tuple-element.51.refs_0_, bf16[512,512]{1,0:T(8,128)(2,1)} %get-tuple-element.52.refs_1_, ...), custom_call_target="tpu_custom_call", output_to_operand_aliasing={{0}: (11, {})} | custom-call | flops 37748736 | bytes 294912 | tf_op jit(solution)/shard_map/pallas_call | solution.py:153
  116.8 1.0 collective-permute-start.15
  117.8 1.4 collective-permute-start.18
  119.2 1.0 collective-permute-start.17
  120.9 6.1 %shard_map.62 = (bf16[8,1024,512]{2,1,0:T(8,128)(2,1)}, bf16[8,1024,512]{2,1,0:T(8,128)(2,1)}) custom-call(s32[2,2]{1,0:T(2,128)} %stack.135.place, f32[1024,512]{1,0:T(8,128)} %get-tuple-element.80.refs_0_, f32[1024,512]{1,0:T(8,128)} %collective-permute-done.16.refs_1_), custom_call_target="tpu_custom_call" | custom-call | bytes 262144 | tf_op jit(solution)/shard_map/pallas_call | solution.py:192
  127.0 15.3 %collective-permute-done.19.refs_3_ = f32[1024,256]{1,0:T(8,128)S(1)} collective-permute-done((f32[1024,256]{1,0:T(8,128)}, f32[1024,256]{1,0:T(8,128)S(1)}, u32[]{:S(2)}, u32[]{:S(2)}) %collective-permute-start.19) | collective-permute-done | bytes 1048608 | tf_op jit(solution)/shard_map/ppermute | solution.py:324
  142.3 0.8 collective-permute-done.15.refs_0_
  143.2 22.4 %all-gather.13.cloned.1.call-done = f32[4096,256]{1,0:T(8,128)} async-done(((f32[1024,256]{1,0:T(8,128)}), f32[4096,256]{1,0:T(8,128)}) %all-gather.13.cloned.1.call-update) | async-done | bytes 4194320 | tf_op jit(solution)/shard_map/all_gather | solution.py:321
  165.5 3.0 slice.8
  169.1 1.5 collective-permute-start.24
  170.6 1.5 collective-permute-start.25
  172.1 4.5 %all-to-all-start.1 = ((f32[4,1024,128]{2,1,0:T(8,128)}), f32[4,1024,128]{2,1,0:T(8,128)}, u32[]{:S(2)}, u32[]{:S(2)}) async-start(f32[4,1024,128]{2,1,0:T(8,128)} %slice.8), calls=%async_computation.1 | async-start | bytes 4194304 | tf_op jit(solution)/shard_map/all_to_all | solution.py:259
  177.3 14.3 %shard_map.63 = (bf16[8,1024,512]{2,1,0:T(8,128)(2,1)}, bf16[8,1024,512]{2,1,0:T(8,128)(2,1)}) custom-call(s32[2,8]{1,0:T(2,128)} %pad_add_fusion.place, f32[1024,256]{1,0:T(8,128)} %collective-permute-done.15.refs_0_, f32[1024,256]{1,0:T(8,128)} %collective-permute-done.17.refs_1_, ...), custom_call_target="tpu_custom_call", output_to_operand_aliasing={{0}: (9, {}), {1}: (10, {})} | custom-call | bytes 524288 | tf_op jit(solution)/shard_map/pallas_call | solution.py:192
  191.6 4.8 %collective-permute-done.24 = f32[1024,256]{1,0:T(8,128)} collective-permute-done((f32[1024,256]{1,0:T(8,128)}, f32[1024,256]{1,0:T(8,128)}, u32[]{:S(2)}, u32[]{:S(2)}) %collective-permute-start.24) | collective-permute-done | bytes 1048608 | tf_op jit(solution)/shard_map/ppermute | solution.py:341
  196.4 1.4 constant_dynamic-update-slice_fusion.1
  197.8 1.4 constant_dynamic-update-slice_fusion.refs_0_
  199.3 3.7 %slice.7 = f32[4,1024,128]{2,1,0:T(8,128)} slice(f32[4,1024,256]{2,1,0:T(8,128)} %bitcast.49), slice={[0:4], [0:1024], [128:256]} | slice | bytes 4194304 | tf_op jit(solution)/shard_map/slice | solution.py:345
  203.0 15.1 %all-to-all-done.1.pieces = f32[4,1024,128]{2,1,0:T(8,128)} async-done(((f32[4,1024,128]{2,1,0:T(8,128)}), f32[4,1024,128]{2,1,0:T(8,128)}, u32[]{:S(2)}, u32[]{:S(2)}) %all-to-all-start.1) | async-done | bytes 2097184 | tf_op jit(solution)/shard_map/all_to_all | solution.py:259
  218.1 4.5 %all-to-all-start = ((f32[4,1024,128]{2,1,0:T(8,128)}), f32[4,1024,128]{2,1,0:T(8,128)}, u32[]{:S(2)}, u32[]{:S(2)}) async-start(f32[4,1024,128]{2,1,0:T(8,128)} %slice.7), calls=%async_computation | async-start | bytes 4194304 | tf_op jit(solution)/shard_map/all_to_all | solution.py:259
  223.3 6.1 %shard_map.64 = (bf16[8,1024,512]{2,1,0:T(8,128)(2,1)}, bf16[8,1024,512]{2,1,0:T(8,128)(2,1)}) custom-call(s32[2,2]{1,0:T(2,128)} %stack.140.place, f32[1024,512]{1,0:T(8,128)} %copy-done.3, f32[1024,512]{1,0:T(8,128)} %collective-permute-done.26.refs_1_, ...), custom_call_target="tpu_custom_call", output_to_operand_aliasing={{0}: (3, {}), {1}: (4, {})} | custom-call | bytes 262144 | tf_op jit(solution)/shard_map/pallas_call | solution.py:192
  229.4 18.6 %shard_map.65.refs_0_ = f32[4,512,4096]{2,1,0:T(8,128)} custom-call(f32[4,1024,128]{2,1,0:T(8,128)} %all-to-all-done.1.pieces, bf16[8,1024,512]{2,1,0:T(8,128)(2,1)} %get-tuple-element.93.high, bf16[8,1024,512]{2,1,0:T(8,128)(2,1)} %get-tuple-element.94.low), custom_call_target="tpu_custom_call" | custom-call | flops 402653184 | bytes 851968 | tf_op jit(solution)/shard_map/pallas_call | solution.py:235
  248.0 4.4 %all-to-all-start.3 = ((f32[4,1024,128]{2,1,0:T(8,128)}), f32[4,1024,128]{2,1,0:T(8,128)}, u32[]{:S(2)}, u32[]{:S(2)}) async-start(f32[4,1024,128]{2,1,0:T(8,128)} %bitcast.51), calls=%async_computation.3 | async-start | bytes 4194304 | tf_op jit(solution)/shard_map/all_to_all | solution.py:259
  252.5 18.6 %shard_map.66.refs_0_ = f32[4,512,4096]{2,1,0:T(8,128)} custom-call(f32[4,1024,128]{2,1,0:T(8,128)} %all-to-all-done.pieces, bf16[8,1024,512]{2,1,0:T(8,128)(2,1)} %get-tuple-element.93.high, bf16[8,1024,512]{2,1,0:T(8,128)(2,1)} %get-tuple-element.94.low, f32[4,512,4096]{2,1,0:T(8,128)} %shard_map.65.refs_0_), custom_call_target="tpu_custom_call", output_to_operand_aliasing={{}: (3, {})} | custom-call | flops 402653184 | bytes 851968 | tf_op jit(solution)/shard_map/pallas_call | solution.py:235
  271.1 5.8 %all-to-all-done.3.pieces = f32[4,1024,128]{2,1,0:T(8,128)} async-done(((f32[4,1024,128]{2,1,0:T(8,128)}), f32[4,1024,128]{2,1,0:T(8,128)}, u32[]{:S(2)}, u32[]{:S(2)}) %all-to-all-start.3) | async-done | bytes 2097184 | tf_op jit(solution)/shard_map/all_to_all | solution.py:259
  276.9 4.5 %all-to-all-start.2 = ((f32[4,1024,128]{2,1,0:T(8,128)}), f32[4,1024,128]{2,1,0:T(8,128)}, u32[]{:S(2)}, u32[]{:S(2)}) async-start(f32[4,1024,128]{2,1,0:T(8,128)} %bitcast.52), calls=%async_computation.2 | async-start | bytes 4194304 | tf_op jit(solution)/shard_map/all_to_all | solution.py:259
  281.3 18.6 %shard_map.67.refs_0_ = f32[4,512,4096]{2,1,0:T(8,128)} custom-call(f32[4,1024,128]{2,1,0:T(8,128)} %all-to-all-done.3.pieces, bf16[8,1024,512]{2,1,0:T(8,128)(2,1)} %get-tuple-element.93.high, bf16[8,1024,512]{2,1,0:T(8,128)(2,1)} %get-tuple-element.94.low, f32[4,512,4096]{2,1,0:T(8,128)} %shard_map.66.refs_0_), custom_call_target="tpu_custom_call", output_to_operand_aliasing={{}: (3, {})} | custom-call | flops 402653184 | bytes 851968 | tf_op jit(solution)/shard_map/pallas_call | solution.py:235
  299.9 5.8 %all-to-all-done.2.pieces = f32[4,1024,128]{2,1,0:T(8,128)} async-done(((f32[4,1024,128]{2,1,0:T(8,128)}), f32[4,1024,128]{2,1,0:T(8,128)}, u32[]{:S(2)}, u32[]{:S(2)}) %all-to-all-start.2) | async-done | bytes 2097184 | tf_op jit(solution)/shard_map/all_to_all | solution.py:259
  305.7 18.6 %shard_map.68 = f32[4,512,4096]{2,1,0:T(8,128)} custom-call(f32[4,1024,128]{2,1,0:T(8,128)} %all-to-all-done.2.pieces, bf16[8,1024,512]{2,1,0:T(8,128)(2,1)} %get-tuple-element.93.high, bf16[8,1024,512]{2,1,0:T(8,128)(2,1)} %get-tuple-element.94.low, f32[4,512,4096]{2,1,0:T(8,128)} %shard_map.67.refs_0_), custom_call_target="tpu_custom_call", output_to_operand_aliasing={{}: (3, {})} | custom-call | flops 402653184 | bytes 851968 | tf_op jit(solution)/shard_map/pallas_call | solution.py:235
  (82 shorter events, 7.4 us)
Async XLA Ops:
  6.5 65.5 %all-gather.9.cloned.1.call-start = ((), (), s32[]{:S(2)}) async-start(), calls=%async_computation.4 | async-start | bytes 3538944 | tf_op jit(solution)/shard_map/all_gather | solution.py:50
  9.2 156.3 %all-gather.13.cloned.1.call-start = ((), (), s32[]{:S(2)}) async-start(), calls=%async_computation.6 | async-start | bytes 5242880 | tf_op jit(solution)/shard_map/all_gather | solution.py:321
  9.3 3.8 %copy-start.4 = (f32[64,2,4096]{2,1,0:T(2,128)S(1)}, f32[64,2,4096]{2,1,0:T(2,128)}, u32[]{:S(2)}) copy-start(f32[64,2,4096]{2,1,0:T(2,128)} %param.7) | copy-start | bytes 6291460
  12.6 8.2 %collective-permute-start.1 = (f32[256,2048]{1,0:T(8,128)}, f32[256,2048]{1,0:T(8,128)}, u32[]{:S(2)}, u32[]{:S(2)}) collective-permute-start(f32[256,2048]{1,0:T(8,128)} %constant_dynamic-slice_fusion), channel_id=1, source_target_pairs={{0,4},{4,0},{8,12},{12,8},{16,20},{20,16},{24,28},{28,24},{1,5},{5... | collective-permute-start | bytes 6291464 | tf_op jit(solution)/shard_map/ppermute | solution.py:278
  14.3 2.1 copy-start
  14.3 2.0 copy-start.7
  15.4 3.3 %collective-permute-start.2 = (f32[2,64,2048]{2,1,0:T(8,128)}, f32[2,64,2048]{2,1,0:T(8,128)}, u32[]{:S(2)}, u32[]{:S(2)}) collective-permute-start(f32[2,64,2048]{2,1,0:T(8,128)} %dynamic-slice_bitcast_fusion), channel_id=1, source_target_pairs={{0,4},{4,0},{8,12},{12,8},{16,20},{20,16},{24,28},{28,24},{1,5},{5... | collective-permute-start | bytes 3145736 | tf_op jit(solution)/shard_map/ppermute | solution.py:280
  16.4 4.4 %copy-start.1 = (f32[2,512,256]{2,1,0:T(8,128)}, f32[2,512,256]{2,1,0:T(8,128)S(1)}, u32[]{:S(2)}) copy-start(f32[2,512,256]{2,1,0:T(8,128)S(1)} %copy.20) | copy-start | bytes 3145732
  16.4 3.4 %collective-permute-start = (f32[1024,256]{1,0:T(8,128)S(1)}, f32[1024,256]{1,0:T(8,128)S(1)}, u32[]{:S(2)}, u32[]{:S(2)}) collective-permute-start(f32[1024,256]{1,0:T(8,128)S(1)} %bitcast.43), channel_id=1, source_target_pairs={{0,4},{4,0},{8,12},{12,8},{16,20},{20,16},{24,28},{28,24},{1,5},{5... | collective-permute-start | bytes 3145736 | tf_op jit(solution)/shard_map/ppermute | solution.py:282
  19.8 1.0 copy-start.2
  25.2 23.8 %collective-permute-start.13 = (f32[1024,128]{1,0:T(8,128)}, f32[1024,128]{1,0:T(8,128)S(1)}, u32[]{:S(2)}, u32[]{:S(2)}) collective-permute-start(f32[1024,128]{1,0:T(8,128)} %get-tuple-element.73), channel_id=1, source_target_pairs={{0,16},{4,20},{8,24},{12,28},{16,0},{20,4},{24,8},{28,12},{1,17},{... | collective-permute-start | bytes 1572872 | tf_op jit(solution)/shard_map/ppermute | solution.py:304
  28.1 24.3 %collective-permute-start.11 = (f32[1024,128]{1,0:T(8,128)}, f32[1024,128]{1,0:T(8,128)}, u32[]{:S(2)}, u32[]{:S(2)}) collective-permute-start(f32[1024,128]{1,0:T(8,128)} %get-tuple-element.70), channel_id=1, source_target_pairs={{0,8},{4,12},{8,0},{12,4},{16,24},{20,28},{24,16},{28,20},{1,9},{5... | collective-permute-start | bytes 1572872 | tf_op jit(solution)/shard_map/ppermute | solution.py:304
  36.1 26.7 %collective-permute-start.5 = (f32[1024,128]{1,0:T(8,128)}, f32[1024,128]{1,0:T(8,128)S(1)}, u32[]{:S(2)}, u32[]{:S(2)}) collective-permute-start(f32[1024,128]{1,0:T(8,128)} %get-tuple-element.62), channel_id=1, source_target_pairs={{0,8},{4,12},{8,0},{12,4},{16,24},{20,28},{24,16},{28,20},{1,9},{5... | collective-permute-start | bytes 1572872 | tf_op jit(solution)/shard_map/ppermute | solution.py:304
  37.2 39.8 %collective-permute-start.10 = (f32[1024,128]{1,0:T(8,128)}, f32[1024,128]{1,0:T(8,128)S(1)}, u32[]{:S(2)}, u32[]{:S(2)}) collective-permute-start(f32[1024,128]{1,0:T(8,128)} %get-tuple-element.68), channel_id=1, source_target_pairs={{0,16},{4,20},{8,24},{12,28},{16,0},{20,4},{24,8},{28,12},{1,17},{... | collective-permute-start | bytes 1572872 | tf_op jit(solution)/shard_map/ppermute | solution.py:304
  51.0 26.0 %collective-permute-start.14 = (f32[1024,128]{1,0:T(8,128)}, f32[1024,128]{1,0:T(8,128)S(1)}, u32[]{:S(2)}, u32[]{:S(2)}) collective-permute-start(f32[1024,128]{1,0:T(8,128)} %add.74), channel_id=1, source_target_pairs={{0,8},{4,12},{8,0},{12,4},{16,24},{20,28},{24,16},{28,20},{1,9},{5... | collective-permute-start | bytes 1572872 | tf_op jit(solution)/shard_map/ppermute | solution.py:309
  54.4 22.6 %collective-permute-start.12 = (f32[1024,128]{1,0:T(8,128)}, f32[1024,128]{1,0:T(8,128)}, u32[]{:S(2)}, u32[]{:S(2)}) collective-permute-start(f32[1024,128]{1,0:T(8,128)} %add.73), channel_id=1, source_target_pairs={{0,16},{4,20},{8,24},{12,28},{16,0},{20,4},{24,8},{28,12},{1,17},{... | collective-permute-start | bytes 1572872 | tf_op jit(solution)/shard_map/ppermute | solution.py:308
  62.8 9.2 %copy-start.10 = (f32[1024,128]{1,0:T(8,128)}, f32[1024,128]{1,0:T(8,128)S(1)}, u32[]{:S(2)}) copy-start(f32[1024,128]{1,0:T(8,128)S(1)} %collective-permute-done.5.refs_7_) | copy-start | bytes 1572868
  62.8 20.8 %collective-permute-start.8 = (f32[1024,128]{1,0:T(8,128)}, f32[1024,128]{1,0:T(8,128)}, u32[]{:S(2)}, u32[]{:S(2)}) collective-permute-start(f32[1024,128]{1,0:T(8,128)} %get-tuple-element.66), channel_id=1, source_target_pairs={{0,16},{4,20},{8,24},{12,28},{16,0},{20,4},{24,8},{28,12},{1,17},{... | collective-permute-start | bytes 1572872 | tf_op jit(solution)/shard_map/ppermute | solution.py:304
  62.8 21.5 %collective-permute-start.6 = (f32[1024,128]{1,0:T(8,128)}, f32[1024,128]{1,0:T(8,128)}, u32[]{:S(2)}, u32[]{:S(2)}) collective-permute-start(f32[1024,128]{1,0:T(8,128)} %get-tuple-element.63), channel_id=1, source_target_pairs={{0,8},{4,12},{8,0},{12,4},{16,24},{20,28},{24,16},{28,20},{1,9},{5... | collective-permute-start | bytes 1572872 | tf_op jit(solution)/shard_map/ppermute | solution.py:304
  77.0 1.0 copy-start.11
  77.0 0.8 copy-start.12
  78.0 8.6 %copy-start.9 = (f32[1024,128]{1,0:T(8,128)S(1)}, f32[1024,128]{1,0:T(8,128)}, u32[]{:S(2)}) copy-start(f32[1024,128]{1,0:T(8,128)} %get-tuple-element.64) | copy-start | bytes 1572868
  83.6 5.1 %copy-start.8 = (f32[1024,128]{1,0:T(8,128)S(1)}, f32[1024,128]{1,0:T(8,128)}, u32[]{:S(2)}) copy-start(f32[1024,128]{1,0:T(8,128)} %get-tuple-element.60) | copy-start | bytes 1572868
  84.3 139.0 %all-gather.15.cloned.1.call-start = ((), (), s32[]{:S(2)}) async-start(), calls=%async_computation.7 | async-start | bytes 2621440 | tf_op jit(solution)/shard_map/all_gather | solution.py:321
  84.6 15.1 %collective-permute-start.3 = (f32[1024,128]{1,0:T(8,128)}, f32[1024,128]{1,0:T(8,128)S(1)}, u32[]{:S(2)}, u32[]{:S(2)}) collective-permute-start(f32[1024,128]{1,0:T(8,128)} %get-tuple-element.58), channel_id=1, source_target_pairs={{0,8},{4,12},{8,0},{12,4},{16,24},{20,28},{24,16},{28,20},{1,9},{5... | collective-permute-start | bytes 1572872 | tf_op jit(solution)/shard_map/ppermute | solution.py:304
  86.1 15.1 %collective-permute-start.4 = (f32[1024,128]{1,0:T(8,128)}, f32[1024,128]{1,0:T(8,128)S(1)}, u32[]{:S(2)}, u32[]{:S(2)}) collective-permute-start(f32[1024,128]{1,0:T(8,128)} %get-tuple-element.59), channel_id=1, source_target_pairs={{0,16},{4,20},{8,24},{12,28},{16,0},{20,4},{24,8},{28,12},{1,17},{... | collective-permute-start | bytes 1572872 | tf_op jit(solution)/shard_map/ppermute | solution.py:304
  87.7 21.3 %collective-permute-start.9 = (f32[1024,128]{1,0:T(8,128)S(1)}, f32[1024,128]{1,0:T(8,128)S(1)}, u32[]{:S(2)}, u32[]{:S(2)}) collective-permute-start(f32[1024,128]{1,0:T(8,128)S(1)} %add.72), channel_id=1, source_target_pairs={{0,8},{4,12},{8,0},{12,4},{16,24},{20,28},{24,16},{28,20},{1,9},{5... | collective-permute-start | bytes 1572872 | tf_op jit(solution)/shard_map/ppermute | solution.py:309
  89.8 20.3 %collective-permute-start.7 = (f32[1024,128]{1,0:T(8,128)S(1)}, f32[1024,128]{1,0:T(8,128)}, u32[]{:S(2)}, u32[]{:S(2)}) collective-permute-start(f32[1024,128]{1,0:T(8,128)S(1)} %add.71), channel_id=1, source_target_pairs={{0,16},{4,20},{8,24},{12,28},{16,0},{20,4},{24,8},{28,12},{1,17},{... | collective-permute-start | bytes 1572872 | tf_op jit(solution)/shard_map/ppermute | solution.py:308
  99.7 10.5 %copy-start.13 = (f32[1024,128]{1,0:T(8,128)}, f32[1024,128]{1,0:T(8,128)S(1)}, u32[]{:S(2)}) copy-start(f32[1024,128]{1,0:T(8,128)S(1)} %collective-permute-done.3.refs_7_) | copy-start | bytes 1572868
  101.2 9.0 %copy-start.14 = (f32[1024,128]{1,0:T(8,128)}, f32[1024,128]{1,0:T(8,128)S(1)}, u32[]{:S(2)}) copy-start(f32[1024,128]{1,0:T(8,128)S(1)} %collective-permute-done.4.refs_8_) | copy-start | bytes 1572868
  108.9 1.2 copy-start.15
  116.1 4.8 %collective-permute-start.16 = (f32[1024,512]{1,0:T(8,128)}, f32[1024,512]{1,0:T(8,128)}, u32[]{:S(2)}, u32[]{:S(2)}) collective-permute-start(f32[1024,512]{1,0:T(8,128)} %get-tuple-element.80.refs_0_), channel_id=1, source_target_pairs={{0,4},{4,0},{8,12},{12,8},{16,20},{20,16},{24,28},{28,24},{1,5},{5... | collective-permute-start | bytes 6291464 | tf_op jit(solution)/shard_map/ppermute | solution.py:327
  116.1 26.2 %collective-permute-start.19 = (f32[1024,256]{1,0:T(8,128)}, f32[1024,256]{1,0:T(8,128)S(1)}, u32[]{:S(2)}, u32[]{:S(2)}) collective-permute-start(f32[1024,256]{1,0:T(8,128)} %get-tuple-element.78), channel_id=1, source_target_pairs={{0,16},{4,20},{8,24},{12,28},{16,0},{20,4},{24,8},{28,12},{1,17},{... | collective-permute-start | bytes 3145736 | tf_op jit(solution)/shard_map/ppermute | solution.py:324
  116.8 26.4 %collective-permute-start.15 = (f32[1024,256]{1,0:T(8,128)}, f32[1024,256]{1,0:T(8,128)}, u32[]{:S(2)}, u32[]{:S(2)}) collective-permute-start(f32[1024,256]{1,0:T(8,128)} %get-tuple-element.79), channel_id=1, source_target_pairs={{0,8},{4,12},{8,0},{12,4},{16,24},{20,28},{24,16},{28,20},{1,9},{5... | collective-permute-start | bytes 3145736 | tf_op jit(solution)/shard_map/ppermute | solution.py:323
  117.8 50.8 %collective-permute-start.18 = (f32[1024,256]{1,0:T(8,128)}, f32[1024,256]{1,0:T(8,128)}, u32[]{:S(2)}, u32[]{:S(2)}) collective-permute-start(f32[1024,256]{1,0:T(8,128)} %get-tuple-element.79), channel_id=1, source_target_pairs={{0,16},{4,20},{8,24},{12,28},{16,0},{20,4},{24,8},{28,12},{1,17},{... | collective-permute-start | bytes 3145736 | tf_op jit(solution)/shard_map/ppermute | solution.py:326
  119.2 49.3 %collective-permute-start.17 = (f32[1024,256]{1,0:T(8,128)}, f32[1024,256]{1,0:T(8,128)}, u32[]{:S(2)}, u32[]{:S(2)}) collective-permute-start(f32[1024,256]{1,0:T(8,128)} %get-tuple-element.78), channel_id=1, source_target_pairs={{0,8},{4,12},{8,0},{12,4},{16,24},{20,28},{24,16},{28,20},{1,9},{5... | collective-permute-start | bytes 3145736 | tf_op jit(solution)/shard_map/ppermute | solution.py:325
  142.3 28.3 %copy-start.5 = (f32[1024,256]{1,0:T(8,128)}, f32[1024,256]{1,0:T(8,128)S(1)}, u32[]{:S(2)}) copy-start(f32[1024,256]{1,0:T(8,128)S(1)} %collective-permute-done.19.refs_3_) | copy-start | bytes 3145732
  142.3 28.3 %collective-permute-start.23 = (f32[1024,256]{1,0:T(8,128)S(1)}, f32[1024,256]{1,0:T(8,128)S(1)}, u32[]{:S(2)}, u32[]{:S(2)}) collective-permute-start(f32[1024,256]{1,0:T(8,128)S(1)} %collective-permute-done.19.refs_3_), channel_id=1, source_target_pairs={{0,4},{4,0},{8,12},{12,8},{16,20},{20,16},{24,28},{28,24},{1,5},{5... | collective-permute-start | bytes 3145736 | tf_op jit(solution)/shard_map/ppermute | solution.py:335
  143.1 34.2 %collective-permute-start.20 = (f32[1024,256]{1,0:T(8,128)}, f32[1024,256]{1,0:T(8,128)}, u32[]{:S(2)}, u32[]{:S(2)}) collective-permute-start(f32[1024,256]{1,0:T(8,128)} %collective-permute-done.15.refs_0_), channel_id=1, source_target_pairs={{0,4},{4,0},{8,12},{12,8},{16,20},{20,16},{24,28},{28,24},{1,5},{5... | collective-permute-start | bytes 3145736 | tf_op jit(solution)/shard_map/ppermute | solution.py:335
  168.6 8.2 %copy-start.16 = (s32[1,8]{1,0:T(1,128)S(1)}, s32[1,8]{1,0:T(1,128)}, u32[]{:S(2)}) copy-start(s32[1,8]{1,0:T(1,128)} %constant.42.clone.1) | copy-start | bytes 100
  168.6 8.8 %collective-permute-start.22 = (f32[1024,256]{1,0:T(8,128)}, f32[1024,256]{1,0:T(8,128)}, u32[]{:S(2)}, u32[]{:S(2)}) collective-permute-start(f32[1024,256]{1,0:T(8,128)} %collective-permute-done.18.refs_2_), channel_id=1, source_target_pairs={{0,4},{4,0},{8,12},{12,8},{16,20},{20,16},{24,28},{28,24},{1,5},{5... | collective-permute-start | bytes 3145736 | tf_op jit(solution)/shard_map/ppermute | solution.py:335
  168.6 8.7 %collective-permute-start.21 = (f32[1024,256]{1,0:T(8,128)}, f32[1024,256]{1,0:T(8,128)}, u32[]{:S(2)}, u32[]{:S(2)}) collective-permute-start(f32[1024,256]{1,0:T(8,128)} %collective-permute-done.17.refs_1_), channel_id=1, source_target_pairs={{0,4},{4,0},{8,12},{12,8},{16,20},{20,16},{24,28},{28,24},{1,5},{5... | collective-permute-start | bytes 3145736 | tf_op jit(solution)/shard_map/ppermute | solution.py:335
  169.1 27.3 %collective-permute-start.24 = (f32[1024,256]{1,0:T(8,128)}, f32[1024,256]{1,0:T(8,128)}, u32[]{:S(2)}, u32[]{:S(2)}) collective-permute-start(f32[1024,256]{1,0:T(8,128)} %collective-permute-done.15.refs_0_), channel_id=1, source_target_pairs={{0,16},{4,20},{8,24},{12,28},{16,0},{20,4},{24,8},{28,12},{1,17},{... | collective-permute-start | bytes 3145736 | tf_op jit(solution)/shard_map/ppermute | solution.py:341
  170.6 1.5 copy-start.6
  170.6 27.2 %collective-permute-start.25 = (f32[1024,256]{1,0:T(8,128)S(1)}, f32[1024,256]{1,0:T(8,128)}, u32[]{:S(2)}, u32[]{:S(2)}) collective-permute-start(f32[1024,256]{1,0:T(8,128)S(1)} %collective-permute-done.19.refs_3_), channel_id=1, source_target_pairs={{0,8},{4,12},{8,0},{12,4},{16,24},{20,28},{24,16},{28,20},{1,9},{5... | collective-permute-start | bytes 3145736 | tf_op jit(solution)/shard_map/ppermute | solution.py:342
  172.1 46.0 %all-to-all-start.1 = ((f32[4,1024,128]{2,1,0:T(8,128)}), f32[4,1024,128]{2,1,0:T(8,128)}, u32[]{:S(2)}, u32[]{:S(2)}) async-start(f32[4,1024,128]{2,1,0:T(8,128)} %slice.8), calls=%async_computation.1 | async-start | bytes 4194304 | tf_op jit(solution)/shard_map/all_to_all | solution.py:259
  176.6 94.5 %all-gather.11.cloned.1.call-start = ((), (), s32[]{:S(2)}) async-start(), calls=%async_computation.5 | async-start | bytes 2621440 | tf_op jit(solution)/shard_map/all_gather | solution.py:321
  199.2 3.8 %copy-start.3 = (f32[1024,512]{1,0:T(8,128)}, f32[1024,512]{1,0:T(8,128)S(1)}, u32[]{:S(2)}) copy-start(f32[1024,512]{1,0:T(8,128)S(1)} %constant_dynamic-update-slice_fusion.refs_0_) | copy-start | bytes 6291460
  199.2 24.1 %collective-permute-start.26 = (f32[1024,512]{1,0:T(8,128)S(1)}, f32[1024,512]{1,0:T(8,128)}, u32[]{:S(2)}, u32[]{:S(2)}) collective-permute-start(f32[1024,512]{1,0:T(8,128)S(1)} %constant_dynamic-update-slice_fusion.refs_0_), channel_id=1, source_target_pairs={{0,4},{4,0},{8,12},{12,8},{16,20},{20,16},{24,28},{28,24},{1,5},{5... | collective-permute-start | bytes 6291464 | tf_op jit(solution)/shard_map/ppermute | solution.py:335
  218.1 29.9 %all-to-all-start = ((f32[4,1024,128]{2,1,0:T(8,128)}), f32[4,1024,128]{2,1,0:T(8,128)}, u32[]{:S(2)}, u32[]{:S(2)}) async-start(f32[4,1024,128]{2,1,0:T(8,128)} %slice.7), calls=%async_computation | async-start | bytes 4194304 | tf_op jit(solution)/shard_map/all_to_all | solution.py:259
  248.0 28.8 %all-to-all-start.3 = ((f32[4,1024,128]{2,1,0:T(8,128)}), f32[4,1024,128]{2,1,0:T(8,128)}, u32[]{:S(2)}, u32[]{:S(2)}) async-start(f32[4,1024,128]{2,1,0:T(8,128)} %bitcast.51), calls=%async_computation.3 | async-start | bytes 4194304 | tf_op jit(solution)/shard_map/all_to_all | solution.py:259
  276.9 28.9 %all-to-all-start.2 = ((f32[4,1024,128]{2,1,0:T(8,128)}), f32[4,1024,128]{2,1,0:T(8,128)}, u32[]{:S(2)}, u32[]{:S(2)}) async-start(f32[4,1024,128]{2,1,0:T(8,128)} %bitcast.52), calls=%async_computation.2 | async-start | bytes 4194304 | tf_op jit(solution)/shard_map/all_to_all | solution.py:259
Sparse Core Ops, SparseCore 0:
  9.4 43.5 all-gather.8
  84.5 81.0 all-gather.12
  167.1 44.4 all-gather.14
  213.0 44.6 all-gather.10
